TPU v7x, 32 devices: a whole 2x2x4 slice. The times are simulated.
32 devices in a mesh: slab: 8 (over y, x, core), batch: 4 (over z).
Axes of the slice: x: 2, y: 2, z: 4, core: 2. Of those that a mesh axis runs over, the one named last changes fastest.
Arguments:
- volumes: bfloat16 [256, 2, 16384], P('slab', None, 'batch'), may hold values from -6 to 6
- band_weights: bfloat16 [2, 512, 32], P(None, 'slab'), may hold values from -1 to 1
- band_start: int32 [2, 512], P(None, 'slab'), may hold values from 0 to 224
- images: bfloat16 [1536, 16384], P('batch'), may hold values from -7 to 7
- noise_precision: float32 [1536], P('batch'), may hold values from 0.005004883 to 0.050048828
- log_prior: float32 [2, 512], P(None, 'slab'), may hold values from -4 to 4
Outputs:
- responsibilities: float32 [2, 512, 1536], P(None, 'slab', 'batch')
- log_evidence: float32 [1536], P('batch')
- backprojection: float32 [256, 2, 16384], P('slab', None, 'batch')
All inputs are finite; a program needn't handle non-finite values.
Results may differ from a plain program's by a relative error of at most 0.0069.
Values may be sent and summed in bfloat16 or wider, within the bound.
No kernel may reach another device: no remote copies, remote signals or barrier semaphores. Data moves between devices by JAX's collectives and lax.ppermute only.
A program may use at most 64 MiB of HBM per device.

v0:
```python
import jax
import jax.numpy as jnp
from jax import lax
from jax.sharding import PartitionSpec as P


def combined_all(part, axis, combine):
    gathered = jax.tree.map(lambda a: lax.all_gather(a, axis), part)

    def take(source):
        return jax.tree.map(lambda a: lax.dynamic_index_in_dim(a, source, 0, False), gathered)

    return lax.fori_loop(
        1, lax.axis_size(axis), lambda source, state: combine(state, take(source)), take(0)
    )


def build_slice(band_weights, band_start, planes):
    offsets = planes[None, None, :] - band_start[:, :, None]
    taps = jnp.arange(band_weights.shape[2], dtype=jnp.int32)
    hits = offsets[..., None] == taps
    values = jnp.where(hits, band_weights.astype(jnp.float32)[:, :, None, :], jnp.float32(0.0))
    return jnp.sum(values, axis=-1)


def combine_scores(first, second):
    top_one, total_one = first
    top_two, total_two = second
    joined = jnp.maximum(top_one, top_two)
    return (joined, total_one * jnp.exp(top_one - joined) + total_two * jnp.exp(top_two - joined))


def local(volumes, band_weights, band_start, images, noise_precision, log_prior):
    plane_count, classes, block = volumes.shape
    all_planes = plane_count * lax.axis_size("slab")
    slice_own = build_slice(band_weights, band_start, jnp.arange(all_planes, dtype=jnp.int32))
    gathered = lax.all_gather(volumes, "slab", axis=0, tiled=True)
    projection = jnp.einsum(
        "koz,zkp->okp", slice_own.astype(jnp.bfloat16), gathered, preferred_element_type=jnp.float32
    ).astype(jnp.bfloat16)
    piece = lax.all_gather(projection, "batch", axis=2, tiled=True)
    columns = images
    inner = jnp.einsum("okp,np->kon", piece, columns, preferred_element_type=jnp.float32)
    wide = piece.astype(jnp.float32)
    inner, energy = (inner, jnp.sum(wide * wide, axis=2))
    score = (
        noise_precision[None, None, :] * (inner - 0.5 * energy.T[:, :, None])
        + log_prior[:, :, None]
    )
    local_top = jnp.max(score, axis=(0, 1))
    local_total = jnp.sum(jnp.exp(score - local_top[None, None, :]), axis=(0, 1))
    top, total = combined_all((local_top, local_total), "slab", combine_scores)
    log_evidence = top + jnp.log(total)
    responsibilities = jnp.exp(score - log_evidence[None, None, :])
    weights = responsibilities.astype(jnp.bfloat16)
    columns = images
    image_sum = lax.psum_scatter(
        jnp.einsum("np,kon->pko", columns, weights, preferred_element_type=jnp.float32),
        "batch",
        scatter_dimension=0,
        tiled=True,
    )
    backprojection = lax.psum_scatter(
        jnp.einsum("koz,pko->zkp", slice_own, image_sum, precision=lax.Precision.HIGHEST),
        "slab",
        scatter_dimension=0,
        tiled=True,
    )
    return (responsibilities, log_evidence, backprojection)


def solution(mesh):
    in_specs = (
        P("slab", None, "batch"),
        P(None, "slab", None),
        P(None, "slab"),
        P("batch", None),
        P("batch"),
        P(None, "slab"),
    )
    out_specs = (P(None, "slab", "batch"), P("batch"), P("slab", None, "batch"))
    return jax.shard_map(local, mesh=mesh, in_specs=in_specs, out_specs=out_specs, check_vma=False)
```

profile of v0, /device:TPU:0, one launch (start us, length us, event | category | flops | bytes accessed | tf_op | source)
XLA Modules:
  0.0 477.5 jit_solution(3316003074103698807)
XLA Ops:
  7.2 0.0 all-gather.7.cloned.1.call-start
  7.2 2.1 copy.16
  9.3 0.0 all-gather.7.cloned.1.call-update
  9.4 0.0 all-gather.9.cloned.1.call-start
  9.4 0.8 copy.15
  10.2 0.8 iota_subtract_fusion
  11.0 1.1 select_reduce_fusion
  12.1 0.0 copy-start.3
  12.1 0.0 copy-start.4
  12.1 37.8 %all-gather.7.cloned.1.call-done = bf16[256,2,4096]{2,0,1:T(8,128)(2,1)} async-done(((bf16[32,2,4096]{2,0,1:T(8,128)(2,1)}), bf16[256,2,4096]{2,0,1:T(8,128)(2,1)}) %all-gather.7.cloned.1.call-update) | async-done | bytes 4194320 | tf_op jit(solution)/shard_map/all_gather | solution.py:37
  49.9 4.0 fusion.3
  53.9 0.0 all-gather.9.cloned.1.call-update
  54.0 0.0 reduce-scatter.2.cloned.1.call-start
  54.0 80.9 %all-gather.9.cloned.1.call-done = bf16[64,2,16384]{2,0,1:T(8,128)(2,1)} async-done(((bf16[64,2,4096]{2,0,1:T(8,128)(2,1)}), bf16[64,2,16384]{2,0,1:T(8,128)(2,1)}) %all-gather.9.cloned.1.call-update) | async-done | bytes 4194320 | tf_op jit(solution)/shard_map/all_gather | solution.py:41
  134.9 0.0 copy-start
  134.9 3.3 multiply_reduce_fusion
  138.2 0.0 copy-done.3
  138.2 0.0 copy-done.4
  138.2 0.1 copy-done
  138.3 8.4 %fusion.18 = (f32[384]{0:T(512)S(1)}, f32[2,64,384]{2,1,0:T(8,128)S(1)}) fusion(f32[2,64]{1,0:T(2,128)S(1)} %copy-done.4, f32[2,64]{1,0:T(2,128)S(1)} %multiply_bitcast_fusion, bf16[64,2,16384]{2,0,1:T(8,128)(2,1)S(1)} %copy-done, bf16[384,16384]{1,0:T(8,128)(2,1)} %param.11, f32[384]{0:T(512)S(1)} %copy-done.3), kind=kOutput, calls=%fused_computation.29 | convolution fusion | flops 1610808960 | bytes 16977920 | tf_op jit(solution)/shard_map/okp,np->kon/dot_general | solution.py:43
  146.7 0.1 exponential_reduce_fusion
  146.8 8.9 %all-gather.3 = f32[8,1,384]{2,1,0:T(1,128)S(1)} all-gather(f32[1,1,384]{2,1,0:T(1,128)S(1)} %reshape.25), channel_id=3, replica_groups=mesh['slab'=8,'batch'=4] {'slab'}, dimensions={0}, use_global_device_ids=true | all-gather | bytes 13824 | tf_op jit(solution)/shard_map/all_gather | solution.py:8
  155.7 8.8 %all-gather.2 = f32[8,1,384]{2,1,0:T(1,128)S(1)} all-gather(f32[1,1,384]{2,1,0:T(1,128)S(1)} %reshape.23), channel_id=2, replica_groups=mesh['slab'=8,'batch'=4] {'slab'}, dimensions={0}, use_global_device_ids=true | all-gather | bytes 13824 | tf_op jit(solution)/shard_map/all_gather | solution.py:8
  164.5 0.5 while.17
  165.0 0.0 copy-start.2
  165.1 0.0 copy-start.1
  165.1 10.2 %convolution_bitcast_fusion = f32[16384,2,64]{0,2,1:T(8,128)} fusion(bf16[384,16384]{1,0:T(8,128)(2,1)} %param.11, f32[2,64,384]{2,1,0:T(8,128)S(1)} %subtract_exponential_fusion), kind=kOutput, calls=%fused_computation.3 | convolution fusion | flops 1610661888 | bytes 21168128 | tf_op jit(solution)/shard_map/np,kon->pko/dot_general | solution.py:58
  175.3 0.0 copy-done.2
  175.3 0.0 copy-done.1
  175.3 0.0 reduce-scatter.2.cloned.1.call-update
  175.3 0.2 all-reduce.3.cloned.1.call-start
  175.6 142.0 %reduce-scatter.2.cloned.1.call-done = f32[4096,2,64]{0,2,1:T(8,128)} async-done(((f32[16384,2,64]{0,2,1:T(8,128)}), f32[4096,2,64]{0,2,1:T(8,128)}) %reduce-scatter.2.cloned.1.call-update) | async-done | bytes 2097168 | tf_op jit(solution)/shard_map/reduce_scatter | solution.py:57
  317.6 10.1 %convolution_bitcast_fusion.1 = f32[256,2,4096]{0,2,1:T(8,128)} fusion(f32[4096,2,64]{0,2,1:T(8,128)} %reduce-scatter.2.cloned.1.call-done, f32[2,64,256]{2,1,0:T(8,128)S(1)} %select_reduce_fusion), kind=kOutput, calls=%fused_computation.8 | convolution fusion | flops 1610612736 | bytes 10616832 | tf_op jit(solution)/shard_map/koz,pko->zkp/dot_general | solution.py:64
  327.7 13.4 %copy.17 = f32[256,2,4096]{2,1,0:T(2,128)} copy(f32[256,2,4096]{0,2,1:T(8,128)} %convolution_bitcast_fusion.1) | data formatting | bytes 16777216 | tf_op jit(solution)/shard_map/koz,pko->zkp/transpose | solution.py:64
  341.2 0.0 copy-start.5
  341.2 0.0 all-reduce.3.cloned.1.call-update
  341.2 0.6 copy-done.5
  341.8 0.6 dynamic-slice
  343.0 125.6 %all-reduce.3.cloned.1.call-done = f32[256,2,4096]{2,1,0:T(2,128)} async-done(((f32[256,2,4096]{2,1,0:T(2,128)}), f32[256,2,4096]{2,1,0:T(2,128)}) %all-reduce.3.cloned.1.call-update) | async-done | bytes 8388624
  468.6 2.3 constant_dynamic-slice_fusion
  (23 shorter events, 0.4 us)
Async XLA Ops:
  7.2 42.8 %all-gather.7.cloned.1.call-start = ((), (), s32[]{:S(2)}) async-start(), calls=%async_computation.1 | async-start | bytes 4718592 | tf_op jit(solution)/shard_map/all_gather | solution.py:37
  9.4 125.5 %all-gather.9.cloned.1.call-start = ((), (), s32[]{:S(2)}) async-start(), calls=%async_computation.2 | async-start | bytes 5242880 | tf_op jit(solution)/shard_map/all_gather | solution.py:41
  12.1 126.1 %copy-start.3 = (f32[384]{0:T(512)S(1)}, f32[384]{0:T(512)}, u32[]{:S(2)}) copy-start(f32[384]{0:T(512)} %param.12) | copy-start | bytes 4612
  12.1 126.1 %copy-start.4 = (f32[2,64]{1,0:T(2,128)S(1)}, f32[2,64]{1,0:T(2,128)}, u32[]{:S(2)}) copy-start(f32[2,64]{1,0:T(2,128)} %param.13) | copy-start | bytes 1540
  54.0 263.6 %reduce-scatter.2.cloned.1.call-start = ((), (), s32[]{:S(2)}) async-start(), calls=%async_computation.3 | async-start | bytes 10485760 | tf_op jit(solution)/shard_map/reduce_scatter | solution.py:57
  134.9 3.4 copy-start
  165.0 10.3 %copy-start.2 = (f32[384]{0:T(512)}, f32[384]{0:T(512)S(1)}, u32[]{:S(2)}) copy-start(f32[384]{0:T(512)S(1)} %log_add_fusion) | copy-start | bytes 4612
  165.1 10.2 %copy-start.1 = (f32[2,64,384]{2,1,0:T(8,128)}, f32[2,64,384]{2,1,0:T(8,128)S(1)}, u32[]{:S(2)}) copy-start(f32[2,64,384]{2,1,0:T(8,128)S(1)} %subtract_exponential_fusion) | copy-start | bytes 589828
  175.3 293.3 %all-reduce.3.cloned.1.call-start = ((), (), s32[]{:S(2)}) async-start(), calls=%async_computation.4 | async-start | bytes 16777216
  341.2 0.7 copy-start.5
Sparse Core Ops, SparseCore 0:
  10.5 39.4 all-gather.6
  54.1 80.7 all-gather.8
  175.5 142.0 reduce-scatter.1
  341.3 127.3 all-reduce.2
where the time goes:
time: 478 us; the launch traced here: 477 us
  waiting for transfers between devices  386 us (81%)
  matrix products  32.8 us (7%)
  local copies, waits for them, and re-layouts  20.3 us (4%)
  blocking collectives  17.7 us (4%)
  between operations  14.5 us (3%)
  other arithmetic  5.38 us (1%)
    reduce_scatter x1, waiting for transfers between devices, local(): lax.psum_scatter(jnp.einsum('np,kon->pko', columns, weights, preferred_el...  142 us
    unnamed x5, waiting for transfers between devices  126 us
    all_gather x1, waiting for transfers between devices, local(): piece = lax.all_gather(projection, 'batch', axis=2, tiled=True)  80.9 us
    all_gather x1, waiting for transfers between devices, local(): gathered = lax.all_gather(volumes, 'slab', axis=0, tiled=True)  37.8 us
    all_gather x2, blocking collectives, combined_all(): gathered = jax.tree.map(lambda a: lax.all_gather(a, axis), part)  17.7 us
    transpose x1, local copies, waits for them, and re-layouts, local(): jnp.einsum('koz,pko->zkp', slice_own, image_sum, precision=lax.Precision....  13.4 us
    dot_general x1, matrix products, local(): jnp.einsum('np,kon->pko', columns, weights, preferred_element_type=jnp.fl...  10.2 us
    dot_general x1, matrix products, local(): jnp.einsum('koz,pko->zkp', slice_own, image_sum, precision=lax.Precision....  10.1 us
  transfers between devices with their start and end apart: 4, of which 4 were waited for; matrix products, arithmetic and copies ran while one was open for 1% of the time, Pallas kernels for 0%

commit v1 on v0

v1 whole, which is shorter than its diff:
```python
import jax
import jax.numpy as jnp
import numpy as np
from jax import lax
from jax.sharding import PartitionSpec as P


def build_slice(band_weights, band_start, planes):
    offsets = planes[None, None, :] - band_start[:, :, None]
    taps = jnp.arange(band_weights.shape[2], dtype=jnp.int32)
    hits = offsets[..., None] == taps
    values = jnp.where(hits, band_weights[:, :, None, :], jnp.float32(0.0))
    return jnp.sum(values, axis=-1)


def shifted(value, axis, step):
    size = lax.axis_size(axis)
    return lax.ppermute(value, axis, [(i, (i + step) % size) for i in range(size)])


def folded_ring(size):
    return list(range(0, size, 2)) + list(range(size - 1 - size % 2, 0, -2))


def paired(value, masks):
    size = lax.axis_size("slab")
    return lax.ppermute(value, "slab", [(i, i ^ masks[i % 2]) for i in range(size)])


def gather_blocks(block):
    size = lax.axis_size("slab")
    bits = [1 << i for i in range(1, size.bit_length() - 1)]
    held = block[None]
    for up, down in zip(bits, reversed(bits)):
        held = jnp.concatenate([held, paired(held, (up, down))])
    return held, paired(held, (1, 1))


def held_masks(size, core):
    bits = [1 << i for i in range(1, size.bit_length() - 1)]
    masks = [0]
    for bit in bits if core == 0 else reversed(bits):
        masks = masks + [mask ^ bit for mask in masks]
    return masks


def local(volumes, band_weights, band_start, images, noise_precision, log_prior):
    planes, classes, block = volumes.shape
    slabs, batches = lax.axis_size("slab"), lax.axis_size("batch")
    slab, batch = lax.axis_index("slab"), lax.axis_index("batch")
    all_planes = planes * slabs
    strip = block // slabs
    own_o = band_weights.shape[1]
    particles = images.shape[0]
    rows = particles // slabs
    f32, bf16 = jnp.float32, jnp.bfloat16

    def fetch(step):
        column = lax.rem(batch + step, batches) * block
        part = lax.dynamic_slice(images, (slab * rows, column), (rows, block))
        return shifted(part, "batch", step)

    fetched = {step: fetch(step) for step in range(1, batches)}

    strips = lax.all_to_all(
        jnp.transpose(volumes, (1, 0, 2)), "slab", split_axis=2, concat_axis=1, tiled=True
    )
    table = jnp.concatenate(
        [
            band_weights.astype(f32),
            band_start.astype(f32)[:, :, None],
        ],
        axis=2,
    )
    table = lax.all_gather(table, "slab", axis=1, tiled=True)
    all_slices = build_slice(
        table[:, :, :-1], table[:, :, -1].astype(jnp.int32), jnp.arange(all_planes, dtype=jnp.int32)
    ).astype(bf16)

    ring = folded_ring(batches)
    place_of = np.argsort(ring)
    hops = [(ring[i], ring[(i + 1) % batches]) for i in range(batches)]
    place = jnp.asarray(place_of, jnp.int32)[batch]
    inner = 0.0
    energy = 0.0
    for step in range(batches):
        owner = jnp.asarray(ring, jnp.int32)[lax.rem(place + batches - step, batches)]
        following = lax.ppermute(strips, "batch", hops) if step < batches - 1 else None
        projection = jnp.einsum(
            "koz,kzp->kop", all_slices, strips, preferred_element_type=f32
        ).astype(bf16)
        columns = lax.dynamic_slice(
            images, (0, owner * block + slab * strip), (particles, strip)
        )
        inner = inner + jnp.einsum("kop,np->kon", projection, columns, preferred_element_type=f32)
        wide = projection.astype(f32)
        energy = energy + jnp.sum(wide * wide, axis=2)
        strips = following

    partial = inner - 0.5 * energy[:, :, None]
    partial = partial.reshape(classes, slabs, own_o, particles)
    partial = lax.all_to_all(partial, "slab", split_axis=1, concat_axis=1, tiled=True)
    score = noise_precision[None, None, :] * jnp.sum(partial, axis=1) + log_prior[:, :, None]

    own_top = jnp.max(score, axis=(0, 1))
    shifted_exp = jnp.exp(score - own_top)
    own_total = jnp.sum(shifted_exp, axis=(0, 1))
    tops, totals = lax.all_gather((own_top, own_total), "slab")
    exps = lax.all_gather(shifted_exp.astype(bf16), "slab")
    top = jnp.max(tops, axis=0)
    total = jnp.sum(totals * jnp.exp(tops - top), axis=0)
    log_evidence = top + jnp.log(total)
    responsibilities = jnp.exp(score - log_evidence)
    scale = jnp.exp(tops - log_evidence)
    weights = (exps.astype(f32) * scale[:, None, None, :]).astype(bf16)

    own_slices = lax.dynamic_slice_in_dim(all_slices, slab * planes, planes, axis=2)
    own_slices = own_slices.reshape(classes, slabs, own_o, planes)
    inserted = jnp.einsum("ksoz,skon->nkz", own_slices, weights, preferred_element_type=f32)
    inserted = inserted.astype(bf16).reshape(particles, classes * planes)

    def back(values, pixels):
        return jnp.einsum("nz,np->zp", values, pixels, preferred_element_type=f32)

    result = back(inserted, lax.dynamic_slice_in_dim(images, batch * block, block, axis=1))

    by_rows = inserted.reshape(slabs, rows, classes * planes)
    orders = jnp.asarray([held_masks(slabs, core) for core in (0, 1)], jnp.int32)
    order = slab ^ orders[slab % 2]
    order = jnp.concatenate([order, slab ^ 1 ^ orders[1 - slab % 2]])
    by_rows = jnp.take(by_rows, order, axis=0).reshape(2, particles // 2, classes * planes)
    for step in range(1, batches):
        mine, other = gather_blocks(fetched[step])
        there = shifted(by_rows, "batch", step)
        result = result + back(there[0], mine.reshape(particles // 2, block))
        result = result + back(there[1], other.reshape(particles // 2, block))
    backprojection = jnp.transpose(result.reshape(classes, planes, block), (1, 0, 2))
    return (responsibilities, log_evidence, backprojection)


def solution(mesh):
    in_specs = (
        P("slab", None, "batch"),
        P(None, "slab", None),
        P(None, "slab"),
        P("batch", None),
        P("batch"),
        P(None, "slab"),
    )
    out_specs = (P(None, "slab", "batch"), P("batch"), P("slab", None, "batch"))
    return jax.shard_map(local, mesh=mesh, in_specs=in_specs, out_specs=out_specs, check_vma=False)
```

time: 478 us -> 182 us (0.38)
  waiting for transfers between devices: 386 us -> 34.2 us
  starting transfers between devices: 0.34 us -> 37.6 us
  blocking collectives: 17.7 us -> 36.6 us
  other arithmetic: 5.38 us -> 18.7 us
  matrix products: 32.8 us -> 23 us
  between operations: 14.5 us -> 6.28 us
    reduce_scatter x1 -> x0, waiting for transfers between devices: 142 us -> none  [local(): lax.psum_scatter(jnp.einsum('np,kon->pko', columns, weights, preferred_el...]
    unnamed x5 -> x0, waiting for transfers between devices: 126 us -> none
    all_gather x2 -> x0, waiting for transfers between devices: 119 us -> none  [the longest x1 80.9 us: local(): piece = lax.all_gather(projection, 'batch', axis=2, tiled=True)]
    ppermute x0 -> x18, starting transfers between devices: none -> 27.4 us  [the longest x6 10.1 us: shifted(): lax.ppermute(value, axis, [(i, (i + step) % size) for i in range(size)])]
    ppermute x0 -> x18, waiting for transfers between devices: none -> 20.9 us  [the longest x3 14.6 us: local(): lax.ppermute(strips, 'batch', hops)]
    all_gather x2 -> x4, blocking collectives: 17.7 us -> 36.6 us  [the longest x2 16.8 us: local(): tops, totals = lax.all_gather((own_top, own_total), 'slab')]
    transpose x1 -> x0, local copies, waits for them, and re-layouts: 13.4 us -> none  [local(): jnp.einsum('koz,pko->zkp', slice_own, image_sum, precision=lax.Precision....]
    all_to_all x0 -> x2, waiting for transfers between devices: none -> 13.2 us  [the longest x1 13.2 us: local(): lax.all_to_all(partial, 'slab', split_axis=1, concat_axis=1, tiled=True)]
  transfers between devices with their start and end apart: 4 -> 20, of which waited for: 4 -> 5; matrix products, arithmetic and copies ran while one was open for 1% -> 28% of each run, Pallas kernels for 0% -> 0%
where the time goes in v1:
time: 182 us; the launch traced here: 180 us
  starting transfers between devices  37.6 us (21%)
  blocking collectives  36.6 us (20%)
  waiting for transfers between devices  34.2 us (19%)
  local copies, waits for them, and re-layouts  24.2 us (13%)
  matrix products  23 us (13%)
  other arithmetic  18.7 us (10%)
  between operations  6.28 us (3%)
    all_gather x2, blocking collectives, local(): tops, totals = lax.all_gather((own_top, own_total), 'slab')  16.8 us
    ppermute x3, waiting for transfers between devices, local(): lax.ppermute(strips, 'batch', hops)  14.6 us
    unnamed x37, local copies, waits for them, and re-layouts  13.3 us
    all_to_all x1, waiting for transfers between devices, local(): lax.all_to_all(partial, 'slab', split_axis=1, concat_axis=1, tiled=True)  13.2 us
    dot_general x7, matrix products, back(): return jnp.einsum('nz,np->zp', values, pixels, preferred_element_type=f32)  12.4 us
    concatenate x6, other arithmetic, gather_blocks(): held = jnp.concatenate([held, paired(held, (up, down))])  10.9 us
    all_gather x1, blocking collectives, local(): table = lax.all_gather(table, 'slab', axis=1, tiled=True)  10.4 us
    ppermute x6, starting transfers between devices, shifted(): lax.ppermute(value, axis, [(i, (i + step) % size) for i in range(size)])  10.1 us
  transfers between devices with their start and end apart: 20, of which 5 were waited for; matrix products, arithmetic and copies ran while one was open for 28% of the time, Pallas kernels for 0%

profile of v1, /device:TPU:0, one launch (start us, length us, event | category | flops | bytes accessed | tf_op | source)
XLA Modules:
  0.0 180.4 jit_solution(3109829155374053534)
XLA Ops:
  0.6 6.0 %copy.151 = bf16[32,2,4096]{0,1,2:T(2,128)(2,1)} copy(bf16[32,2,4096]{2,1,0:T(2,128)(2,1)} %param.12) | data formatting | bytes 1048576 | tf_op args[0]
  6.6 3.2 %bitcast_bitcast_fusion = bf16[4096,2,32]{2,1,0:T(2,128)(2,1)S(1)} fusion(bf16[32,2,4096]{0,1,2:T(2,128)(2,1)} %copy.151), kind=kLoop, calls=%fused_computation.96 | loop fusion | bytes 1048576
  9.8 2.7 %reshape.229 = bf16[8,2,16384]{2,1,0:T(2,128)(2,1)} reshape(bf16[4096,2,32]{2,1,0:T(2,128)(2,1)S(1)} %bitcast_bitcast_fusion) | data formatting | bytes 1048576
  12.5 5.3 %all-to-all-start = ((bf16[8,2,16384]{2,1,0:T(2,128)(2,1)}), bf16[8,2,16384]{2,1,0:T(2,128)(2,1)S(1)}, u32[]{:S(2)}, u32[]{:S(2)}) async-start(bf16[8,2,16384]{2,1,0:T(2,128)(2,1)} %reshape.229), calls=%async_computation | async-start | bytes 1048576 | tf_op jit(solution)/shard_map/all_to_all | solution.py:65
  17.8 2.3 %fusion.45 = (bf16[48,4096]{1,0:T(8,128)(2,1)}, bf16[48,4096]{1,0:T(8,128)(2,1)}, bf16[48,4096]{1,0:T(8,128)(2,1)}) fusion(bf16[384,16384]{1,0:T(8,128)(2,1)} %param.15, s32[]{:T(128)S(6)} %select_n.106, s32[]{:T(128)S(6)} %select_n.107, s32[]{:T(128)S(6)} %select_n.109, s32[]{:T(128)S(6)} %select_n.108), kind=kLoop, calls=%fused_computation.94 | loop fusion | bytes 2359312 | tf_op jit(solution)/shard_map/dynamic_slice | solution.py:60
  20.1 3.6 %collective-permute-start.14 = (bf16[48,4096]{1,0:T(8,128)(2,1)}, bf16[48,4096]{1,0:T(8,128)(2,1)}, u32[]{:S(2)}, u32[]{:S(2)}) collective-permute-start(bf16[48,4096]{1,0:T(8,128)(2,1)} %get-tuple-element.4), channel_id=1, source_target_pairs={{0,3},{1,0},{2,1},{3,2},{4,7},{5,4},{6,5},{7,6},{8,11},{9,8},{10,9... | collective-permute-start | bytes 1179656 | tf_op jit(solution)/shard_map/ppermute | solution.py:18
  23.7 1.0 collective-permute-start.4
  24.9 10.4 %all_gather.19 = f32[2,512,33]{2,0,1:T(2,128)S(1)} all-gather(f32[2,64,33]{2,0,1:T(2,128)S(1)} %copy.148), channel_id=1, replica_groups=mesh['slab'=8,'batch'=4] {'slab'}, dimensions={1}, use_global_device_ids=true | all-gather | bytes 152064 | tf_op jit(solution)/shard_map/all_gather | solution.py:75
  36.7 6.0 %select_reduce_fusion = bf16[2,512,256]{2,1,0:T(8,128)(2,1)S(1)} fusion(f32[2,512,32]{2,1,0:T(8,128)S(1)} %copy.150, s32[2,512,256]{2,1,0:T(8,128)S(1)} %iota_subtract_fusion), kind=kLoop, calls=%fused_computation.1 | loop fusion | flops 24903680 | bytes 1703936 | tf_op jit(solution)/shard_map/reduce_sum | solution.py:13
  50.4 1.5 collective-permute-start.15
  51.8 6.3 %collective-permute-done.9 = bf16[48,4096]{1,0:T(8,128)(2,1)S(1)} collective-permute-done((bf16[48,4096]{1,0:T(8,128)(2,1)}, bf16[48,4096]{1,0:T(8,128)(2,1)S(1)}, u32[]{:S(2)}, u32[]{:S(2)}) %collective-permute-start.9) | collective-permute-done | bytes 393248 | tf_op jit(solution)/shard_map/ppermute | solution.py:18
  58.1 1.7 collective-permute-start.10
  60.2 1.0 reshape.230
  61.2 1.3 copy.177
  62.5 1.5 multiply_reduce_fusion.3
  64.3 2.5 %collective-permute-start = (bf16[2,256,512]{1,2,0:T(8,128)(2,1)S(1)}, bf16[2,256,512]{1,2,0:T(8,128)(2,1)S(1)}, u32[]{:S(2)}, u32[]{:S(2)}) collective-permute-start(bf16[2,256,512]{1,2,0:T(8,128)(2,1)S(1)} %copy.156), channel_id=1, source_target_pairs={{0,2},{2,3},{3,1},{1,0},{4,6},{6,7},{7,5},{5,4},{8,10},{10,11},{11... | collective-permute-start | bytes 1572872 | tf_op jit(solution)/shard_map/ppermute | solution.py:88
  66.8 1.7 fusion.13
  68.5 2.1 %pad_maximum_fusion.5 = bf16[2,48,4096]{2,1,0:T(8,128)(2,1)} fusion(bf16[1,48,4096]{2,1,0:T(8,128)(2,1)} %collective-permute-done.15, bf16[1,48,4096]{2,1,0:T(8,128)(2,1)} %bitcast.44), kind=kLoop, calls=%fused_computation.30 | loop fusion | flops 393216 | bytes 1572864 | tf_op jit(solution)/shard_map/concatenate | solution.py:35
  70.6 1.5 collective-permute-start.16
  72.1 1.1 pad_maximum_fusion.4
  73.8 1.1 pad_maximum_fusion.3
  74.8 1.5 collective-permute-start.6
  77.3 3.3 %collective-permute-start.1 = (bf16[2,256,512]{1,2,0:T(8,128)(2,1)S(1)}, bf16[2,256,512]{1,2,0:T(8,128)(2,1)S(1)}, u32[]{:S(2)}, u32[]{:S(2)}) collective-permute-start(bf16[2,256,512]{1,2,0:T(8,128)(2,1)S(1)} %collective-permute-done), channel_id=1, source_target_pairs={{0,2},{2,3},{3,1},{1,0},{4,6},{6,7},{7,5},{5,4},{8,10},{10,11},{11... | collective-permute-start | bytes 1572872 | tf_op jit(solution)/shard_map/ppermute | solution.py:88
  81.1 1.8 fusion.11
  82.8 7.3 %collective-permute-done.1 = bf16[2,256,512]{1,2,0:T(8,128)(2,1)S(1)} collective-permute-done((bf16[2,256,512]{1,2,0:T(8,128)(2,1)S(1)}, bf16[2,256,512]{1,2,0:T(8,128)(2,1)S(1)}, u32[]{:S(2)}, u32[]{:S(2)}) %collective-permute-start.1) | collective-permute-done | bytes 524320 | tf_op jit(solution)/shard_map/ppermute | solution.py:88
  90.1 3.4 %collective-permute-start.2 = (bf16[2,256,512]{1,2,0:T(8,128)(2,1)S(1)}, bf16[2,256,512]{1,2,0:T(8,128)(2,1)S(1)}, u32[]{:S(2)}, u32[]{:S(2)}) collective-permute-start(bf16[2,256,512]{1,2,0:T(8,128)(2,1)S(1)} %collective-permute-done.1), channel_id=1, source_target_pairs={{0,2},{2,3},{3,1},{1,0},{4,6},{6,7},{7,5},{5,4},{8,10},{10,11},{11... | collective-permute-start | bytes 1572872 | tf_op jit(solution)/shard_map/ppermute | solution.py:88
  94.0 1.7 fusion.9
  95.7 6.4 %collective-permute-done.2 = bf16[2,256,512]{1,2,0:T(8,128)(2,1)S(1)} collective-permute-done((bf16[2,256,512]{1,2,0:T(8,128)(2,1)S(1)}, bf16[2,256,512]{1,2,0:T(8,128)(2,1)S(1)}, u32[]{:S(2)}, u32[]{:S(2)}) %collective-permute-start.2) | collective-permute-done | bytes 524320 | tf_op jit(solution)/shard_map/ppermute | solution.py:88
  102.6 2.1 %add_subtract_fusion = f32[2,512,384]{2,1,0:T(8,128)S(1)} fusion(f32[2,512,384]{2,1,0:T(8,128)S(1)} %fusion.9, f32[2,512,384]{2,1,0:T(8,128)S(1)} %fusion.13, f32[2,512,384]{2,1,0:T(8,128)S(1)} %fusion.11, bf16[2,512,512]{1,2,0:T(8,128)(2,1)S(1)} %get-tuple-element.15, f32[2,512]{1,0:T(2,128)S(1)} %add_multiply_fusion, bf16[384,16384]{1,0:T(8,128)(2,1)} %param.15, ...), kind=kOutput, calls=%fused_computation.19 | convolution fusion | flops 404226048 | bytes 7737348 | tf_op jit(solution)/shard_map/kop,np->kon/dot_general | solution.py:95
  104.7 1.3 copy.160
  106.0 4.8 %all-to-all-start.1 = ((f32[2,8,64,384]{3,2,0,1:T(8,128)}), f32[2,8,64,384]{3,2,0,1:T(8,128)S(1)}, u32[]{:S(2)}, u32[]{:S(2)}) async-start(f32[2,8,64,384]{3,2,0,1:T(8,128)} %copy.160), calls=%async_computation.1 | async-start | bytes 3145728 | tf_op jit(solution)/shard_map/all_to_all | solution.py:102
  110.8 2.7 %pad_maximum_fusion.2 = bf16[4,48,4096]{2,1,0:T(8,128)(2,1)} fusion(bf16[2,48,4096]{2,1,0:T(8,128)(2,1)} %collective-permute-done.16, bf16[1,48,4096]{2,1,0:T(8,128)(2,1)} %collective-permute-done.15, bf16[1,48,4096]{2,1,0:T(8,128)(2,1)} %bitcast.44), kind=kLoop, calls=%fused_computation.17 | loop fusion | flops 1572864 | bytes 3145728 | tf_op jit(solution)/shard_map/concatenate | solution.py:35
  114.0 2.5 %pad_maximum_fusion.1 = bf16[4,48,4096]{2,1,0:T(8,128)(2,1)} fusion(bf16[2,48,4096]{2,1,0:T(8,128)(2,1)} %collective-permute-done.11, bf16[1,48,4096]{2,1,0:T(8,128)(2,1)} %collective-permute-done.10, bf16[1,48,4096]{2,1,0:T(8,128)(2,1)S(1)} %bitcast.151), kind=kLoop, calls=%fused_computation.16 | loop fusion | flops 1572864 | bytes 3145728 | tf_op jit(solution)/shard_map/concatenate | solution.py:35
  116.7 1.4 pad_maximum_fusion
  118.6 13.2 %all-to-all-done.1 = f32[2,8,64,384]{3,2,0,1:T(8,128)S(1)} async-done(((f32[2,8,64,384]{3,2,0,1:T(8,128)}), f32[2,8,64,384]{3,2,0,1:T(8,128)S(1)}, u32[]{:S(2)}, u32[]{:S(2)}) %all-to-all-start.1) | async-done | bytes 1572896 | tf_op jit(solution)/shard_map/all_to_all | solution.py:102
  132.2 7.9 %all-gather.2 = f32[8,1,384]{2,1,0:T(1,128)S(1)} all-gather(f32[1,1,384]{2,1,0:T(1,128)S(1)} %reshape.218), channel_id=2, replica_groups=mesh['slab'=8,'batch'=4] {'slab'}, dimensions={0}, use_global_device_ids=true | all-gather | bytes 13824 | tf_op jit(solution)/shard_map/all_gather | solution.py:108
  140.1 8.8 %all-gather.3 = f32[8,1,384]{2,1,0:T(1,128)S(1)} all-gather(f32[1,1,384]{2,1,0:T(1,128)S(1)} %reshape.220), channel_id=3, replica_groups=mesh['slab'=8,'batch'=4] {'slab'}, dimensions={0}, use_global_device_ids=true | all-gather | bytes 13824 | tf_op jit(solution)/shard_map/all_gather | solution.py:108
  149.2 9.5 %all_gather.24 = bf16[8,2,64,384]{3,2,1,0:T(8,128)(2,1)S(1)} all-gather(bf16[1,2,64,384]{3,2,1,0:T(8,128)(2,1)S(1)} %fusion.23), channel_id=1, replica_groups=mesh['slab'=8,'batch'=4] {'slab'}, dimensions={0}, use_global_device_ids=true | all-gather | bytes 884736 | tf_op jit(solution)/shard_map/all_gather | solution.py:109
  159.9 2.3 %collective-permute-start.13 = (bf16[2,192,64]{2,1,0:T(8,128)(2,1)S(1)}, bf16[2,192,64]{2,1,0:T(8,128)(2,1)S(1)}, u32[]{:S(2)}, u32[]{:S(2)}) collective-permute-start(bf16[2,192,64]{2,1,0:T(8,128)(2,1)S(1)} %bitcast_select_fusion), channel_id=1, source_target_pairs={{0,3},{1,0},{2,1},{3,2},{4,7},{5,4},{6,5},{7,6},{8,11},{9,8},{10,9... | collective-permute-start | bytes 147464 | tf_op jit(solution)/shard_map/ppermute | solution.py:18
  162.2 1.3 collective-permute-start.8
  164.2 2.6 %fusion.4 = f32[64,4096]{1,0:T(8,128)S(1)} fusion(bf16[384,64]{0,1:T(8,128)(2,1)S(1)} %bitcast.155, bf16[384,16384]{1,0:T(8,128)(2,1)} %param.15, s32[]{:T(128)S(6)} %select_n.99), kind=kOutput, calls=%fused_computation.9 | convolution fusion | flops 201326592 | bytes 4243460 | tf_op jit(solution)/shard_map/nz,np->zp/dot_general | solution.py:123
  166.8 2.0 %collective-permute-start.3 = (bf16[2,192,64]{2,1,0:T(8,128)(2,1)S(1)}, bf16[2,192,64]{2,1,0:T(8,128)(2,1)S(1)}, u32[]{:S(2)}, u32[]{:S(2)}) collective-permute-start(bf16[2,192,64]{2,1,0:T(8,128)(2,1)S(1)} %bitcast_select_fusion), channel_id=1, source_target_pairs={{0,1},{1,2},{2,3},{3,0},{4,5},{5,6},{6,7},{7,4},{8,9},{9,10},{10,1... | collective-permute-start | bytes 147464 | tf_op jit(solution)/shard_map/ppermute | solution.py:18
  168.8 1.8 %fusion.25 = f32[64,4096]{1,0:T(8,128)S(1)} fusion(bf16[192,4096]{1,0:T(8,128)(2,1)} %bitcast.47, bf16[2,192,64]{2,1,0:T(8,128)(2,1)S(1)} %collective-permute-done.13), kind=kOutput, calls=%fused_computation.55 | convolution fusion | flops 100663296 | bytes 2670592 | tf_op jit(solution)/shard_map/nz,np->zp/dot_general | solution.py:123
  170.6 1.8 %fusion.26 = f32[64,4096]{1,0:T(8,128)S(1)} fusion(bf16[192,4096]{1,0:T(8,128)(2,1)} %bitcast.45, bf16[2,192,64]{2,1,0:T(8,128)(2,1)S(1)} %collective-permute-done.13), kind=kOutput, calls=%fused_computation.57 | convolution fusion | flops 100663296 | bytes 2670592 | tf_op jit(solution)/shard_map/nz,np->zp/dot_general | solution.py:123
  172.5 1.8 %fusion.27 = f32[64,4096]{1,0:T(8,128)S(1)} fusion(bf16[192,4096]{1,0:T(8,128)(2,1)} %bitcast.42, bf16[2,192,64]{2,1,0:T(8,128)(2,1)S(1)} %collective-permute-done.8), kind=kOutput, calls=%fused_computation.59 | convolution fusion | flops 100663296 | bytes 2670592 | tf_op jit(solution)/shard_map/nz,np->zp/dot_general | solution.py:123
  174.4 1.8 %fusion.28 = f32[64,4096]{1,0:T(8,128)S(1)} fusion(bf16[192,4096]{1,0:T(8,128)(2,1)} %bitcast.40, bf16[2,192,64]{2,1,0:T(8,128)(2,1)S(1)} %collective-permute-done.8), kind=kOutput, calls=%fused_computation.61 | convolution fusion | flops 100663296 | bytes 2670592 | tf_op jit(solution)/shard_map/nz,np->zp/dot_general | solution.py:123
  176.7 2.0 %fusion.3 = f32[64,4096]{1,0:T(8,128)S(1)} fusion(f32[64,4096]{1,0:T(8,128)S(1)} %fusion.25, f32[64,4096]{1,0:T(8,128)S(1)} %fusion.26, f32[64,4096]{1,0:T(8,128)S(1)} %fusion.27, f32[64,4096]{1,0:T(8,128)S(1)} %fusion.28, f32[64,4096]{1,0:T(8,128)S(1)} %convolution_add_fusion.1, bf16[192,4096]{1,0:T(8,128)(2,1)} %bitcast.37, ...), kind=kOutput, calls=%fused_computation.7 | convolution fusion | flops 101974016 | bytes 7913472 | tf_op jit(solution)/shard_map/nz,np->zp/dot_general | solution.py:123
  178.7 1.8 copy.189
  (94 shorter events, 11.7 us)
Async XLA Ops:
  12.5 12.2 %copy-start.13 = (s32[2,64]{1,0:T(2,128)S(1)}, s32[2,64]{1,0:T(2,128)}, u32[]{:S(2)}) copy-start(s32[2,64]{1,0:T(2,128)} %param.14) | copy-start | bytes 1540
  12.5 12.2 %copy-start.10 = (bf16[2,64,32]{1,2,0:T(8,128)(2,1)S(1)}, bf16[2,64,32]{1,2,0:T(8,128)(2,1)}, u32[]{:S(2)}) copy-start(bf16[2,64,32]{1,2,0:T(8,128)(2,1)} %param.13) | copy-start | bytes 24580
  12.5 47.7 %all-to-all-start = ((bf16[8,2,16384]{2,1,0:T(2,128)(2,1)}), bf16[8,2,16384]{2,1,0:T(2,128)(2,1)S(1)}, u32[]{:S(2)}, u32[]{:S(2)}) async-start(bf16[8,2,16384]{2,1,0:T(2,128)(2,1)} %reshape.229), calls=%async_computation | async-start | bytes 1048576 | tf_op jit(solution)/shard_map/all_to_all | solution.py:65
  20.1 30.3 %collective-permute-start.14 = (bf16[48,4096]{1,0:T(8,128)(2,1)}, bf16[48,4096]{1,0:T(8,128)(2,1)}, u32[]{:S(2)}, u32[]{:S(2)}) collective-permute-start(bf16[48,4096]{1,0:T(8,128)(2,1)} %get-tuple-element.4), channel_id=1, source_target_pairs={{0,3},{1,0},{2,1},{3,2},{4,7},{5,4},{6,5},{7,6},{8,11},{9,8},{10,9... | collective-permute-start | bytes 1179656 | tf_op jit(solution)/shard_map/ppermute | solution.py:18
  23.7 34.4 %collective-permute-start.9 = (bf16[48,4096]{1,0:T(8,128)(2,1)}, bf16[48,4096]{1,0:T(8,128)(2,1)S(1)}, u32[]{:S(2)}, u32[]{:S(2)}) collective-permute-start(bf16[48,4096]{1,0:T(8,128)(2,1)} %get-tuple-element.5), channel_id=1, source_target_pairs={{0,2},{1,3},{2,0},{3,1},{4,6},{5,7},{6,4},{7,5},{8,10},{9,11},{10,... | collective-permute-start | bytes 1179656 | tf_op jit(solution)/shard_map/ppermute | solution.py:18
  23.7 36.1 %collective-permute-start.4 = (bf16[48,4096]{1,0:T(8,128)(2,1)}, bf16[48,4096]{1,0:T(8,128)(2,1)S(1)}, u32[]{:S(2)}, u32[]{:S(2)}) collective-permute-start(bf16[48,4096]{1,0:T(8,128)(2,1)} %get-tuple-element.3), channel_id=1, source_target_pairs={{0,1},{1,2},{2,3},{3,0},{4,5},{5,6},{6,7},{7,4},{8,9},{9,10},{10,1... | collective-permute-start | bytes 1179656 | tf_op jit(solution)/shard_map/ppermute | solution.py:18
  35.8 0.7 copy-start.12
  36.1 6.7 %copy-start.14 = (s32[4]{0:T(128)S(1)}, s32[4]{0:T(128)}, u32[]{:S(2)}) copy-start(s32[4]{0:T(128)} %constant.105.clone) | copy-start | bytes 52
  36.1 9.9 %copy-start.11 = (s32[4]{0:T(128)S(1)}, s32[4]{0:T(128)}, u32[]{:S(2)}) copy-start(s32[4]{0:T(128)} %constant.106.clone) | copy-start | bytes 52
  42.7 17.5 %copy-start.4 = (bf16[2,512,256]{2,1,0:T(8,128)(2,1)}, bf16[2,512,256]{2,1,0:T(8,128)(2,1)S(1)}, u32[]{:S(2)}) copy-start(bf16[2,512,256]{2,1,0:T(8,128)(2,1)S(1)} %select_reduce_fusion) | copy-start | bytes 1572868
  50.4 18.1 %collective-permute-start.15 = (bf16[1,48,4096]{2,1,0:T(8,128)(2,1)}, bf16[1,48,4096]{2,1,0:T(8,128)(2,1)}, u32[]{:S(2)}, u32[]{:S(2)}) collective-permute-start(bf16[1,48,4096]{2,1,0:T(8,128)(2,1)} %bitcast.44), channel_id=1, source_target_pairs={{0,8},{4,20},{8,0},{12,28},{16,24},{20,4},{24,16},{28,12},{1,9},{5... | collective-permute-start | bytes 1179656 | tf_op jit(solution)/shard_map/ppermute | solution.py:27
  58.1 13.9 %copy-start.2 = (bf16[48,4096]{1,0:T(8,128)(2,1)}, bf16[48,4096]{1,0:T(8,128)(2,1)S(1)}, u32[]{:S(2)}) copy-start(bf16[48,4096]{1,0:T(8,128)(2,1)S(1)} %collective-permute-done.9) | copy-start | bytes 1179652
  58.1 13.9 %collective-permute-start.10 = (bf16[1,48,4096]{2,1,0:T(8,128)(2,1)S(1)}, bf16[1,48,4096]{2,1,0:T(8,128)(2,1)}, u32[]{:S(2)}, u32[]{:S(2)}) collective-permute-start(bf16[1,48,4096]{2,1,0:T(8,128)(2,1)S(1)} %bitcast.149), channel_id=1, source_target_pairs={{0,8},{4,20},{8,0},{12,28},{16,24},{20,4},{24,16},{28,12},{1,9},{5... | collective-permute-start | bytes 1179656 | tf_op jit(solution)/shard_map/ppermute | solution.py:27
  59.8 14.0 %copy-start = (bf16[48,4096]{1,0:T(8,128)(2,1)}, bf16[48,4096]{1,0:T(8,128)(2,1)S(1)}, u32[]{:S(2)}) copy-start(bf16[48,4096]{1,0:T(8,128)(2,1)S(1)} %collective-permute-done.4) | copy-start | bytes 1179652
  59.8 14.0 %collective-permute-start.5 = (bf16[1,48,4096]{2,1,0:T(8,128)(2,1)S(1)}, bf16[1,48,4096]{2,1,0:T(8,128)(2,1)}, u32[]{:S(2)}, u32[]{:S(2)}) collective-permute-start(bf16[1,48,4096]{2,1,0:T(8,128)(2,1)S(1)} %bitcast.146), channel_id=1, source_target_pairs={{0,8},{4,20},{8,0},{12,28},{16,24},{20,4},{24,16},{28,12},{1,9},{5... | collective-permute-start | bytes 1179656 | tf_op jit(solution)/shard_map/ppermute | solution.py:27
  64.3 13.0 %collective-permute-start = (bf16[2,256,512]{1,2,0:T(8,128)(2,1)S(1)}, bf16[2,256,512]{1,2,0:T(8,128)(2,1)S(1)}, u32[]{:S(2)}, u32[]{:S(2)}) collective-permute-start(bf16[2,256,512]{1,2,0:T(8,128)(2,1)S(1)} %copy.156), channel_id=1, source_target_pairs={{0,2},{2,3},{3,1},{1,0},{4,6},{6,7},{7,5},{5,4},{8,10},{10,11},{11... | collective-permute-start | bytes 1572872 | tf_op jit(solution)/shard_map/ppermute | solution.py:88
  70.6 10.0 %copy-start.5 = (bf16[2,512,256]{2,1,0:T(8,128)(2,1)S(1)}, bf16[2,512,256]{2,1,0:T(8,128)(2,1)}, u32[]{:S(2)}) copy-start(bf16[2,512,256]{2,1,0:T(8,128)(2,1)} %copy-done.4) | copy-start | bytes 1572868
  70.6 40.2 %collective-permute-start.16 = (bf16[2,48,4096]{2,1,0:T(8,128)(2,1)}, bf16[2,48,4096]{2,1,0:T(8,128)(2,1)}, u32[]{:S(2)}, u32[]{:S(2)}) collective-permute-start(bf16[2,48,4096]{2,1,0:T(8,128)(2,1)} %pad_maximum_fusion.5), channel_id=1, source_target_pairs={{0,16},{4,12},{8,24},{12,4},{16,0},{20,28},{24,8},{28,20},{1,17},{... | collective-permute-start | bytes 2359304 | tf_op jit(solution)/shard_map/ppermute | solution.py:27
  73.1 40.9 %collective-permute-start.11 = (bf16[2,48,4096]{2,1,0:T(8,128)(2,1)S(1)}, bf16[2,48,4096]{2,1,0:T(8,128)(2,1)}, u32[]{:S(2)}, u32[]{:S(2)}) collective-permute-start(bf16[2,48,4096]{2,1,0:T(8,128)(2,1)S(1)} %pad_maximum_fusion.4), channel_id=1, source_target_pairs={{0,16},{4,12},{8,24},{12,4},{16,0},{20,28},{24,8},{28,20},{1,17},{... | collective-permute-start | bytes 2359304 | tf_op jit(solution)/shard_map/ppermute | solution.py:27
  74.8 41.8 %collective-permute-start.6 = (bf16[2,48,4096]{2,1,0:T(8,128)(2,1)S(1)}, bf16[2,48,4096]{2,1,0:T(8,128)(2,1)}, u32[]{:S(2)}, u32[]{:S(2)}) collective-permute-start(bf16[2,48,4096]{2,1,0:T(8,128)(2,1)S(1)} %pad_maximum_fusion.3), channel_id=1, source_target_pairs={{0,16},{4,12},{8,24},{12,4},{16,0},{20,28},{24,8},{28,20},{1,17},{... | collective-permute-start | bytes 2359304 | tf_op jit(solution)/shard_map/ppermute | solution.py:27
  77.3 12.8 %collective-permute-start.1 = (bf16[2,256,512]{1,2,0:T(8,128)(2,1)S(1)}, bf16[2,256,512]{1,2,0:T(8,128)(2,1)S(1)}, u32[]{:S(2)}, u32[]{:S(2)}) collective-permute-start(bf16[2,256,512]{1,2,0:T(8,128)(2,1)S(1)} %collective-permute-done), channel_id=1, source_target_pairs={{0,2},{2,3},{3,1},{1,0},{4,6},{6,7},{7,5},{5,4},{8,10},{10,11},{11... | collective-permute-start | bytes 1572872 | tf_op jit(solution)/shard_map/ppermute | solution.py:88
  90.1 12.0 %collective-permute-start.2 = (bf16[2,256,512]{1,2,0:T(8,128)(2,1)S(1)}, bf16[2,256,512]{1,2,0:T(8,128)(2,1)S(1)}, u32[]{:S(2)}, u32[]{:S(2)}) collective-permute-start(bf16[2,256,512]{1,2,0:T(8,128)(2,1)S(1)} %collective-permute-done.1), channel_id=1, source_target_pairs={{0,2},{2,3},{3,1},{1,0},{4,6},{6,7},{7,5},{5,4},{8,10},{10,11},{11... | collective-permute-start | bytes 1572872 | tf_op jit(solution)/shard_map/ppermute | solution.py:88
  106.0 25.8 %all-to-all-start.1 = ((f32[2,8,64,384]{3,2,0,1:T(8,128)}), f32[2,8,64,384]{3,2,0,1:T(8,128)S(1)}, u32[]{:S(2)}, u32[]{:S(2)}) async-start(f32[2,8,64,384]{3,2,0,1:T(8,128)} %copy.160), calls=%async_computation.1 | async-start | bytes 3145728 | tf_op jit(solution)/shard_map/all_to_all | solution.py:102
  110.8 3.2 %copy-start.3 = (bf16[48,4096]{1,0:T(8,128)(2,1)S(1)}, bf16[48,4096]{1,0:T(8,128)(2,1)}, u32[]{:S(2)}) copy-start(bf16[48,4096]{1,0:T(8,128)(2,1)} %copy-done.2) | copy-start | bytes 1179652
  113.5 3.1 %copy-start.1 = (bf16[48,4096]{1,0:T(8,128)(2,1)S(1)}, bf16[48,4096]{1,0:T(8,128)(2,1)}, u32[]{:S(2)}) copy-start(bf16[48,4096]{1,0:T(8,128)(2,1)} %copy-done) | copy-start | bytes 1179652
  113.5 53.2 %collective-permute-start.17 = (bf16[4,48,4096]{2,1,0:T(8,128)(2,1)}, bf16[4,48,4096]{2,1,0:T(8,128)(2,1)}, u32[]{:S(2)}, u32[]{:S(2)}) collective-permute-start(bf16[4,48,4096]{2,1,0:T(8,128)(2,1)} %pad_maximum_fusion.2), channel_id=1, source_target_pairs={{0,4},{4,0},{8,12},{12,8},{16,20},{20,16},{24,28},{28,24},{1,5},{5... | collective-permute-start | bytes 4718600 | tf_op jit(solution)/shard_map/ppermute | solution.py:27
  116.6 55.9 %collective-permute-start.12 = (bf16[4,48,4096]{2,1,0:T(8,128)(2,1)}, bf16[4,48,4096]{2,1,0:T(8,128)(2,1)}, u32[]{:S(2)}, u32[]{:S(2)}) collective-permute-start(bf16[4,48,4096]{2,1,0:T(8,128)(2,1)} %pad_maximum_fusion.1), channel_id=1, source_target_pairs={{0,4},{4,0},{8,12},{12,8},{16,20},{20,16},{24,28},{28,24},{1,5},{5... | collective-permute-start | bytes 4718600 | tf_op jit(solution)/shard_map/ppermute | solution.py:27
  118.0 13.9 %copy-start.7 = (f32[384]{0:T(512)S(1)}, f32[384]{0:T(512)}, u32[]{:S(2)}) copy-start(f32[384]{0:T(512)} %param.16) | copy-start | bytes 4612
  118.1 13.9 %copy-start.9 = (f32[2,64]{1,0:T(2,128)S(1)}, f32[2,64]{1,0:T(2,128)}, u32[]{:S(2)}) copy-start(f32[2,64]{1,0:T(2,128)} %param.17) | copy-start | bytes 1540
  118.1 58.6 %collective-permute-start.7 = (bf16[4,48,4096]{2,1,0:T(8,128)(2,1)S(1)}, bf16[4,48,4096]{2,1,0:T(8,128)(2,1)}, u32[]{:S(2)}, u32[]{:S(2)}) collective-permute-start(bf16[4,48,4096]{2,1,0:T(8,128)(2,1)S(1)} %pad_maximum_fusion), channel_id=1, source_target_pairs={{0,4},{4,0},{8,12},{12,8},{16,20},{20,16},{24,28},{28,24},{1,5},{5... | collective-permute-start | bytes 4718600 | tf_op jit(solution)/shard_map/ppermute | solution.py:27
  131.9 26.7 %copy-start.6 = (bf16[2,512,32]{2,1,0:T(8,128)(2,1)S(1)}, bf16[2,512,32]{2,1,0:T(8,128)(2,1)}, u32[]{:S(2)}) copy-start(bf16[2,512,32]{2,1,0:T(8,128)(2,1)} %constant_dynamic-slice_fusion.2) | copy-start | bytes 196612
  149.0 15.2 %copy-start.8 = (f32[384]{0:T(512)}, f32[384]{0:T(512)S(1)}, u32[]{:S(2)}) copy-start(f32[384]{0:T(512)S(1)} %log_add_fusion) | copy-start | bytes 4612
  159.9 8.9 %collective-permute-start.13 = (bf16[2,192,64]{2,1,0:T(8,128)(2,1)S(1)}, bf16[2,192,64]{2,1,0:T(8,128)(2,1)S(1)}, u32[]{:S(2)}, u32[]{:S(2)}) collective-permute-start(bf16[2,192,64]{2,1,0:T(8,128)(2,1)S(1)} %bitcast_select_fusion), channel_id=1, source_target_pairs={{0,3},{1,0},{2,1},{3,2},{4,7},{5,4},{6,5},{7,6},{8,11},{9,8},{10,9... | collective-permute-start | bytes 147464 | tf_op jit(solution)/shard_map/ppermute | solution.py:18
  162.2 10.3 %collective-permute-start.8 = (bf16[2,192,64]{2,1,0:T(8,128)(2,1)S(1)}, bf16[2,192,64]{2,1,0:T(8,128)(2,1)S(1)}, u32[]{:S(2)}, u32[]{:S(2)}) collective-permute-start(bf16[2,192,64]{2,1,0:T(8,128)(2,1)S(1)} %bitcast_select_fusion), channel_id=1, source_target_pairs={{0,2},{1,3},{2,0},{3,1},{4,6},{5,7},{6,4},{7,5},{8,10},{9,11},{10,... | collective-permute-start | bytes 147464 | tf_op jit(solution)/shard_map/ppermute | solution.py:18
  166.8 9.4 %collective-permute-start.3 = (bf16[2,192,64]{2,1,0:T(8,128)(2,1)S(1)}, bf16[2,192,64]{2,1,0:T(8,128)(2,1)S(1)}, u32[]{:S(2)}, u32[]{:S(2)}) collective-permute-start(bf16[2,192,64]{2,1,0:T(8,128)(2,1)S(1)} %bitcast_select_fusion), channel_id=1, source_target_pairs={{0,1},{1,2},{2,3},{3,0},{4,5},{5,6},{6,7},{7,4},{8,9},{9,10},{10,1... | collective-permute-start | bytes 147464 | tf_op jit(solution)/shard_map/ppermute | solution.py:18

commit v2 on v0

v2 whole, which is shorter than its diff:
```python
import jax
import jax.numpy as jnp
from jax import lax
from jax.experimental import pallas as pl
from jax.experimental.pallas import tpu as pltpu
from jax.sharding import PartitionSpec as P

f32, bf16 = jnp.float32, jnp.bfloat16
params = pltpu.CompilerParams(vmem_limit_bytes=60 << 20)


def after(value, *others):
    return lax.optimization_barrier((value,) + others)[0]


def turned_taps(table, classes, own_o):
    depth, group = table.shape
    taps = depth - 5
    period = taps * classes
    tap = lax.broadcasted_iota(jnp.int32, (period, taps), 1)
    row = lax.broadcasted_iota(jnp.int32, (period, taps), 0)
    spread = jnp.where(row // classes == tap, 1.0, 0.0).astype(bf16)
    base = jnp.dot(spread, table[:taps].astype(bf16), preferred_element_type=f32)
    start = 128.0 * table[taps : taps + 1] + table[taps + 1 : taps + 2]
    start = start.astype(jnp.int32)
    for bit in range((taps - 1).bit_length()):
        moved = pltpu.roll(base, classes << bit, 0)
        base = jnp.where(start & (1 << bit) != 0, moved, base)
    row = lax.broadcasted_iota(jnp.int32, (period, group), 0)
    column = lax.broadcasted_iota(jnp.int32, (period, group), 1)
    return jnp.where(row % classes == column // own_o, base, 0.0), start


def window(turned, slab, planes, taps, classes):
    base, start = turned
    if planes % taps == 0:
        rows = jnp.concatenate([base] * (planes // taps))
    else:
        width = planes * classes
        rows = base[:width]
        for i in range(1, taps // planes):
            rows = jnp.where(
                slab % (taps // planes) == i, base[i * width : (i + 1) * width], rows
            )
    row = lax.broadcasted_iota(jnp.int32, rows.shape, 0)
    place = slab * planes + row // classes - start
    return jnp.where(jnp.logical_and(place >= 0, place < taps), rows, 0.0)


def even_first(one, two, core):
    return [jnp.where(core == 0, one, two), jnp.where(core == 0, two, one)]


def window_kernel(planes, classes, own_o, order_ref, tables_ref, out_ref):
    group = tables_ref.shape[2]
    taps = tables_ref.shape[1] - 5
    width = planes * classes
    core = order_ref[0] & 1
    for i in range(out_ref.shape[0]):
        tables = even_first(tables_ref[2 * i], tables_ref[2 * i + 1], core)
        for side, table in enumerate(tables):
            turned = turned_taps(table, classes, own_o)
            for part, slab in enumerate((order_ref[0], order_ref[0] ^ 1)):
                rows = window(turned, slab, planes, taps, classes)
                out_ref[
                    i, part * width : (part + 1) * width, side * group : (side + 1) * group
                ] = rows.astype(bf16)


def window_slices(order, tables, planes, classes, own_o):
    slabs, _, group = tables.shape
    vmem = pl.BlockSpec(memory_space=pltpu.VMEM)
    return pl.pallas_call(
        lambda *refs: window_kernel(planes, classes, own_o, *refs),
        in_specs=[pl.BlockSpec(memory_space=pltpu.SMEM), vmem],
        out_specs=vmem,
        out_shape=jax.ShapeDtypeStruct((slabs // 2, 2 * planes * classes, 2 * group), bf16),
        compiler_params=params,
        name="window_slices",
    )(order, tables)


def shifted(value, axis, step):
    size = lax.axis_size(axis)
    return lax.ppermute(value, axis, [(i, (i + step) % size) for i in range(size)])


def paired(value, masks):
    size = lax.axis_size("slab")
    return lax.ppermute(value, "slab", [(i, i ^ masks[i % 2]) for i in range(size)])


def mask_steps(size):
    bits = [1 << i for i in range(1, size.bit_length() - 1)]
    return list(zip(bits, reversed(bits)))


def held_masks(size, core):
    masks = [0]
    for step in mask_steps(size):
        masks = masks + [mask ^ step[core] for mask in masks]
    return masks


def block_orders():
    size = lax.axis_size("slab")
    slab = lax.axis_index("slab")
    core = slab & 1
    masks = list(zip(held_masks(size, 0), held_masks(size, 1)))
    own = [slab ^ (even + core * (odd - even)) for even, odd in masks]
    other = [slab ^ 1 ^ (odd + core * (even - odd)) for even, odd in masks]
    return own, other


def chip_places(parity):
    chips = lax.axis_size("slab") // 2
    chip = lax.axis_index("slab") // 2
    depth = chips.bit_length() - 1
    places = []
    for other in range(chips):
        apart = chip ^ other
        turned = sum(((apart >> i) & 1) << (depth - 1 - i) for i in range(depth))
        places.append(apart + parity * (turned - apart))
    return places


def spread_start(block):
    return [block] + [paired(block, step) for step in mask_steps(lax.axis_size("slab"))]


def spread_end(blocks):
    held = blocks[:2]
    for step, block in zip(mask_steps(lax.axis_size("slab"))[1:], blocks[2:]):
        held = held + [block] + [paired(each, step) for each in held[1:]]
    return held


def sum_images_kernel(*refs):
    count = refs[-1].shape[0]
    values = [ref for ref in refs[:-2] if ref.shape[1] == 2 * count]
    pixels = refs[len(values) : -2]
    rows = values[0].shape[0]
    contract = (((0,), (0,)), ((), ()))
    total = 0.0
    place = 0
    for pixel in pixels:
        for top in range(0, pixel.shape[0], rows):
            total += lax.dot_general(
                values[place][...],
                pixel[top : top + rows],
                contract,
                preferred_element_type=f32,
            )
            place += 1
    refs[-2][...] = total[:count]
    refs[-1][...] = total[count:]


def sum_images(values, pixels):
    rows, width = values[0].shape
    block = pixels[0].shape[1]
    tile = min(block, 2048)
    half = jax.ShapeDtypeStruct((width // 2, block), f32)
    return pl.pallas_call(
        sum_images_kernel,
        grid=(block // tile,),
        in_specs=[pl.BlockSpec((rows, width), lambda i: (0, 0))] * len(values)
        + [pl.BlockSpec((pixel.shape[0], tile), lambda i: (0, i)) for pixel in pixels],
        out_specs=[pl.BlockSpec((width // 2, tile), lambda i: (0, i))] * 2,
        out_shape=[half, half],
        compiler_params=params,
        name="sum_images",
    )(*values, *pixels)


def add_parts_kernel(one_ref, two_ref, out_ref):
    total = one_ref[...] + two_ref[...]
    out_ref[...] = total.reshape(out_ref.shape)


def add_parts(one, two, classes):
    width, block = one.shape
    tile = min(block, 4096)
    part = pl.BlockSpec((width, tile), lambda i: (0, i))
    return pl.pallas_call(
        add_parts_kernel,
        grid=(block // tile,),
        in_specs=[part] * 2,
        out_specs=pl.BlockSpec((width // classes, classes, tile), lambda i: (0, 0, i)),
        out_shape=jax.ShapeDtypeStruct((width // classes, classes, block), f32),
        compiler_params=params,
        name="add_parts",
    )(one, two)


def project_kernel(planes, classes, own_o, depth, order_ref, *refs):
    pieces, (out_ref, prior_ref, tables_ref) = refs[:-3], refs[-3:]
    width = planes * classes
    group = classes * own_o
    taps = depth - 5
    block = pieces[0].shape[1]
    core = order_ref[0] & 1
    lines = -(-depth * group // block)
    for i, piece in enumerate(pieces):
        flat = piece[2 * width :].astype(f32)
        for side in range(2):
            table = []
            for line in range(depth):
                row, column = divmod(line * group, block)
                row += side * lines
                table.append(flat[row : row + 1, column : column + group])
            tables_ref[2 * i + side] = jnp.concatenate(table)
    chip = even_first(tables_ref[0], tables_ref[1], core)
    prior = [jnp.sum(table[taps + 2 :], axis=0, keepdims=True) for table in chip]
    prior_ref[...] = jnp.concatenate(prior, axis=1)
    turned = [turned_taps(table, classes, own_o) for table in chip]
    slices = []
    for i in range(len(pieces)):
        for slab in (order_ref[i], order_ref[i] ^ 1):
            parts = [window(one, slab, planes, taps, classes) for one in turned]
            slices.append(jnp.concatenate(parts, axis=1))
    slices = jnp.concatenate(slices).T.astype(bf16)
    tile = min(block, 512)

    def some(i, energy):
        columns = pl.ds(pl.multiple_of(i * tile, tile), tile)
        stack = jnp.concatenate([piece[: 2 * width, columns] for piece in pieces])
        projection = jnp.dot(slices, stack, preferred_element_type=f32)
        projection = projection.astype(bf16).astype(f32).T
        out_ref[columns] = projection.astype(bf16)
        return energy + jnp.sum(projection * projection, axis=0, keepdims=True)

    energy = lax.fori_loop(0, block // tile, some, jnp.zeros((1, 2 * group), f32))
    high = energy.astype(bf16).astype(f32)
    middle = (energy - high).astype(bf16).astype(f32)
    parts = [high, middle, energy - high - middle, jnp.zeros((13, 2 * group), f32)]
    parts = jnp.concatenate(parts)
    out_ref[block:] = parts.astype(bf16)


def project(order, pieces, planes, classes, own_o, depth):
    block = pieces[0].shape[1]
    group = classes * own_o
    vmem = pl.BlockSpec(memory_space=pltpu.VMEM)
    return pl.pallas_call(
        lambda *refs: project_kernel(planes, classes, own_o, depth, *refs),
        in_specs=[pl.BlockSpec(memory_space=pltpu.SMEM)] + [vmem] * len(pieces),
        out_specs=[vmem] * 3,
        out_shape=[
            jax.ShapeDtypeStruct((block + 16, 2 * group), bf16),
            jax.ShapeDtypeStruct((1, 2 * group), f32),
            jax.ShapeDtypeStruct((2 * len(pieces), depth, group), f32),
        ],
        compiler_params=params,
        name="project",
    )(order, *pieces)


def match_kernel(count, order_ref, mine_ref, theirs_ref, *refs):
    pieces, out_ref, pixels_ref = refs[:-2], refs[-2], refs[-1]
    rows = pieces[0].shape[0] // count
    half = mine_ref.shape[0] - 16
    core = order_ref[0] & 1
    wide = [piece[...] if rows % 16 == 0 else piece[...].astype(f32) for piece in pieces]
    stack = [piece[i * rows : (i + 1) * rows] for i in range(count) for piece in wide]
    pixels_ref[...] = jnp.concatenate(stack).astype(bf16)
    squares = mine_ref[half:].astype(f32) + theirs_ref[half:].astype(f32)
    energy = jnp.sum(squares, axis=0, keepdims=True)
    total = -0.5 * energy
    for side, projection in ((core, mine_ref), (1 - core, theirs_ref)):
        columns = pl.ds(pl.multiple_of(side * half, half), half)
        total += jnp.dot(pixels_ref[:, columns], projection[:half], preferred_element_type=f32)
    out_ref[...] = total.reshape(out_ref.shape)


def match(order, mine, theirs, pieces, count):
    rows, block = pieces[0].shape
    rows_all = rows * len(pieces)
    columns = mine.shape[1]
    vmem = pl.BlockSpec(memory_space=pltpu.VMEM)
    return pl.pallas_call(
        lambda *refs: match_kernel(count, *refs),
        in_specs=[pl.BlockSpec(memory_space=pltpu.SMEM)] + [vmem] * (2 + len(pieces)),
        out_specs=[vmem] * 2,
        out_shape=[
            jax.ShapeDtypeStruct((count, rows_all // count, columns), f32),
            jax.ShapeDtypeStruct((rows_all, block), bf16),
        ],
        compiler_params=params,
        name="match",
    )(order, mine, theirs, *pieces)


def pick(blocks, order):
    return jnp.concatenate([lax.dynamic_slice_in_dim(blocks, i, 1) for i in order])


def in_three(value):
    high = lax.reduce_precision(value, 8, 7)
    rest = value - high
    middle = lax.reduce_precision(rest, 8, 7)
    return [part.astype(bf16) for part in (high, middle, rest - middle)]


def local(volumes, band_weights, band_start, images, noise_precision, log_prior):
    planes, classes, block = volumes.shape
    slabs, batches = lax.axis_size("slab"), lax.axis_size("batch")
    slab, batch = lax.axis_index("slab"), lax.axis_index("batch")
    core = slab & 1
    chips = slabs // 2
    own_o, taps = band_weights.shape[1:]
    particles = images.shape[0]
    rows = particles // slabs
    width = planes * classes
    group = classes * own_o
    own_order, other_order = block_orders()

    def fetch(step, *earlier):
        column = lax.rem(batch + step, batches) * block
        part = lax.dynamic_slice(images, (slab * rows, column), (rows, block))
        return shifted(after(part, *earlier) if earlier else part, "batch", step)

    half = batches // 2
    steps = [step for step in range(1, batches) if step != half]
    fetched = [fetch(step) for step in steps]
    last = fetch(half)

    coarse = band_start // 128
    table = jnp.concatenate(
        [
            band_weights.reshape(group, taps).T,
            jnp.stack([coarse, band_start - 128 * coarse]).reshape(2, group).astype(bf16),
            jnp.stack(in_three(log_prior)).reshape(3, group),
        ]
    )
    depth = table.shape[0]
    side = block // 2
    extra = -(-table.size // side)
    table = jnp.pad(table.reshape(-1), (0, extra * side - table.size)).reshape(extra, side)
    flat = volumes.reshape(width, block)
    mine = lax.dynamic_slice_in_dim(flat, core * side, side, axis=1)
    give = lax.dynamic_slice_in_dim(flat, (1 - core) * side, side, axis=1)
    theirs = paired(jnp.concatenate([give, table]), (1, 1))
    shard = jnp.concatenate([mine, theirs[:width], table, theirs[width:]])
    shards = spread_end(spread_start(shard))
    near = spread_start(after(jnp.concatenate(fetched), *shards[1:])) if steps else []
    order = jnp.stack(own_order)
    mine, prior, tables = project(order, shards, planes, classes, own_o, depth)
    mine = after(mine, last, *near)
    theirs = paired(mine, (1, 1))

    own = [lax.dynamic_slice(images, (i * rows, batch * block), (rows, block)) for i in own_order]
    total, pixels = match(order, mine, theirs, own, 1)
    total = total[0]
    pixels = [pixels]
    if steps:
        parts, pixel = match(order, mine, theirs, spread_end(near), len(steps))
        pixels.append(pixel)
        for step, part in zip(steps, parts):
            total = total + shifted(part, "batch", -step)
    part, pixel = match(order, mine, theirs, spread_end(spread_start(last)), 1)
    pixels.append(pixel)
    total = total + shifted(part[0], "batch", -half)
    total = total.reshape(chips, rows, 2 * group)

    def by_rows(blocks):
        return pick(blocks, chip_places(core))

    noise = lax.dynamic_index_in_dim(noise_precision.reshape(chips, 2, rows), core, 1, False)
    score = noise[:, :, None] * by_rows(total) + prior
    own_top = jnp.max(score, axis=2)
    shifted_exp = jnp.exp(score - own_top[:, :, None])
    own_total = jnp.sum(shifted_exp, axis=2)
    count = chips * rows
    lines = -(-count // (2 * group))
    sides = jnp.stack(in_three(own_top.reshape(count)) + in_three(own_total.reshape(count)))
    sides = jnp.pad(sides, ((0, 0), (0, lines * 2 * group - count))).reshape(-1, 2 * group)
    packed = jnp.concatenate([shifted_exp.astype(bf16).reshape(count, 2 * group), sides])
    mates = [list(range(parity, slabs, 2)) for parity in (0, 1)]
    packed = lax.all_gather(packed, "slab", axis_index_groups=mates)
    exps = packed[:, :count]
    sides = packed[:, count:].reshape(chips, 6, lines * 2 * group)[:, :, :count].astype(f32)
    tops = sides[:, 0] + sides[:, 1] + sides[:, 2]
    totals = sides[:, 3] + sides[:, 4] + sides[:, 5]
    top = jnp.max(tops, axis=0)
    log_evidence = top + jnp.log(jnp.sum(totals * jnp.exp(tops - top), axis=0))
    scale = jnp.exp(tops - log_evidence)
    weights = (exps.astype(f32) * scale[:, :, None]).astype(bf16)

    chip_order = [i // 2 for i in own_order]
    both = pick(window_slices(order, tables, planes, classes, own_o), chip_places(core))
    inserted = jnp.einsum("qzo,qno->nz", both, weights, preferred_element_type=f32).astype(bf16)
    inserted = pick(inserted.reshape(chips, rows, 2 * width), chip_order)
    inserted = inserted.reshape(count, 2 * width)
    there = [inserted] + [shifted(inserted, "batch", step) for step in steps + [half]]

    responsibilities = jnp.exp(score.reshape(count, 2 * group) - log_evidence[:, None])
    lines = -(-count // group)
    evidence = jnp.pad(log_evidence, (0, lines * group - count)).reshape(lines, group)
    halves = even_first(responsibilities[:, :group], responsibilities[:, group:], core)
    mine = jnp.concatenate([halves[0], evidence])
    theirs = paired(jnp.concatenate([halves[1], evidence]), (1, 1))

    def in_order(one, two):
        return jnp.stack(even_first(one, two, core), axis=1)

    responsibilities = in_order(
        mine[:count].reshape(chips, rows, group), theirs[:count].reshape(chips, rows, group)
    ).reshape(particles, group)
    evidence = [each[count:].reshape(-1)[:count].reshape(chips, rows) for each in (mine, theirs)]
    log_evidence = in_order(*evidence).reshape(particles)

    there[0] = after(there[0], theirs)
    keep, give = sum_images(there, pixels)
    backprojection = add_parts(keep, paired(give, (1, 1)), classes)
    return (
        responsibilities.T.reshape(classes, own_o, particles),
        log_evidence,
        backprojection,
    )


def solution(mesh):
    in_specs = (
        P("slab", None, "batch"),
        P(None, "slab", None),
        P(None, "slab"),
        P("batch", None),
        P("batch"),
        P(None, "slab"),
    )
    out_specs = (P(None, "slab", "batch"), P("batch"), P("slab", None, "batch"))
    return jax.shard_map(local, mesh=mesh, in_specs=in_specs, out_specs=out_specs, check_vma=False)
```

time: 478 us -> 133 us (0.28)
  waiting for transfers between devices: 386 us -> 52.9 us
  matrix products: 32.8 us -> 0.32 us
  Pallas kernels: 0 us -> 26.8 us
  starting transfers between devices: 0.34 us -> 23.2 us
  between operations: 14.5 us -> 0.99 us
  blocking collectives: 17.7 us -> 9.81 us
  local copies, waits for them, and re-layouts: 20.3 us -> 14.5 us
    reduce_scatter x1 -> x0, waiting for transfers between devices: 142 us -> none  [local(): lax.psum_scatter(jnp.einsum('np,kon->pko', columns, weights, preferred_el...]
    unnamed x5 -> x0, waiting for transfers between devices: 126 us -> none
    all_gather x2 -> x0, waiting for transfers between devices: 119 us -> none  [the longest x1 80.9 us: local(): piece = lax.all_gather(projection, 'batch', axis=2, tiled=True)]
    ppermute x0 -> x22, waiting for transfers between devices: none -> 52.9 us  [the longest x9 37.4 us: shifted(): lax.ppermute(value, axis, [(i, (i + step) % size) for i in range(size)])]
    dot_general x4 -> x1, matrix products: 32.8 us -> 0.32 us  [local(): jnp.einsum('qzo,qno->nz', both, weights, preferred_element_type=f32)]
    pallas_call x0 -> x7, Pallas kernels: none -> 26.8 us  [the longest x3 12.7 us: match(): pl.pallas_call(lambda *refs: match_kernel(count, *refs), in_specs=[pl.Blo...]
    ppermute x0 -> x22, starting transfers between devices: none -> 23.2 us  [the longest x9 11.9 us: shifted(): lax.ppermute(value, axis, [(i, (i + step) % size) for i in range(size)])]
    transpose x1, local copies, waits for them, and re-layouts: 13.4 us -> 0.81 us  [local(): responsibilities.T.reshape(classes, own_o, particles)]
  transfers between devices with their start and end apart: 4 -> 22, of which waited for: 4 -> 10; matrix products, arithmetic and copies ran while one was open for 1% -> 7% of each run, Pallas kernels for 0% -> 15%
where the time goes in v2:
time: 133 us
  waiting for transfers between devices  52.9 us (40%)
  Pallas kernels  26.8 us (20%)
  starting transfers between devices  23.2 us (17%)
  local copies, waits for them, and re-layouts  14.5 us (11%)
  blocking collectives  9.81 us (7%)
  other arithmetic  3.97 us (3%)
    ppermute x9, waiting for transfers between devices, shifted(): lax.ppermute(value, axis, [(i, (i + step) % size) for i in range(size)])  37.4 us
    ppermute x13, waiting for transfers between devices, paired(): lax.ppermute(value, 'slab', [(i, i ^ masks[i % 2]) for i in range(size)])  15.5 us
    pallas_call x3, Pallas kernels, match(): pl.pallas_call(lambda *refs: match_kernel(count, *refs), in_specs=[pl.Blo...  12.7 us
    ppermute x9, starting transfers between devices, shifted(): lax.ppermute(value, axis, [(i, (i + step) % size) for i in range(size)])  11.9 us
    ppermute x13, starting transfers between devices, paired(): lax.ppermute(value, 'slab', [(i, i ^ masks[i % 2]) for i in range(size)])  11.3 us
    all_gather x1, blocking collectives, local(): packed = lax.all_gather(packed, 'slab', axis_index_groups=mates)  9.81 us
    pallas_call x1, Pallas kernels, project(): pl.pallas_call(lambda *refs: project_kernel(planes, classes, own_o, depth...  4.72 us
    pallas_call x1, Pallas kernels, sum_images(): pl.pallas_call(sum_images_kernel, grid=(block // tile,), in_specs=[pl.Blo...  4.71 us
  transfers between devices with their start and end apart: 22, of which 10 were waited for; matrix products, arithmetic and copies ran while one was open for 7% of the time, Pallas kernels for 15%

profile of v2, /device:TPU:0, one launch (start us, length us, event | category | flops | bytes accessed | tf_op | source)
XLA Modules:
  0.0 132.5 jit_solution(8998625554076266048)
XLA Ops:
  0.6 1.2 reshape.313
  1.9 0.7 fusion.22
  2.8 0.7 subtract_convert_fusion
  3.7 0.7 copy.28
  4.7 0.5 collective-permute-start
  5.2 1.2 collective-permute-done
  6.5 2.9 %collective-permute-start.1 = (bf16[134,2048]{1,0:T(8,128)(2,1)S(1)}, bf16[134,2048]{1,0:T(8,128)(2,1)S(1)}, u32[]{:S(2)}, u32[]{:S(2)}) collective-permute-start(bf16[134,2048]{1,0:T(8,128)(2,1)S(1)} %pad_maximum_fusion.1.refs_1_), channel_id=1, source_target_pairs={{0,8},{4,20},{8,0},{12,28},{16,24},{20,4},{24,16},{28,12},{1,9},{5... | collective-permute-start | bytes 1646600 | tf_op jit(solution)/shard_map/ppermute | solution.py:90
  9.4 3.0 %fusion.26 = (bf16[48,4096]{1,0:T(8,128)(2,1)}, bf16[48,4096]{1,0:T(8,128)(2,1)}, bf16[48,4096]{1,0:T(8,128)(2,1)}, bf16[48,4096]{1,0:T(8,128)(2,1)S(1)}, bf16[4...) fusion(bf16[384,16384]{1,0:T(8,128)(2,1)} %param.9, s32[]{:T(128)S(6)} %select_n.175, ...), kind=kLoop, calls=%fused_computation.95 | loop fusion | bytes 5505056 | tf_op jit(solution)/shard_map/dynamic_slice | solution.py:352
  12.4 1.6 %collective-permute-start.5 = (bf16[48,4096]{1,0:T(8,128)(2,1)S(1)}, bf16[48,4096]{1,0:T(8,128)(2,1)S(1)}, u32[]{:S(2)}, u32[]{:S(2)}) collective-permute-start(bf16[48,4096]{1,0:T(8,128)(2,1)S(1)} %get-tuple-element.44), channel_id=1, source_target_pairs={{0,1},{1,2},{2,3},{3,0},{4,5},{5,6},{6,7},{7,4},{8,9},{9,10},{10,1... | collective-permute-start | bytes 1179656 | tf_op jit(solution)/shard_map/ppermute | solution.py:85
  14.0 2.2 %collective-permute-start.6 = (bf16[48,4096]{1,0:T(8,128)(2,1)S(1)}, bf16[48,4096]{1,0:T(8,128)(2,1)S(1)}, u32[]{:S(2)}, u32[]{:S(2)}) collective-permute-start(bf16[48,4096]{1,0:T(8,128)(2,1)S(1)} %get-tuple-element.43), channel_id=1, source_target_pairs={{0,3},{1,0},{2,1},{3,2},{4,7},{5,4},{6,5},{7,6},{8,11},{9,8},{10,9... | collective-permute-start | bytes 1179656 | tf_op jit(solution)/shard_map/ppermute | solution.py:85
  16.3 1.5 %collective-permute-start.2 = (bf16[134,2048]{1,0:T(8,128)(2,1)S(1)}, bf16[134,2048]{1,0:T(8,128)(2,1)S(1)}, u32[]{:S(2)}, u32[]{:S(2)}) collective-permute-start(bf16[134,2048]{1,0:T(8,128)(2,1)S(1)} %pad_maximum_fusion.1.refs_1_), channel_id=1, source_target_pairs={{0,16},{4,12},{8,24},{12,4},{16,0},{20,28},{24,8},{28,20},{1,17},{... | collective-permute-start | bytes 1646600 | tf_op jit(solution)/shard_map/ppermute | solution.py:90
  17.8 1.4 %collective-permute-start.3 = (bf16[134,2048]{1,0:T(8,128)(2,1)S(1)}, bf16[134,2048]{1,0:T(8,128)(2,1)}, u32[]{:S(2)}, u32[]{:S(2)}) collective-permute-start(bf16[134,2048]{1,0:T(8,128)(2,1)S(1)} %collective-permute-done.1.refs_2_), channel_id=1, source_target_pairs={{0,16},{4,12},{8,24},{12,4},{16,0},{20,28},{24,8},{28,20},{1,17},{... | collective-permute-start | bytes 1646600 | tf_op jit(solution)/shard_map/ppermute | solution.py:90
  19.2 7.1 %collective-permute-done.5 = bf16[48,4096]{1,0:T(8,128)(2,1)S(1)} collective-permute-done((bf16[48,4096]{1,0:T(8,128)(2,1)S(1)}, bf16[48,4096]{1,0:T(8,128)(2,1)S(1)}, u32[]{:S(2)}, u32[]{:S(2)}) %collective-permute-start.5) | collective-permute-done | bytes 393248 | tf_op jit(solution)/shard_map/ppermute | solution.py:85
  26.3 6.8 %collective-permute-done.6 = bf16[48,4096]{1,0:T(8,128)(2,1)S(1)} collective-permute-done((bf16[48,4096]{1,0:T(8,128)(2,1)S(1)}, bf16[48,4096]{1,0:T(8,128)(2,1)S(1)}, u32[]{:S(2)}, u32[]{:S(2)}) %collective-permute-start.6) | collective-permute-done | bytes 393248 | tf_op jit(solution)/shard_map/ppermute | solution.py:85
  33.2 1.6 %collective-permute-start.7 = (bf16[96,4096]{1,0:T(8,128)(2,1)S(1)}, bf16[96,4096]{1,0:T(8,128)(2,1)S(1)}, u32[]{:S(2)}, u32[]{:S(2)}) collective-permute-start(bf16[96,4096]{1,0:T(8,128)(2,1)S(1)} %pad_maximum_fusion.refs_3_), channel_id=1, source_target_pairs={{0,8},{4,20},{8,0},{12,28},{16,24},{20,4},{24,16},{28,12},{1,9},{5... | collective-permute-start | bytes 2359304 | tf_op jit(solution)/shard_map/ppermute | solution.py:90
  34.7 0.5 collective-permute-start.8
  35.2 1.3 collective-permute-start.4
  36.5 0.7 pad_add_fusion.refs_0_
  37.2 4.7 %project.1 = (bf16[2064,256]{1,0:T(8,128)(2,1)}, f32[1,256]{1,0:T(1,128)}, f32[8,37,128]{2,1,0:T(8,128)}) custom-call(s32[4]{0:T(128)} %pad_add_fusion.refs_0_, bf16[134,2048]{1,0:T(8,128)(2,1)} %copy-done.2, bf16[134,2048]{1,0:T(8,128)(2,1)} %copy-done.7, bf16[134,2048]{1,0:T(8,128)(2,1)} %copy-done.8, bf16[134,2048]{1,0:T(8,128)(2,1)} %collective-permute-done.3.refs_4_), custom_call_target="tpu_custom_call" | custom-call | tf_op jit(solution)/shard_map/project/pallas_call | solution.py:245
  41.9 13.1 %collective-permute-done.4.refs_3_ = bf16[48,4096]{1,0:T(8,128)(2,1)} collective-permute-done((bf16[48,4096]{1,0:T(8,128)(2,1)}, bf16[48,4096]{1,0:T(8,128)(2,1)}, u32[]{:S(2)}, u32[]{:S(2)}) %collective-permute-start.4) | collective-permute-done | bytes 393248 | tf_op jit(solution)/shard_map/ppermute | solution.py:85
  55.1 1.7 %collective-permute-start.10 = (bf16[96,4096]{1,0:T(8,128)(2,1)S(1)}, bf16[96,4096]{1,0:T(8,128)(2,1)S(1)}, u32[]{:S(2)}, u32[]{:S(2)}) collective-permute-start(bf16[96,4096]{1,0:T(8,128)(2,1)S(1)} %collective-permute-done.7.refs_4_), channel_id=1, source_target_pairs={{0,16},{4,12},{8,24},{12,4},{16,0},{20,28},{24,8},{28,20},{1,17},{... | collective-permute-start | bytes 2359304 | tf_op jit(solution)/shard_map/ppermute | solution.py:90
  57.5 11.7 %collective-permute-done.13.refs_4_ = bf16[48,4096]{1,0:T(8,128)(2,1)} collective-permute-done((bf16[48,4096]{1,0:T(8,128)(2,1)}, bf16[48,4096]{1,0:T(8,128)(2,1)}, u32[]{:S(2)}, u32[]{:S(2)}) %collective-permute-start.13) | collective-permute-done | bytes 393248 | tf_op jit(solution)/shard_map/ppermute | solution.py:90
  69.6 1.5 %collective-permute-done.10.refs_6_ = bf16[96,4096]{1,0:T(8,128)(2,1)S(1)} collective-permute-done((bf16[96,4096]{1,0:T(8,128)(2,1)S(1)}, bf16[96,4096]{1,0:T(8,128)(2,1)S(1)}, u32[]{:S(2)}, u32[]{:S(2)}) %collective-permute-start.10) | collective-permute-done | bytes 786464 | tf_op jit(solution)/shard_map/ppermute | solution.py:90
  71.1 0.9 copy-done.6
  72.0 1.1 copy-done
  73.1 5.2 %match.4 = (f32[2,192,256]{2,1,0:T(8,128)}, bf16[384,4096]{1,0:T(8,128)(2,1)}) custom-call(s32[4]{0:T(128)} %pad_add_fusion.refs_0_, bf16[2064,256]{1,0:T(8,128)(2,1)} %get-tuple-element.19.refs_1_, bf16[2064,256]{1,0:T(8,128)(2,1)} %copy-done, bf16[96,4096]{1,0:T(8,128)(2,1)} %copy-done.1, bf16[96,4096]{1,0:T(8,128)(2,1)} %copy-done.4, ...), custom_call_target="tpu_custom_call" | custom-call | tf_op jit(solution)/shard_map/match/pallas_call | solution.py:281
  78.3 1.0 slice_bitcast_fusion.1
  79.3 2.3 %collective-permute-start.11 = (f32[192,256]{1,0:T(8,128)S(1)}, f32[192,256]{1,0:T(8,128)S(1)}, u32[]{:S(2)}, u32[]{:S(2)}) collective-permute-start(f32[192,256]{1,0:T(8,128)S(1)} %get-tuple-element.49), channel_id=1, source_target_pairs={{0,3},{1,0},{2,1},{3,2},{4,7},{5,4},{6,5},{7,6},{8,11},{9,8},{10,9... | collective-permute-start | bytes 589832 | tf_op jit(solution)/shard_map/ppermute | solution.py:85
  81.6 3.7 %match.5 = (f32[1,192,256]{2,1,0:T(8,128)}, bf16[192,4096]{1,0:T(8,128)(2,1)}) custom-call(s32[4]{0:T(128)} %pad_add_fusion.refs_0_, bf16[2064,256]{1,0:T(8,128)(2,1)} %get-tuple-element.19.refs_1_, bf16[2064,256]{1,0:T(8,128)(2,1)} %copy-done, bf16[48,4096]{1,0:T(8,128)(2,1)} %collective-permute-done.4.refs_3_, ...), custom_call_target="tpu_custom_call" | custom-call | tf_op jit(solution)/shard_map/match/pallas_call | solution.py:281
  85.4 0.6 collective-permute-start.16
  86.0 0.5 broadcast.80
  86.5 0.7 fusion.25
  87.3 2.0 %window_slices.1 = bf16[4,128,256]{2,1,0:T(8,128)(2,1)} custom-call(s32[4]{0:T(128)} %pad_add_fusion.refs_0_, f32[8,37,128]{2,1,0:T(8,128)} %get-tuple-element.24.refs_1_), custom_call_target="tpu_custom_call" | custom-call | tf_op jit(solution)/shard_map/window_slices/pallas_call | solution.py:73
  89.3 1.0 constant_dynamic-slice_fusion.7
  90.2 3.7 %match.3 = (f32[1,192,256]{2,1,0:T(8,128)}, bf16[192,4096]{1,0:T(8,128)(2,1)}) custom-call(s32[4]{0:T(128)} %pad_add_fusion.refs_0_, bf16[2064,256]{1,0:T(8,128)(2,1)} %get-tuple-element.19.refs_1_, bf16[2064,256]{1,0:T(8,128)(2,1)} %copy-done, bf16[48,4096]{1,0:T(8,128)(2,1)} %get-tuple-element.42.refs_3_, bf16[48,4096]{1,0:T(8,128)(2,1)} %get-tuple-element.41.refs_4_, ...), custom_call_target="tpu_custom_call" | custom-call | tf_op jit(solution)/shard_map/match/pallas_call | solution.py:281
  94.0 5.2 %collective-permute-done.16 = f32[192,256]{1,0:T(8,128)S(1)} collective-permute-done((f32[192,256]{1,0:T(8,128)}, f32[192,256]{1,0:T(8,128)S(1)}, u32[]{:S(2)}, u32[]{:S(2)}) %collective-permute-start.16) | collective-permute-done | bytes 196640 | tf_op jit(solution)/shard_map/ppermute | solution.py:85
  99.2 1.0 fusion.13
  101.0 9.8 %all-gather.1 = bf16[4,198,256]{2,1,0:T(8,128)(2,1)S(1)} all-gather(bf16[1,198,256]{2,1,0:T(8,128)(2,1)S(1)} %fusion.16), channel_id=2, replica_groups={{0,8,16,24},{4,12,20,28},{1,9,17,25},{5,13,21,29},{2,10,18,26},{6,14,22..., dimensions={0}, use_global_device_ids=true | all-gather | bytes 506880 | tf_op jit(solution)/shard_map/all_gather | solution.py:380
  111.7 3.8 %collective-permute-start.19 = (bf16[192,128]{1,0:T(8,128)(2,1)S(1)}, bf16[192,128]{1,0:T(8,128)(2,1)S(1)}, u32[]{:S(2)}, u32[]{:S(2)}) collective-permute-start(bf16[192,128]{1,0:T(8,128)(2,1)S(1)} %bitcast.66), channel_id=1, source_target_pairs={{0,3},{1,0},{2,1},{3,2},{4,7},{5,4},{6,5},{7,6},{8,11},{9,8},{10,9... | collective-permute-start | bytes 147464 | tf_op jit(solution)/shard_map/ppermute | solution.py:85
  115.5 2.5 %collective-permute-done.18.refs_1_ = bf16[192,128]{1,0:T(8,128)(2,1)S(1)} collective-permute-done((bf16[192,128]{1,0:T(8,128)(2,1)S(1)}, bf16[192,128]{1,0:T(8,128)(2,1)S(1)}, u32[]{:S(2)}, u32[]{:S(2)}) %collective-permute-start.18) | collective-permute-done | bytes 49184 | tf_op jit(solution)/shard_map/ppermute | solution.py:85
  118.0 2.7 %collective-permute-done.20.refs_3_ = bf16[192,128]{1,0:T(8,128)(2,1)S(1)} collective-permute-done((bf16[192,128]{1,0:T(8,128)(2,1)S(1)}, bf16[192,128]{1,0:T(8,128)(2,1)S(1)}, u32[]{:S(2)}, u32[]{:S(2)}) %collective-permute-start.20) | collective-permute-done | bytes 49184 | tf_op jit(solution)/shard_map/ppermute | solution.py:85
  120.7 0.6 copy-done.12
  121.3 4.7 %sum_images.1 = (f32[64,4096]{1,0:T(8,128)}, f32[64,4096]{1,0:T(8,128)}) custom-call(bf16[192,128]{1,0:T(8,128)(2,1)} %bitcast.68, bf16[192,128]{1,0:T(8,128)(2,1)} %copy-done.10, bf16[192,128]{1,0:T(8,128)(2,1)} %copy-done.11, bf16[192,128]{1,0:T(8,128)(2,1)} %copy-done.12, bf16[192,4096]{1,0:T(8,128)(2,1)} %get-tuple-element.26.refs_4_, ...), custom_call_target="tpu_custom_call" | custom-call | tf_op jit(solution)/shard_map/sum_images/pallas_call | solution.py:164
  126.2 0.7 reshape.324
  126.9 0.8 copy.32
  127.7 1.1 collective-permute-done.21.two_ref
  128.9 1.0 copy-done.3
  129.9 2.7 %add_parts.1 = f32[32,2,4096]{2,1,0:T(2,128)} custom-call(f32[64,4096]{1,0:T(8,128)} %get-tuple-element.29.one_ref, f32[64,4096]{1,0:T(8,128)} %copy-done.3), custom_call_target="tpu_custom_call" | custom-call | tf_op jit(solution)/shard_map/add_parts/pallas_call | solution.py:185
  (95 shorter events, 3.9 us)
Async XLA Ops:
  4.7 1.7 %collective-permute-start = (bf16[67,2048]{1,0:T(8,128)(2,1)S(1)}, bf16[67,2048]{1,0:T(8,128)(2,1)S(1)}, u32[]{:S(2)}, u32[]{:S(2)}) collective-permute-start(bf16[67,2048]{1,0:T(8,128)(2,1)S(1)} %pad_maximum_fusion.2), channel_id=1, source_target_pairs={{0,4},{4,0},{8,12},{12,8},{16,20},{20,16},{24,28},{28,24},{1,5},{5... | collective-permute-start | bytes 823304 | tf_op jit(solution)/shard_map/ppermute | solution.py:90
  6.5 9.8 %copy-start.2 = (bf16[134,2048]{1,0:T(8,128)(2,1)}, bf16[134,2048]{1,0:T(8,128)(2,1)S(1)}, u32[]{:S(2)}) copy-start(bf16[134,2048]{1,0:T(8,128)(2,1)S(1)} %pad_maximum_fusion.1.refs_1_) | copy-start | bytes 1646596
  6.5 11.3 %collective-permute-start.1 = (bf16[134,2048]{1,0:T(8,128)(2,1)S(1)}, bf16[134,2048]{1,0:T(8,128)(2,1)S(1)}, u32[]{:S(2)}, u32[]{:S(2)}) collective-permute-start(bf16[134,2048]{1,0:T(8,128)(2,1)S(1)} %pad_maximum_fusion.1.refs_1_), channel_id=1, source_target_pairs={{0,8},{4,20},{8,0},{12,28},{16,24},{20,4},{24,16},{28,12},{1,9},{5... | collective-permute-start | bytes 1646600 | tf_op jit(solution)/shard_map/ppermute | solution.py:90
  12.4 13.8 %collective-permute-start.5 = (bf16[48,4096]{1,0:T(8,128)(2,1)S(1)}, bf16[48,4096]{1,0:T(8,128)(2,1)S(1)}, u32[]{:S(2)}, u32[]{:S(2)}) collective-permute-start(bf16[48,4096]{1,0:T(8,128)(2,1)S(1)} %get-tuple-element.44), channel_id=1, source_target_pairs={{0,1},{1,2},{2,3},{3,0},{4,5},{5,6},{6,7},{7,4},{8,9},{9,10},{10,1... | collective-permute-start | bytes 1179656 | tf_op jit(solution)/shard_map/ppermute | solution.py:85
  14.0 19.1 %collective-permute-start.6 = (bf16[48,4096]{1,0:T(8,128)(2,1)S(1)}, bf16[48,4096]{1,0:T(8,128)(2,1)S(1)}, u32[]{:S(2)}, u32[]{:S(2)}) collective-permute-start(bf16[48,4096]{1,0:T(8,128)(2,1)S(1)} %get-tuple-element.43), channel_id=1, source_target_pairs={{0,3},{1,0},{2,1},{3,2},{4,7},{5,4},{6,5},{7,6},{8,11},{9,8},{10,9... | collective-permute-start | bytes 1179656 | tf_op jit(solution)/shard_map/ppermute | solution.py:85
  16.3 16.9 %collective-permute-start.2 = (bf16[134,2048]{1,0:T(8,128)(2,1)S(1)}, bf16[134,2048]{1,0:T(8,128)(2,1)S(1)}, u32[]{:S(2)}, u32[]{:S(2)}) collective-permute-start(bf16[134,2048]{1,0:T(8,128)(2,1)S(1)} %pad_maximum_fusion.1.refs_1_), channel_id=1, source_target_pairs={{0,16},{4,12},{8,24},{12,4},{16,0},{20,28},{24,8},{28,20},{1,17},{... | collective-permute-start | bytes 1646600 | tf_op jit(solution)/shard_map/ppermute | solution.py:90
  17.8 19.4 %copy-start.7 = (bf16[134,2048]{1,0:T(8,128)(2,1)}, bf16[134,2048]{1,0:T(8,128)(2,1)S(1)}, u32[]{:S(2)}) copy-start(bf16[134,2048]{1,0:T(8,128)(2,1)S(1)} %collective-permute-done.1.refs_2_) | copy-start | bytes 1646596
  17.8 15.4 %collective-permute-start.3 = (bf16[134,2048]{1,0:T(8,128)(2,1)S(1)}, bf16[134,2048]{1,0:T(8,128)(2,1)}, u32[]{:S(2)}, u32[]{:S(2)}) collective-permute-start(bf16[134,2048]{1,0:T(8,128)(2,1)S(1)} %collective-permute-done.1.refs_2_), channel_id=1, source_target_pairs={{0,16},{4,12},{8,24},{12,4},{16,0},{20,28},{24,8},{28,20},{1,17},{... | collective-permute-start | bytes 1646600 | tf_op jit(solution)/shard_map/ppermute | solution.py:90
  33.1 8.8 %copy-start.1 = (bf16[96,4096]{1,0:T(8,128)(2,1)}, bf16[96,4096]{1,0:T(8,128)(2,1)S(1)}, u32[]{:S(2)}) copy-start(bf16[96,4096]{1,0:T(8,128)(2,1)S(1)} %pad_maximum_fusion.refs_3_) | copy-start | bytes 2359300
  33.1 4.0 %copy-start.8 = (bf16[134,2048]{1,0:T(8,128)(2,1)}, bf16[134,2048]{1,0:T(8,128)(2,1)S(1)}, u32[]{:S(2)}) copy-start(bf16[134,2048]{1,0:T(8,128)(2,1)S(1)} %collective-permute-done.2.refs_3_) | copy-start | bytes 1646596
  33.2 21.8 %collective-permute-start.7 = (bf16[96,4096]{1,0:T(8,128)(2,1)S(1)}, bf16[96,4096]{1,0:T(8,128)(2,1)S(1)}, u32[]{:S(2)}, u32[]{:S(2)}) collective-permute-start(bf16[96,4096]{1,0:T(8,128)(2,1)S(1)} %pad_maximum_fusion.refs_3_), channel_id=1, source_target_pairs={{0,8},{4,20},{8,0},{12,28},{16,24},{20,4},{24,16},{28,12},{1,9},{5... | collective-permute-start | bytes 2359304 | tf_op jit(solution)/shard_map/ppermute | solution.py:90
  34.7 20.3 %collective-permute-start.8 = (bf16[96,4096]{1,0:T(8,128)(2,1)S(1)}, bf16[96,4096]{1,0:T(8,128)(2,1)S(1)}, u32[]{:S(2)}, u32[]{:S(2)}) collective-permute-start(bf16[96,4096]{1,0:T(8,128)(2,1)S(1)} %pad_maximum_fusion.refs_3_), channel_id=1, source_target_pairs={{0,16},{4,12},{8,24},{12,4},{16,0},{20,28},{24,8},{28,20},{1,17},{... | collective-permute-start | bytes 2359304 | tf_op jit(solution)/shard_map/ppermute | solution.py:90
  35.2 19.7 %collective-permute-start.4 = (bf16[48,4096]{1,0:T(8,128)(2,1)}, bf16[48,4096]{1,0:T(8,128)(2,1)}, u32[]{:S(2)}, u32[]{:S(2)}) collective-permute-start(bf16[48,4096]{1,0:T(8,128)(2,1)} %get-tuple-element.45), channel_id=1, source_target_pairs={{0,2},{1,3},{2,0},{3,1},{4,6},{5,7},{6,4},{7,5},{8,10},{9,11},{10,... | collective-permute-start | bytes 1179656 | tf_op jit(solution)/shard_map/ppermute | solution.py:85
  37.2 32.3 %copy-start.14 = (f32[384]{0:T(512)S(1)}, f32[384]{0:T(512)}, u32[]{:S(2)}) copy-start(f32[384]{0:T(512)} %param.10) | copy-start | bytes 4612
  55.0 16.1 %copy-start.4 = (bf16[96,4096]{1,0:T(8,128)(2,1)}, bf16[96,4096]{1,0:T(8,128)(2,1)S(1)}, u32[]{:S(2)}) copy-start(bf16[96,4096]{1,0:T(8,128)(2,1)S(1)} %collective-permute-done.7.refs_4_) | copy-start | bytes 2359300
  55.0 16.1 %copy-start.5 = (bf16[96,4096]{1,0:T(8,128)(2,1)}, bf16[96,4096]{1,0:T(8,128)(2,1)S(1)}, u32[]{:S(2)}) copy-start(bf16[96,4096]{1,0:T(8,128)(2,1)S(1)} %collective-permute-done.8.refs_5_) | copy-start | bytes 2359300
  55.0 16.1 %collective-permute-start.9 = (bf16[2064,256]{1,0:T(8,128)(2,1)}, bf16[2064,256]{1,0:T(8,128)(2,1)S(1)}, u32[]{:S(2)}, u32[]{:S(2)}) collective-permute-start(bf16[2064,256]{1,0:T(8,128)(2,1)} %get-tuple-element.19.refs_1_), channel_id=1, source_target_pairs={{0,4},{4,0},{8,12},{12,8},{16,20},{20,16},{24,28},{28,24},{1,5},{5... | collective-permute-start | bytes 3170312 | tf_op jit(solution)/shard_map/ppermute | solution.py:90
  55.1 16.0 %collective-permute-start.10 = (bf16[96,4096]{1,0:T(8,128)(2,1)S(1)}, bf16[96,4096]{1,0:T(8,128)(2,1)S(1)}, u32[]{:S(2)}, u32[]{:S(2)}) collective-permute-start(bf16[96,4096]{1,0:T(8,128)(2,1)S(1)} %collective-permute-done.7.refs_4_), channel_id=1, source_target_pairs={{0,16},{4,12},{8,24},{12,4},{16,0},{20,28},{24,8},{28,20},{1,17},{... | collective-permute-start | bytes 2359304 | tf_op jit(solution)/shard_map/ppermute | solution.py:90
  56.8 12.4 %collective-permute-start.13 = (bf16[48,4096]{1,0:T(8,128)(2,1)}, bf16[48,4096]{1,0:T(8,128)(2,1)}, u32[]{:S(2)}, u32[]{:S(2)}) collective-permute-start(bf16[48,4096]{1,0:T(8,128)(2,1)} %collective-permute-done.4.refs_3_), channel_id=1, source_target_pairs={{0,8},{4,20},{8,0},{12,28},{16,24},{20,4},{24,16},{28,12},{1,9},{5... | collective-permute-start | bytes 1179656 | tf_op jit(solution)/shard_map/ppermute | solution.py:90
  57.1 24.6 %collective-permute-start.14 = (bf16[48,4096]{1,0:T(8,128)(2,1)}, bf16[48,4096]{1,0:T(8,128)(2,1)}, u32[]{:S(2)}, u32[]{:S(2)}) collective-permute-start(bf16[48,4096]{1,0:T(8,128)(2,1)} %collective-permute-done.4.refs_3_), channel_id=1, source_target_pairs={{0,16},{4,12},{8,24},{12,4},{16,0},{20,28},{24,8},{28,20},{1,17},{... | collective-permute-start | bytes 1179656 | tf_op jit(solution)/shard_map/ppermute | solution.py:90
  69.2 12.5 %collective-permute-start.15 = (bf16[48,4096]{1,0:T(8,128)(2,1)}, bf16[48,4096]{1,0:T(8,128)(2,1)}, u32[]{:S(2)}, u32[]{:S(2)}) collective-permute-start(bf16[48,4096]{1,0:T(8,128)(2,1)} %collective-permute-done.13.refs_4_), channel_id=1, source_target_pairs={{0,16},{4,12},{8,24},{12,4},{16,0},{20,28},{24,8},{28,20},{1,17},{... | collective-permute-start | bytes 1179656 | tf_op jit(solution)/shard_map/ppermute | solution.py:90
  71.1 0.9 copy-start.6
  72.0 1.1 copy-start
  79.3 14.6 %collective-permute-start.11 = (f32[192,256]{1,0:T(8,128)S(1)}, f32[192,256]{1,0:T(8,128)S(1)}, u32[]{:S(2)}, u32[]{:S(2)}) collective-permute-start(f32[192,256]{1,0:T(8,128)S(1)} %get-tuple-element.49), channel_id=1, source_target_pairs={{0,3},{1,0},{2,1},{3,2},{4,7},{5,4},{6,5},{7,6},{8,11},{9,8},{10,9... | collective-permute-start | bytes 589832 | tf_op jit(solution)/shard_map/ppermute | solution.py:85
  81.6 12.3 %collective-permute-start.12 = (f32[192,256]{1,0:T(8,128)S(1)}, f32[192,256]{1,0:T(8,128)S(1)}, u32[]{:S(2)}, u32[]{:S(2)}) collective-permute-start(f32[192,256]{1,0:T(8,128)S(1)} %get-tuple-element.50), channel_id=1, source_target_pairs={{0,1},{1,2},{2,3},{3,0},{4,5},{5,6},{6,7},{7,4},{8,9},{9,10},{10,1... | collective-permute-start | bytes 589832 | tf_op jit(solution)/shard_map/ppermute | solution.py:85
  85.4 13.8 %collective-permute-start.16 = (f32[192,256]{1,0:T(8,128)}, f32[192,256]{1,0:T(8,128)S(1)}, u32[]{:S(2)}, u32[]{:S(2)}) collective-permute-start(f32[192,256]{1,0:T(8,128)} %bitcast.79), channel_id=1, source_target_pairs={{0,2},{1,3},{2,0},{3,1},{4,6},{5,7},{6,4},{7,5},{8,10},{9,11},{10,... | collective-permute-start | bytes 589832 | tf_op jit(solution)/shard_map/ppermute | solution.py:85
  93.9 6.2 %copy-start.13 = (f32[1,256]{1,0:T(1,128)S(1)}, f32[1,256]{1,0:T(1,128)}, u32[]{:S(2)}) copy-start(f32[1,256]{1,0:T(1,128)} %get-tuple-element.23) | copy-start | bytes 3076
  111.1 4.3 %collective-permute-start.17 = (f32[194,128]{1,0:T(8,128)S(1)}, f32[194,128]{1,0:T(8,128)S(1)}, u32[]{:S(2)}, u32[]{:S(2)}) collective-permute-start(f32[194,128]{1,0:T(8,128)S(1)} %pad_maximum_fusion.5), channel_id=1, source_target_pairs={{0,4},{4,0},{8,12},{12,8},{16,20},{20,16},{24,28},{28,24},{1,5},{5... | collective-permute-start | bytes 297992 | tf_op jit(solution)/shard_map/ppermute | solution.py:90
  111.6 9.1 %copy-start.9 = (bf16[4,48,128]{2,1,0:T(8,128)(2,1)}, bf16[4,48,128]{2,1,0:T(8,128)(2,1)S(1)}, u32[]{:S(2)}) copy-start(bf16[4,48,128]{2,1,0:T(8,128)(2,1)S(1)} %pad_maximum_fusion.6) | copy-start | bytes 147460
  111.6 6.4 %collective-permute-start.18 = (bf16[192,128]{1,0:T(8,128)(2,1)S(1)}, bf16[192,128]{1,0:T(8,128)(2,1)S(1)}, u32[]{:S(2)}, u32[]{:S(2)}) collective-permute-start(bf16[192,128]{1,0:T(8,128)(2,1)S(1)} %bitcast.65), channel_id=1, source_target_pairs={{0,1},{1,2},{2,3},{3,0},{4,5},{5,6},{6,7},{7,4},{8,9},{9,10},{10,1... | collective-permute-start | bytes 147464 | tf_op jit(solution)/shard_map/ppermute | solution.py:85
  111.7 6.3 %collective-permute-start.19 = (bf16[192,128]{1,0:T(8,128)(2,1)S(1)}, bf16[192,128]{1,0:T(8,128)(2,1)S(1)}, u32[]{:S(2)}, u32[]{:S(2)}) collective-permute-start(bf16[192,128]{1,0:T(8,128)(2,1)S(1)} %bitcast.66), channel_id=1, source_target_pairs={{0,3},{1,0},{2,1},{3,2},{4,7},{5,4},{6,5},{7,6},{8,11},{9,8},{10,9... | collective-permute-start | bytes 147464 | tf_op jit(solution)/shard_map/ppermute | solution.py:85
  115.5 5.2 %collective-permute-start.20 = (bf16[192,128]{1,0:T(8,128)(2,1)S(1)}, bf16[192,128]{1,0:T(8,128)(2,1)S(1)}, u32[]{:S(2)}, u32[]{:S(2)}) collective-permute-start(bf16[192,128]{1,0:T(8,128)(2,1)S(1)} %bitcast.67), channel_id=1, source_target_pairs={{0,2},{1,3},{2,0},{3,1},{4,6},{5,7},{6,4},{7,5},{8,10},{9,11},{10,... | collective-permute-start | bytes 147464 | tf_op jit(solution)/shard_map/ppermute | solution.py:85
  118.0 2.7 %copy-start.10 = (bf16[192,128]{1,0:T(8,128)(2,1)}, bf16[192,128]{1,0:T(8,128)(2,1)S(1)}, u32[]{:S(2)}) copy-start(bf16[192,128]{1,0:T(8,128)(2,1)S(1)} %collective-permute-done.18.refs_1_) | copy-start | bytes 147460
  118.0 2.7 %copy-start.11 = (bf16[192,128]{1,0:T(8,128)(2,1)}, bf16[192,128]{1,0:T(8,128)(2,1)S(1)}, u32[]{:S(2)}) copy-start(bf16[192,128]{1,0:T(8,128)(2,1)S(1)} %collective-permute-done.19.refs_2_) | copy-start | bytes 147460
  120.7 0.6 copy-start.12
  126.0 2.9 %collective-permute-start.21 = (f32[64,4096]{1,0:T(8,128)}, f32[64,4096]{1,0:T(8,128)S(1)}, u32[]{:S(2)}, u32[]{:S(2)}) collective-permute-start(f32[64,4096]{1,0:T(8,128)} %get-tuple-element.30), channel_id=1, source_target_pairs={{0,4},{4,0},{8,12},{12,8},{16,20},{20,16},{24,28},{28,24},{1,5},{5... | collective-permute-start | bytes 3145736 | tf_op jit(solution)/shard_map/ppermute | solution.py:90
  128.9 1.0 copy-start.3

commit v3 on v2

--- a/solution.py
+++ b/solution.py
@@ -7,6 +7,11 @@
 
 f32, bf16 = jnp.float32, jnp.bfloat16
 params = pltpu.CompilerParams(vmem_limit_bytes=60 << 20)
+
+
+def cost(flops, *arrays):
+    size = sum(array.size * array.dtype.itemsize for array in arrays)
+    return pl.CostEstimate(flops=flops, bytes_accessed=size, transcendentals=0)
 
 
 def after(value, *others):
@@ -76,6 +81,7 @@
         out_specs=vmem,
         out_shape=jax.ShapeDtypeStruct((slabs // 2, 2 * planes * classes, 2 * group), bf16),
         compiler_params=params,
+        cost_estimate=cost(0, tables),
         name="window_slices",
     )(order, tables)
 
@@ -153,7 +159,7 @@
             )
             place += 1
     refs[-2][...] = total[:count]
-    refs[-1][...] = total[count:]
+    refs[-1][...] = total[count:].astype(bf16)
 
 
 def sum_images(values, pixels):
@@ -167,8 +173,9 @@
         in_specs=[pl.BlockSpec((rows, width), lambda i: (0, 0))] * len(values)
         + [pl.BlockSpec((pixel.shape[0], tile), lambda i: (0, i)) for pixel in pixels],
         out_specs=[pl.BlockSpec((width // 2, tile), lambda i: (0, i))] * 2,
-        out_shape=[half, half],
+        out_shape=[half, jax.ShapeDtypeStruct((width // 2, block), bf16)],
         compiler_params=params,
+        cost_estimate=cost(2 * rows * len(values) * width * block, *values, *pixels),
         name="sum_images",
     )(*values, *pixels)
 
@@ -189,6 +196,7 @@
         out_specs=pl.BlockSpec((width // classes, classes, tile), lambda i: (0, 0, i)),
         out_shape=jax.ShapeDtypeStruct((width // classes, classes, block), f32),
         compiler_params=params,
+        cost_estimate=cost(2 * width * block, one, two, one),
         name="add_parts",
     )(one, two)
 
@@ -252,17 +260,17 @@
             jax.ShapeDtypeStruct((2 * len(pieces), depth, group), f32),
         ],
         compiler_params=params,
+        cost_estimate=cost(8 * len(pieces) * planes * classes * group * block, *pieces),
         name="project",
     )(order, *pieces)
 
 
-def match_kernel(count, order_ref, mine_ref, theirs_ref, *refs):
+def match_kernel(order_ref, mine_ref, theirs_ref, *refs):
     pieces, out_ref, pixels_ref = refs[:-2], refs[-2], refs[-1]
-    rows = pieces[0].shape[0] // count
     half = mine_ref.shape[0] - 16
     core = order_ref[0] & 1
-    wide = [piece[...] if rows % 16 == 0 else piece[...].astype(f32) for piece in pieces]
-    stack = [piece[i * rows : (i + 1) * rows] for i in range(count) for piece in wide]
+    exact = pieces[0].shape[0] % 16 == 0
+    stack = [piece[...] if exact else piece[...].astype(f32) for piece in pieces]
     pixels_ref[...] = jnp.concatenate(stack).astype(bf16)
     squares = mine_ref[half:].astype(f32) + theirs_ref[half:].astype(f32)
     energy = jnp.sum(squares, axis=0, keepdims=True)
@@ -273,20 +281,22 @@
     out_ref[...] = total.reshape(out_ref.shape)
 
 
-def match(order, mine, theirs, pieces, count):
+def match(order, mine, theirs, batches):
+    pieces = sum(batches, [])
     rows, block = pieces[0].shape
     rows_all = rows * len(pieces)
     columns = mine.shape[1]
     vmem = pl.BlockSpec(memory_space=pltpu.VMEM)
     return pl.pallas_call(
-        lambda *refs: match_kernel(count, *refs),
+        match_kernel,
         in_specs=[pl.BlockSpec(memory_space=pltpu.SMEM)] + [vmem] * (2 + len(pieces)),
         out_specs=[vmem] * 2,
         out_shape=[
-            jax.ShapeDtypeStruct((count, rows_all // count, columns), f32),
+            jax.ShapeDtypeStruct((len(batches), rows_all // len(batches), columns), f32),
             jax.ShapeDtypeStruct((rows_all, block), bf16),
         ],
         compiler_params=params,
+        cost_estimate=cost(2 * rows_all * block * columns, mine, theirs, *pieces),
         name="match",
     )(order, mine, theirs, *pieces)
 
@@ -315,15 +325,15 @@
     group = classes * own_o
     own_order, other_order = block_orders()
 
-    def fetch(step, *earlier):
+    def part_for(step):
         column = lax.rem(batch + step, batches) * block
-        part = lax.dynamic_slice(images, (slab * rows, column), (rows, block))
-        return shifted(after(part, *earlier) if earlier else part, "batch", step)
+        return lax.dynamic_slice(images, (slab * rows, column), (rows, block))
 
     half = batches // 2
     steps = [step for step in range(1, batches) if step != half]
-    fetched = [fetch(step) for step in steps]
-    last = fetch(half)
+    steps = steps + [half]
+    parts = [part_for(step) for step in steps]
+    fetched = [shifted(part, "batch", step) for part, step in zip(parts, steps)]
 
     coarse = band_start // 128
     table = jnp.concatenate(
@@ -337,30 +347,37 @@
     side = block // 2
     extra = -(-table.size // side)
     table = jnp.pad(table.reshape(-1), (0, extra * side - table.size)).reshape(extra, side)
-    flat = volumes.reshape(width, block)
+    flat = after(volumes, *parts).reshape(width, block)
     mine = lax.dynamic_slice_in_dim(flat, core * side, side, axis=1)
     give = lax.dynamic_slice_in_dim(flat, (1 - core) * side, side, axis=1)
     theirs = paired(jnp.concatenate([give, table]), (1, 1))
     shard = jnp.concatenate([mine, theirs[:width], table, theirs[width:]])
-    shards = spread_end(spread_start(shard))
-    near = spread_start(after(jnp.concatenate(fetched), *shards[1:])) if steps else []
+    shards = spread_start(shard)
+    if len(shards) > 1:
+        shards[1] = after(shards[1], *fetched[:1])
+    shards = spread_end(shards)
+    near = []
+    for part in fetched[:-1]:
+        ties = (near[-1]) if near else (shards[1:])
+        near.append(spread_start(after(part, *ties)))
     order = jnp.stack(own_order)
     mine, prior, tables = project(order, shards, planes, classes, own_o, depth)
-    mine = after(mine, last, *near)
+    held = []
+    mine = after(mine, fetched[-1], *sum(near, []))
     theirs = paired(mine, (1, 1))
 
     own = [lax.dynamic_slice(images, (i * rows, batch * block), (rows, block)) for i in own_order]
-    total, pixels = match(order, mine, theirs, own, 1)
+    total, pixels = match(order, mine, theirs, [own])
     total = total[0]
     pixels = [pixels]
-    if steps:
-        parts, pixel = match(order, mine, theirs, spread_end(near), len(steps))
+    last = spread_start(fetched[-1])
+    for step, each in zip(steps, near):
+        part, pixel = match(order, mine, theirs, [spread_end(each)])
         pixels.append(pixel)
-        for step, part in zip(steps, parts):
-            total = total + shifted(part, "batch", -step)
-    part, pixel = match(order, mine, theirs, spread_end(spread_start(last)), 1)
+        total = total + shifted(part[0], "batch", -step)
+    part, pixel = match(order, mine, theirs, [spread_end(last)])
     pixels.append(pixel)
-    total = total + shifted(part[0], "batch", -half)
+    total = total + shifted(part[0], "batch", -steps[-1])
     total = total.reshape(chips, rows, 2 * group)
 
     def by_rows(blocks):
@@ -376,8 +393,8 @@
     sides = jnp.stack(in_three(own_top.reshape(count)) + in_three(own_total.reshape(count)))
     sides = jnp.pad(sides, ((0, 0), (0, lines * 2 * group - count))).reshape(-1, 2 * group)
     packed = jnp.concatenate([shifted_exp.astype(bf16).reshape(count, 2 * group), sides])
-    mates = [list(range(parity, slabs, 2)) for parity in (0, 1)]
-    packed = lax.all_gather(packed, "slab", axis_index_groups=mates)
+    packed = [packed] + [paired(packed, (2 * i, 2 * i)) for i in range(1, chips)]
+    packed = jnp.stack(packed)
     exps = packed[:, :count]
     sides = packed[:, count:].reshape(chips, 6, lines * 2 * group)[:, :, :count].astype(f32)
     tops = sides[:, 0] + sides[:, 1] + sides[:, 2]
@@ -388,11 +405,13 @@
     weights = (exps.astype(f32) * scale[:, :, None]).astype(bf16)
 
     chip_order = [i // 2 for i in own_order]
-    both = pick(window_slices(order, tables, planes, classes, own_o), chip_places(core))
+    places = list(zip(held_masks(slabs, 0), held_masks(slabs, 1)))
+    places = [(even + core * (odd - even)) // 2 for even, odd in places]
+    both = pick(window_slices(order, tables, planes, classes, own_o), places)
     inserted = jnp.einsum("qzo,qno->nz", both, weights, preferred_element_type=f32).astype(bf16)
     inserted = pick(inserted.reshape(chips, rows, 2 * width), chip_order)
     inserted = inserted.reshape(count, 2 * width)
-    there = [inserted] + [shifted(inserted, "batch", step) for step in steps + [half]]
+    there = [inserted] + [shifted(inserted, "batch", step) for step in steps]
 
     responsibilities = jnp.exp(score.reshape(count, 2 * group) - log_evidence[:, None])
     lines = -(-count // group)

time: 133 us -> 126 us (0.947)
  starting transfers between devices: 23.2 us -> 39.5 us
  waiting for transfers between devices: 52.9 us -> 39.6 us
  blocking collectives: 9.81 us -> 0 us
  Pallas kernels: 26.8 us -> 28.7 us
  other arithmetic: 3.97 us -> 2.54 us
    ppermute x9, waiting for transfers between devices: 37.4 us -> 19.3 us  [shifted(): lax.ppermute(value, axis, [(i, (i + step) % size) for i in range(size)])]
    ppermute x13 -> x19, starting transfers between devices: 11.3 us -> 24.1 us  [paired(): lax.ppermute(value, 'slab', [(i, i ^ masks[i % 2]) for i in range(size)])]
    all_gather x1 -> x0, blocking collectives: 9.81 us -> none  [local(): packed = lax.all_gather(packed, 'slab', axis_index_groups=mates)]
    ppermute x13 -> x19, waiting for transfers between devices: 15.5 us -> 20.3 us  [paired(): lax.ppermute(value, 'slab', [(i, i ^ masks[i % 2]) for i in range(size)])]
    ppermute x9, starting transfers between devices: 11.9 us -> 15.3 us  [shifted(): lax.ppermute(value, axis, [(i, (i + step) % size) for i in range(size)])]
    pallas_call x3 -> x4, Pallas kernels: 12.7 us -> 15 us  [match(): pl.pallas_call(match_kernel, in_specs=[pl.BlockSpec(memory_space=pltpu.SM...]
    unnamed x31 -> x55, local copies, waits for them, and re-layouts: 4.34 us -> 6.32 us
  transfers between devices with their start and end apart: 22 -> 28, of which waited for: 10 -> 13; matrix products, arithmetic and copies ran while one was open for 7% -> 3% of each run, Pallas kernels for 15% -> 17%
where the time goes in v3:
time: 126 us; the launch traced here: 125 us
  waiting for transfers between devices  39.6 us (31%)
  starting transfers between devices  39.5 us (31%)
  Pallas kernels  28.7 us (23%)
  local copies, waits for them, and re-layouts  13.6 us (11%)
  other arithmetic  2.54 us (2%)
    ppermute x19, starting transfers between devices, paired(): lax.ppermute(value, 'slab', [(i, i ^ masks[i % 2]) for i in range(size)])  24.1 us
    ppermute x19, waiting for transfers between devices, paired(): lax.ppermute(value, 'slab', [(i, i ^ masks[i % 2]) for i in range(size)])  20.3 us
    ppermute x9, waiting for transfers between devices, shifted(): lax.ppermute(value, axis, [(i, (i + step) % size) for i in range(size)])  19.3 us
    ppermute x9, starting transfers between devices, shifted(): lax.ppermute(value, axis, [(i, (i + step) % size) for i in range(size)])  15.3 us
    pallas_call x4, Pallas kernels, match(): pl.pallas_call(match_kernel, in_specs=[pl.BlockSpec(memory_space=pltpu.SM...  15 us
    unnamed x55, local copies, waits for them, and re-layouts  6.32 us
    pallas_call x1, Pallas kernels, project(): pl.pallas_call(lambda *refs: project_kernel(planes, classes, own_o, depth...  4.75 us
    pallas_call x1, Pallas kernels, sum_images(): pl.pallas_call(sum_images_kernel, grid=(block // tile,), in_specs=[pl.Blo...  4.45 us
  transfers between devices with their start and end apart: 28, of which 13 were waited for; matrix products, arithmetic and copies ran while one was open for 3% of the time, Pallas kernels for 17%

profile of v3, /device:TPU:0, one launch (start us, length us, event | category | flops | bytes accessed | tf_op | source)
XLA Modules:
  0.0 125.4 jit_solution(2178218212773268715)
XLA Ops:
  0.7 3.1 %fusion.28 = (bf16[48,4096]{1,0:T(8,128)(2,1)}, bf16[48,4096]{1,0:T(8,128)(2,1)}, bf16[48,4096]{1,0:T(8,128)(2,1)}, bf16[48,4096]{1,0:T(8,128)(2,1)S(1)}, bf16[4...) fusion(bf16[384,16384]{1,0:T(8,128)(2,1)} %param.9, s32[]{:T(128)S(6)} %select_n.186, ...), kind=kLoop, calls=%fused_computation.99 | loop fusion | bytes 5505056 | tf_op jit(solution)/shard_map/dynamic_slice | solution.py:369
  5.3 1.2 collective-permute-done
  6.6 2.9 %collective-permute-start.1 = (bf16[134,2048]{1,0:T(8,128)(2,1)S(1)}, bf16[134,2048]{1,0:T(8,128)(2,1)S(1)}, u32[]{:S(2)}, u32[]{:S(2)}) collective-permute-start(bf16[134,2048]{1,0:T(8,128)(2,1)S(1)} %pad_maximum_fusion.refs_1_), channel_id=1, source_target_pairs={{0,8},{4,20},{8,0},{12,28},{16,24},{20,4},{24,16},{28,12},{1,9},{5... | collective-permute-start | bytes 1646600 | tf_op jit(solution)/shard_map/ppermute | solution.py:96
  9.5 1.6 %collective-permute-start.2 = (bf16[48,4096]{1,0:T(8,128)(2,1)S(1)}, bf16[48,4096]{1,0:T(8,128)(2,1)S(1)}, u32[]{:S(2)}, u32[]{:S(2)}) collective-permute-start(bf16[48,4096]{1,0:T(8,128)(2,1)S(1)} %get-tuple-element.55), channel_id=1, source_target_pairs={{0,1},{1,2},{2,3},{3,0},{4,5},{5,6},{6,7},{7,4},{8,9},{9,10},{10,1... | collective-permute-start | bytes 1179656 | tf_op jit(solution)/shard_map/ppermute | solution.py:91
  11.1 1.5 %collective-permute-start.3 = (bf16[134,2048]{1,0:T(8,128)(2,1)S(1)}, bf16[134,2048]{1,0:T(8,128)(2,1)S(1)}, u32[]{:S(2)}, u32[]{:S(2)}) collective-permute-start(bf16[134,2048]{1,0:T(8,128)(2,1)S(1)} %pad_maximum_fusion.refs_1_), channel_id=1, source_target_pairs={{0,16},{4,12},{8,24},{12,4},{16,0},{20,28},{24,8},{28,20},{1,17},{... | collective-permute-start | bytes 1646600 | tf_op jit(solution)/shard_map/ppermute | solution.py:96
  12.6 9.7 %collective-permute-done.2.refs_0_ = bf16[48,4096]{1,0:T(8,128)(2,1)S(1)} collective-permute-done((bf16[48,4096]{1,0:T(8,128)(2,1)S(1)}, bf16[48,4096]{1,0:T(8,128)(2,1)S(1)}, u32[]{:S(2)}, u32[]{:S(2)}) %collective-permute-start.2) | collective-permute-done | bytes 393248 | tf_op jit(solution)/shard_map/ppermute | solution.py:91
  22.3 2.1 %collective-permute-start.4 = (bf16[134,2048]{1,0:T(8,128)(2,1)S(1)}, bf16[134,2048]{1,0:T(8,128)(2,1)S(1)}, u32[]{:S(2)}, u32[]{:S(2)}) collective-permute-start(bf16[134,2048]{1,0:T(8,128)(2,1)S(1)} %collective-permute-done.1.refs_2_), channel_id=1, source_target_pairs={{0,16},{4,12},{8,24},{12,4},{16,0},{20,28},{24,8},{28,20},{1,17},{... | collective-permute-start | bytes 1646600 | tf_op jit(solution)/shard_map/ppermute | solution.py:96
  24.4 3.6 %collective-permute-start.8 = (bf16[48,4096]{1,0:T(8,128)(2,1)S(1)}, bf16[48,4096]{1,0:T(8,128)(2,1)S(1)}, u32[]{:S(2)}, u32[]{:S(2)}) collective-permute-start(bf16[48,4096]{1,0:T(8,128)(2,1)S(1)} %get-tuple-element.54), channel_id=1, source_target_pairs={{0,3},{1,0},{2,1},{3,2},{4,7},{5,4},{6,5},{7,6},{8,11},{9,8},{10,9... | collective-permute-start | bytes 1179656 | tf_op jit(solution)/shard_map/ppermute | solution.py:91
  28.1 3.9 %collective-permute-done.4.refs_4_ = bf16[134,2048]{1,0:T(8,128)(2,1)S(1)} collective-permute-done((bf16[134,2048]{1,0:T(8,128)(2,1)S(1)}, bf16[134,2048]{1,0:T(8,128)(2,1)S(1)}, u32[]{:S(2)}, u32[]{:S(2)}) %collective-permute-start.4) | collective-permute-done | bytes 548896 | tf_op jit(solution)/shard_map/ppermute | solution.py:96
  31.9 1.5 %collective-permute-start.6 = (bf16[48,4096]{1,0:T(8,128)(2,1)S(1)}, bf16[48,4096]{1,0:T(8,128)(2,1)S(1)}, u32[]{:S(2)}, u32[]{:S(2)}) collective-permute-start(bf16[48,4096]{1,0:T(8,128)(2,1)S(1)} %collective-permute-done.2.refs_0_), channel_id=1, source_target_pairs={{0,8},{4,20},{8,0},{12,28},{16,24},{20,4},{24,16},{28,12},{1,9},{5... | collective-permute-start | bytes 1179656 | tf_op jit(solution)/shard_map/ppermute | solution.py:96
  33.4 2.2 %collective-permute-start.7 = (bf16[48,4096]{1,0:T(8,128)(2,1)S(1)}, bf16[48,4096]{1,0:T(8,128)(2,1)S(1)}, u32[]{:S(2)}, u32[]{:S(2)}) collective-permute-start(bf16[48,4096]{1,0:T(8,128)(2,1)S(1)} %collective-permute-done.2.refs_0_), channel_id=1, source_target_pairs={{0,16},{4,12},{8,24},{12,4},{16,0},{20,28},{24,8},{28,20},{1,17},{... | collective-permute-start | bytes 1179656 | tf_op jit(solution)/shard_map/ppermute | solution.py:96
  35.6 2.6 %collective-permute-start.5 = (bf16[48,4096]{1,0:T(8,128)(2,1)S(1)}, bf16[48,4096]{1,0:T(8,128)(2,1)}, u32[]{:S(2)}, u32[]{:S(2)}) collective-permute-start(bf16[48,4096]{1,0:T(8,128)(2,1)S(1)} %get-tuple-element.53), channel_id=1, source_target_pairs={{0,2},{1,3},{2,0},{3,1},{4,6},{5,7},{6,4},{7,5},{8,10},{9,11},{10,... | collective-permute-start | bytes 1179656 | tf_op jit(solution)/shard_map/ppermute | solution.py:91
  38.2 3.7 %collective-permute-done.6.refs_1_ = bf16[48,4096]{1,0:T(8,128)(2,1)S(1)} collective-permute-done((bf16[48,4096]{1,0:T(8,128)(2,1)S(1)}, bf16[48,4096]{1,0:T(8,128)(2,1)S(1)}, u32[]{:S(2)}, u32[]{:S(2)}) %collective-permute-start.6) | collective-permute-done | bytes 393248 | tf_op jit(solution)/shard_map/ppermute | solution.py:96
  41.9 0.8 copy-done.10
  42.6 1.5 %collective-permute-start.10 = (bf16[48,4096]{1,0:T(8,128)(2,1)S(1)}, bf16[48,4096]{1,0:T(8,128)(2,1)}, u32[]{:S(2)}, u32[]{:S(2)}) collective-permute-start(bf16[48,4096]{1,0:T(8,128)(2,1)S(1)} %collective-permute-done.8.refs_0_), channel_id=1, source_target_pairs={{0,16},{4,12},{8,24},{12,4},{16,0},{20,28},{24,8},{28,20},{1,17},{... | collective-permute-start | bytes 1179656 | tf_op jit(solution)/shard_map/ppermute | solution.py:96
  44.1 1.7 %collective-permute-start.9 = (bf16[48,4096]{1,0:T(8,128)(2,1)S(1)}, bf16[48,4096]{1,0:T(8,128)(2,1)}, u32[]{:S(2)}, u32[]{:S(2)}) collective-permute-start(bf16[48,4096]{1,0:T(8,128)(2,1)S(1)} %collective-permute-done.8.refs_0_), channel_id=1, source_target_pairs={{0,8},{4,20},{8,0},{12,28},{16,24},{20,4},{24,16},{28,12},{1,9},{5... | collective-permute-start | bytes 1179656 | tf_op jit(solution)/shard_map/ppermute | solution.py:96
  46.4 4.8 %project.1 = (bf16[2064,256]{1,0:T(8,128)(2,1)}, f32[1,256]{1,0:T(1,128)}, f32[8,37,128]{2,1,0:T(8,128)}) custom-call(s32[4]{0:T(128)} %pad_add_fusion.refs_0_.order_ref, bf16[134,2048]{1,0:T(8,128)(2,1)} %copy-done.1, bf16[134,2048]{1,0:T(8,128)(2,1)} %copy-done.3, bf16[134,2048]{1,0:T(8,128)(2,1)} %copy-done.4, bf16[134,2048]{1,0:T(8,128)(2,1)} %copy-done.5), custom_call_target="tpu_custom_call" | custom-call | flops 536870912 | bytes 2195456 | tf_op jit(solution)/shard_map/project/pallas_call | solution.py:253
  51.2 1.3 %collective-permute-done.5.refs_0_ = bf16[48,4096]{1,0:T(8,128)(2,1)} collective-permute-done((bf16[48,4096]{1,0:T(8,128)(2,1)S(1)}, bf16[48,4096]{1,0:T(8,128)(2,1)}, u32[]{:S(2)}, u32[]{:S(2)}) %collective-permute-start.5) | collective-permute-done | bytes 393248 | tf_op jit(solution)/shard_map/ppermute | solution.py:91
  52.5 1.2 collective-permute-start.16
  53.7 1.0 collective-permute-start.12
  54.7 1.1 collective-permute-start.14
  55.8 1.0 collective-permute-start.17
  56.7 7.4 %collective-permute-done.16.refs_1_ = bf16[48,4096]{1,0:T(8,128)(2,1)S(1)} collective-permute-done((bf16[48,4096]{1,0:T(8,128)(2,1)}, bf16[48,4096]{1,0:T(8,128)(2,1)S(1)}, u32[]{:S(2)}, u32[]{:S(2)}) %collective-permute-start.16) | collective-permute-done | bytes 393248 | tf_op jit(solution)/shard_map/ppermute | solution.py:96
  64.1 2.4 %collective-permute-start.18 = (bf16[48,4096]{1,0:T(8,128)(2,1)S(1)}, bf16[48,4096]{1,0:T(8,128)(2,1)S(1)}, u32[]{:S(2)}, u32[]{:S(2)}) collective-permute-start(bf16[48,4096]{1,0:T(8,128)(2,1)S(1)} %collective-permute-done.16.refs_1_), channel_id=1, source_target_pairs={{0,16},{4,12},{8,24},{12,4},{16,0},{20,28},{24,8},{28,20},{1,17},{... | collective-permute-start | bytes 1179656 | tf_op jit(solution)/shard_map/ppermute | solution.py:96
  66.5 0.7 copy-done.17
  67.2 1.1 copy-done
  68.3 3.8 %match.5 = (f32[1,192,256]{2,1,0:T(8,128)}, bf16[192,4096]{1,0:T(8,128)(2,1)}) custom-call(s32[4]{0:T(128)} %pad_add_fusion.refs_0_.order_ref, bf16[2064,256]{1,0:T(8,128)(2,1)} %get-tuple-element.27.mine_ref, bf16[2064,256]{1,0:T(8,128)(2,1)} %copy-done, bf16[48,4096]{1,0:T(8,128)(2,1)} %copy-done.8, bf16[48,4096]{1,0:T(8,128)(2,1)} %copy-done.10, ...), custom_call_target="tpu_custom_call" | custom-call | flops 402653184 | bytes 3686400 | tf_op jit(solution)/shard_map/match/pallas_call | solution.py:290
  72.1 3.0 %collective-permute-start.13 = (f32[192,256]{1,0:T(8,128)}, f32[192,256]{1,0:T(8,128)S(1)}, u32[]{:S(2)}, u32[]{:S(2)}) collective-permute-start(f32[192,256]{1,0:T(8,128)} %bitcast.89), channel_id=1, source_target_pairs={{0,3},{1,0},{2,1},{3,2},{4,7},{5,4},{6,5},{7,6},{8,11},{9,8},{10,9... | collective-permute-start | bytes 589832 | tf_op jit(solution)/shard_map/ppermute | solution.py:91
  75.9 3.7 %match.6 = (f32[1,192,256]{2,1,0:T(8,128)}, bf16[192,4096]{1,0:T(8,128)(2,1)}) custom-call(s32[4]{0:T(128)} %pad_add_fusion.refs_0_.order_ref, bf16[2064,256]{1,0:T(8,128)(2,1)} %get-tuple-element.27.mine_ref, bf16[2064,256]{1,0:T(8,128)(2,1)} %copy-done, bf16[48,4096]{1,0:T(8,128)(2,1)} %copy-done.9, bf16[48,4096]{1,0:T(8,128)(2,1)} %collective-permute-done.9.refs_1_, ...), custom_call_target="tpu_custom_call" | custom-call | flops 402653184 | bytes 3686400 | tf_op jit(solution)/shard_map/match/pallas_call | solution.py:290
  80.5 0.8 copy-done.15
  81.2 3.7 %match.7 = (f32[1,192,256]{2,1,0:T(8,128)}, bf16[192,4096]{1,0:T(8,128)(2,1)}) custom-call(s32[4]{0:T(128)} %pad_add_fusion.refs_0_.order_ref, bf16[2064,256]{1,0:T(8,128)(2,1)} %get-tuple-element.27.mine_ref, bf16[2064,256]{1,0:T(8,128)(2,1)} %copy-done, bf16[48,4096]{1,0:T(8,128)(2,1)} %collective-permute-done.5.refs_0_, bf16[48,4096]{1,0:T(8,128)(2,1)} %copy-done.13, ...), custom_call_target="tpu_custom_call" | custom-call | flops 402653184 | bytes 3686400 | tf_op jit(solution)/shard_map/match/pallas_call | solution.py:290
  86.9 2.0 %window_slices.1 = bf16[4,128,256]{2,1,0:T(8,128)(2,1)} custom-call(s32[4]{0:T(128)} %pad_add_fusion.refs_0_.order_ref, f32[8,37,128]{2,1,0:T(8,128)} %get-tuple-element.33.refs_1_), custom_call_target="tpu_custom_call" | custom-call | bytes 151552 | tf_op jit(solution)/shard_map/window_slices/pallas_call | solution.py:78
  88.9 3.8 %match.4 = (f32[1,192,256]{2,1,0:T(8,128)}, bf16[192,4096]{1,0:T(8,128)(2,1)}) custom-call(s32[4]{0:T(128)} %pad_add_fusion.refs_0_.order_ref, bf16[2064,256]{1,0:T(8,128)(2,1)} %get-tuple-element.27.mine_ref, bf16[2064,256]{1,0:T(8,128)(2,1)} %copy-done, bf16[48,4096]{1,0:T(8,128)(2,1)} %get-tuple-element.52.refs_0_, ...), custom_call_target="tpu_custom_call" | custom-call | flops 402653184 | bytes 3686400 | tf_op jit(solution)/shard_map/match/pallas_call | solution.py:290
  92.7 3.1 %collective-permute-done.19 = f32[192,256]{1,0:T(8,128)S(1)} collective-permute-done((f32[192,256]{1,0:T(8,128)}, f32[192,256]{1,0:T(8,128)S(1)}, u32[]{:S(2)}, u32[]{:S(2)}) %collective-permute-start.19) | collective-permute-done | bytes 196640 | tf_op jit(solution)/shard_map/ppermute | solution.py:91
  95.8 1.0 fusion.13
  98.4 1.1 collective-permute-start.21
  99.5 1.8 %collective-permute-start.22 = (bf16[198,256]{1,0:T(8,128)(2,1)S(1)}, bf16[198,256]{1,0:T(8,128)(2,1)S(1)}, u32[]{:S(2)}, u32[]{:S(2)}) collective-permute-start(bf16[198,256]{1,0:T(8,128)(2,1)S(1)} %get-tuple-element.75), channel_id=1, source_target_pairs={{0,24},{4,28},{8,16},{12,20},{16,8},{20,12},{24,0},{28,4},{1,25},{... | collective-permute-start | bytes 304136 | tf_op jit(solution)/shard_map/ppermute | solution.py:96
  101.3 1.8 %collective-permute-done.20 = bf16[198,256]{1,0:T(8,128)(2,1)S(1)} collective-permute-done((bf16[198,256]{1,0:T(8,128)(2,1)S(1)}, bf16[198,256]{1,0:T(8,128)(2,1)S(1)}, u32[]{:S(2)}, u32[]{:S(2)}) %collective-permute-start.20) | collective-permute-done | bytes 101408 | tf_op jit(solution)/shard_map/ppermute | solution.py:96
  103.1 0.8 collective-permute-done.21
  103.9 1.1 collective-permute-done.22
  105.8 0.8 collective-permute-start.24
  106.6 3.1 %collective-permute-start.25 = (bf16[192,128]{1,0:T(8,128)(2,1)S(1)}, bf16[192,128]{1,0:T(8,128)(2,1)S(1)}, u32[]{:S(2)}, u32[]{:S(2)}) collective-permute-start(bf16[192,128]{1,0:T(8,128)(2,1)S(1)} %bitcast.76), channel_id=1, source_target_pairs={{0,3},{1,0},{2,1},{3,2},{4,7},{5,4},{6,5},{7,6},{8,11},{9,8},{10,9... | collective-permute-start | bytes 147464 | tf_op jit(solution)/shard_map/ppermute | solution.py:91
  109.7 2.5 %collective-permute-done.24.refs_1_ = bf16[192,128]{1,0:T(8,128)(2,1)S(1)} collective-permute-done((bf16[192,128]{1,0:T(8,128)(2,1)S(1)}, bf16[192,128]{1,0:T(8,128)(2,1)S(1)}, u32[]{:S(2)}, u32[]{:S(2)}) %collective-permute-start.24) | collective-permute-done | bytes 49184 | tf_op jit(solution)/shard_map/ppermute | solution.py:91
  112.2 2.7 %collective-permute-done.26.refs_3_ = bf16[192,128]{1,0:T(8,128)(2,1)S(1)} collective-permute-done((bf16[192,128]{1,0:T(8,128)(2,1)S(1)}, bf16[192,128]{1,0:T(8,128)(2,1)S(1)}, u32[]{:S(2)}, u32[]{:S(2)}) %collective-permute-start.26) | collective-permute-done | bytes 49184 | tf_op jit(solution)/shard_map/ppermute | solution.py:91
  115.5 4.5 %sum_images.1 = (f32[64,4096]{1,0:T(8,128)}, bf16[64,4096]{1,0:T(8,128)(2,1)}) custom-call(bf16[192,128]{1,0:T(8,128)(2,1)} %bitcast.78, bf16[192,128]{1,0:T(8,128)(2,1)} %copy-done.19, bf16[192,128]{1,0:T(8,128)(2,1)} %copy-done.20, bf16[192,128]{1,0:T(8,128)(2,1)} %copy-done.21, bf16[192,4096]{1,0:T(8,128)(2,1)} %get-tuple-element.35.refs_4_, ...), custom_call_target="tpu_custom_call" | custom-call | flops 805306368 | bytes 6488064 | tf_op jit(solution)/shard_map/sum_images/pallas_call | solution.py:170
  120.9 0.8 copy.27
  122.1 0.8 copy-done.6
  122.9 2.5 %add_parts.1 = f32[32,2,4096]{2,1,0:T(2,128)} custom-call(f32[64,4096]{1,0:T(8,128)} %get-tuple-element.39.one_ref, bf16[64,4096]{1,0:T(8,128)(2,1)} %copy-done.6), custom_call_target="tpu_custom_call" | custom-call | flops 524288 | bytes 2621440 | tf_op jit(solution)/shard_map/add_parts/pallas_call | solution.py:192
  (129 shorter events, 9.7 us)
Async XLA Ops:
  0.7 3.1 %copy-start.7 = (bf16[32,2,4096]{2,1,0:T(2,128)(2,1)S(1)}, bf16[32,2,4096]{2,1,0:T(2,128)(2,1)}, u32[]{:S(2)}) copy-start(bf16[32,2,4096]{2,1,0:T(2,128)(2,1)} %param.6) | copy-start | bytes 1572868
  0.7 3.3 %copy-start.25 = (f32[2,64]{1,0:T(2,128)S(1)}, f32[2,64]{1,0:T(2,128)}, u32[]{:S(2)}) copy-start(f32[2,64]{1,0:T(2,128)} %param.11) | copy-start | bytes 1540
  0.7 3.6 %copy-start.26 = (s32[2,64]{1,0:T(2,128)S(1)}, s32[2,64]{1,0:T(2,128)}, u32[]{:S(2)}) copy-start(s32[2,64]{1,0:T(2,128)} %param.8) | copy-start | bytes 1540
  0.7 3.8 %copy-start.23 = (bf16[2,64,32]{1,2,0:T(8,128)(2,1)S(1)}, bf16[2,64,32]{1,2,0:T(8,128)(2,1)}, u32[]{:S(2)}) copy-start(bf16[2,64,32]{1,2,0:T(8,128)(2,1)} %param.7) | copy-start | bytes 24580
  4.7 1.7 %collective-permute-start = (bf16[67,2048]{1,0:T(8,128)(2,1)S(1)}, bf16[67,2048]{1,0:T(8,128)(2,1)S(1)}, u32[]{:S(2)}, u32[]{:S(2)}) collective-permute-start(bf16[67,2048]{1,0:T(8,128)(2,1)S(1)} %pad_maximum_fusion.7), channel_id=1, source_target_pairs={{0,4},{4,0},{8,12},{12,8},{16,20},{20,16},{24,28},{28,24},{1,5},{5... | collective-permute-start | bytes 823304 | tf_op jit(solution)/shard_map/ppermute | solution.py:96
  6.6 39.8 %copy-start.1 = (bf16[134,2048]{1,0:T(8,128)(2,1)}, bf16[134,2048]{1,0:T(8,128)(2,1)S(1)}, u32[]{:S(2)}) copy-start(bf16[134,2048]{1,0:T(8,128)(2,1)S(1)} %pad_maximum_fusion.refs_1_) | copy-start | bytes 1646596
  6.6 15.7 %collective-permute-start.1 = (bf16[134,2048]{1,0:T(8,128)(2,1)S(1)}, bf16[134,2048]{1,0:T(8,128)(2,1)S(1)}, u32[]{:S(2)}, u32[]{:S(2)}) collective-permute-start(bf16[134,2048]{1,0:T(8,128)(2,1)S(1)} %pad_maximum_fusion.refs_1_), channel_id=1, source_target_pairs={{0,8},{4,20},{8,0},{12,28},{16,24},{20,4},{24,16},{28,12},{1,9},{5... | collective-permute-start | bytes 1646600 | tf_op jit(solution)/shard_map/ppermute | solution.py:96
  9.5 12.8 %collective-permute-start.2 = (bf16[48,4096]{1,0:T(8,128)(2,1)S(1)}, bf16[48,4096]{1,0:T(8,128)(2,1)S(1)}, u32[]{:S(2)}, u32[]{:S(2)}) collective-permute-start(bf16[48,4096]{1,0:T(8,128)(2,1)S(1)} %get-tuple-element.55), channel_id=1, source_target_pairs={{0,1},{1,2},{2,3},{3,0},{4,5},{5,6},{6,7},{7,4},{8,9},{9,10},{10,1... | collective-permute-start | bytes 1179656 | tf_op jit(solution)/shard_map/ppermute | solution.py:91
  11.1 17.0 %collective-permute-start.3 = (bf16[134,2048]{1,0:T(8,128)(2,1)S(1)}, bf16[134,2048]{1,0:T(8,128)(2,1)S(1)}, u32[]{:S(2)}, u32[]{:S(2)}) collective-permute-start(bf16[134,2048]{1,0:T(8,128)(2,1)S(1)} %pad_maximum_fusion.refs_1_), channel_id=1, source_target_pairs={{0,16},{4,12},{8,24},{12,4},{16,0},{20,28},{24,8},{28,20},{1,17},{... | collective-permute-start | bytes 1646600 | tf_op jit(solution)/shard_map/ppermute | solution.py:96
  22.3 45.0 %copy-start.8 = (bf16[48,4096]{1,0:T(8,128)(2,1)}, bf16[48,4096]{1,0:T(8,128)(2,1)S(1)}, u32[]{:S(2)}) copy-start(bf16[48,4096]{1,0:T(8,128)(2,1)S(1)} %collective-permute-done.2.refs_0_) | copy-start | bytes 1179652
  22.3 24.1 %copy-start.3 = (bf16[134,2048]{1,0:T(8,128)(2,1)}, bf16[134,2048]{1,0:T(8,128)(2,1)S(1)}, u32[]{:S(2)}) copy-start(bf16[134,2048]{1,0:T(8,128)(2,1)S(1)} %collective-permute-done.1.refs_2_) | copy-start | bytes 1646596
  22.3 9.6 %collective-permute-start.4 = (bf16[134,2048]{1,0:T(8,128)(2,1)S(1)}, bf16[134,2048]{1,0:T(8,128)(2,1)S(1)}, u32[]{:S(2)}, u32[]{:S(2)}) collective-permute-start(bf16[134,2048]{1,0:T(8,128)(2,1)S(1)} %collective-permute-done.1.refs_2_), channel_id=1, source_target_pairs={{0,16},{4,12},{8,24},{12,4},{16,0},{20,28},{24,8},{28,20},{1,17},{... | collective-permute-start | bytes 1646600 | tf_op jit(solution)/shard_map/ppermute | solution.py:96
  24.4 13.8 %collective-permute-start.8 = (bf16[48,4096]{1,0:T(8,128)(2,1)S(1)}, bf16[48,4096]{1,0:T(8,128)(2,1)S(1)}, u32[]{:S(2)}, u32[]{:S(2)}) collective-permute-start(bf16[48,4096]{1,0:T(8,128)(2,1)S(1)} %get-tuple-element.54), channel_id=1, source_target_pairs={{0,3},{1,0},{2,1},{3,2},{4,7},{5,4},{6,5},{7,6},{8,11},{9,8},{10,9... | collective-permute-start | bytes 1179656 | tf_op jit(solution)/shard_map/ppermute | solution.py:91
  28.0 18.4 %copy-start.4 = (bf16[134,2048]{1,0:T(8,128)(2,1)}, bf16[134,2048]{1,0:T(8,128)(2,1)S(1)}, u32[]{:S(2)}) copy-start(bf16[134,2048]{1,0:T(8,128)(2,1)S(1)} %collective-permute-done.3.refs_3_) | copy-start | bytes 1646596
  31.9 14.5 %copy-start.5 = (bf16[134,2048]{1,0:T(8,128)(2,1)}, bf16[134,2048]{1,0:T(8,128)(2,1)S(1)}, u32[]{:S(2)}) copy-start(bf16[134,2048]{1,0:T(8,128)(2,1)S(1)} %collective-permute-done.4.refs_4_) | copy-start | bytes 1646596
  31.9 10.0 %collective-permute-start.6 = (bf16[48,4096]{1,0:T(8,128)(2,1)S(1)}, bf16[48,4096]{1,0:T(8,128)(2,1)S(1)}, u32[]{:S(2)}, u32[]{:S(2)}) collective-permute-start(bf16[48,4096]{1,0:T(8,128)(2,1)S(1)} %collective-permute-done.2.refs_0_), channel_id=1, source_target_pairs={{0,8},{4,20},{8,0},{12,28},{16,24},{20,4},{24,16},{28,12},{1,9},{5... | collective-permute-start | bytes 1179656 | tf_op jit(solution)/shard_map/ppermute | solution.py:96
  33.4 8.5 %collective-permute-start.7 = (bf16[48,4096]{1,0:T(8,128)(2,1)S(1)}, bf16[48,4096]{1,0:T(8,128)(2,1)S(1)}, u32[]{:S(2)}, u32[]{:S(2)}) collective-permute-start(bf16[48,4096]{1,0:T(8,128)(2,1)S(1)} %collective-permute-done.2.refs_0_), channel_id=1, source_target_pairs={{0,16},{4,12},{8,24},{12,4},{16,0},{20,28},{24,8},{28,20},{1,17},{... | collective-permute-start | bytes 1179656 | tf_op jit(solution)/shard_map/ppermute | solution.py:96
  35.6 16.9 %collective-permute-start.5 = (bf16[48,4096]{1,0:T(8,128)(2,1)S(1)}, bf16[48,4096]{1,0:T(8,128)(2,1)}, u32[]{:S(2)}, u32[]{:S(2)}) collective-permute-start(bf16[48,4096]{1,0:T(8,128)(2,1)S(1)} %get-tuple-element.53), channel_id=1, source_target_pairs={{0,2},{1,3},{2,0},{3,1},{4,6},{5,7},{6,4},{7,5},{8,10},{9,11},{10,... | collective-permute-start | bytes 1179656 | tf_op jit(solution)/shard_map/ppermute | solution.py:91
  38.2 13.0 %copy-start.9 = (bf16[48,4096]{1,0:T(8,128)(2,1)}, bf16[48,4096]{1,0:T(8,128)(2,1)S(1)}, u32[]{:S(2)}) copy-start(bf16[48,4096]{1,0:T(8,128)(2,1)S(1)} %collective-permute-done.8.refs_0_) | copy-start | bytes 1179652
  42.6 1.5 %copy-start.12 = (bf16[48,4096]{1,0:T(8,128)(2,1)}, bf16[48,4096]{1,0:T(8,128)(2,1)S(1)}, u32[]{:S(2)}) copy-start(bf16[48,4096]{1,0:T(8,128)(2,1)S(1)} %collective-permute-done.7.refs_2_) | copy-start | bytes 1179652
  42.6 9.9 %collective-permute-start.10 = (bf16[48,4096]{1,0:T(8,128)(2,1)S(1)}, bf16[48,4096]{1,0:T(8,128)(2,1)}, u32[]{:S(2)}, u32[]{:S(2)}) collective-permute-start(bf16[48,4096]{1,0:T(8,128)(2,1)S(1)} %collective-permute-done.8.refs_0_), channel_id=1, source_target_pairs={{0,16},{4,12},{8,24},{12,4},{16,0},{20,28},{24,8},{28,20},{1,17},{... | collective-permute-start | bytes 1179656 | tf_op jit(solution)/shard_map/ppermute | solution.py:96
  44.1 8.4 %collective-permute-start.9 = (bf16[48,4096]{1,0:T(8,128)(2,1)S(1)}, bf16[48,4096]{1,0:T(8,128)(2,1)}, u32[]{:S(2)}, u32[]{:S(2)}) collective-permute-start(bf16[48,4096]{1,0:T(8,128)(2,1)S(1)} %collective-permute-done.8.refs_0_), channel_id=1, source_target_pairs={{0,8},{4,20},{8,0},{12,28},{16,24},{20,4},{24,16},{28,12},{1,9},{5... | collective-permute-start | bytes 1179656 | tf_op jit(solution)/shard_map/ppermute | solution.py:96
  46.4 7.3 %copy-start.11 = (bf16[48,4096]{1,0:T(8,128)(2,1)S(1)}, bf16[48,4096]{1,0:T(8,128)(2,1)}, u32[]{:S(2)}) copy-start(bf16[48,4096]{1,0:T(8,128)(2,1)} %copy-done.10) | copy-start | bytes 1179652
  52.5 14.7 %collective-permute-start.11 = (bf16[2064,256]{1,0:T(8,128)(2,1)}, bf16[2064,256]{1,0:T(8,128)(2,1)S(1)}, u32[]{:S(2)}, u32[]{:S(2)}) collective-permute-start(bf16[2064,256]{1,0:T(8,128)(2,1)} %get-tuple-element.27.mine_ref), channel_id=1, source_target_pairs={{0,4},{4,0},{8,12},{12,8},{16,20},{20,16},{24,28},{28,24},{1,5},{5... | collective-permute-start | bytes 3170312 | tf_op jit(solution)/shard_map/ppermute | solution.py:96
  52.5 11.6 %collective-permute-start.16 = (bf16[48,4096]{1,0:T(8,128)(2,1)}, bf16[48,4096]{1,0:T(8,128)(2,1)S(1)}, u32[]{:S(2)}, u32[]{:S(2)}) collective-permute-start(bf16[48,4096]{1,0:T(8,128)(2,1)} %collective-permute-done.5.refs_0_), channel_id=1, source_target_pairs={{0,8},{4,20},{8,0},{12,28},{16,24},{20,4},{24,16},{28,12},{1,9},{5... | collective-permute-start | bytes 1179656 | tf_op jit(solution)/shard_map/ppermute | solution.py:96
  53.7 12.7 %collective-permute-start.12 = (bf16[48,4096]{1,0:T(8,128)(2,1)S(1)}, bf16[48,4096]{1,0:T(8,128)(2,1)S(1)}, u32[]{:S(2)}, u32[]{:S(2)}) collective-permute-start(bf16[48,4096]{1,0:T(8,128)(2,1)S(1)} %copy-done.11), channel_id=1, source_target_pairs={{0,16},{4,12},{8,24},{12,4},{16,0},{20,28},{24,8},{28,20},{1,17},{... | collective-permute-start | bytes 1179656 | tf_op jit(solution)/shard_map/ppermute | solution.py:96
  54.7 20.5 %collective-permute-start.14 = (bf16[48,4096]{1,0:T(8,128)(2,1)}, bf16[48,4096]{1,0:T(8,128)(2,1)S(1)}, u32[]{:S(2)}, u32[]{:S(2)}) collective-permute-start(bf16[48,4096]{1,0:T(8,128)(2,1)} %collective-permute-done.9.refs_1_), channel_id=1, source_target_pairs={{0,16},{4,12},{8,24},{12,4},{16,0},{20,28},{24,8},{28,20},{1,17},{... | collective-permute-start | bytes 1179656 | tf_op jit(solution)/shard_map/ppermute | solution.py:96
  55.8 23.9 %collective-permute-start.17 = (bf16[48,4096]{1,0:T(8,128)(2,1)}, bf16[48,4096]{1,0:T(8,128)(2,1)S(1)}, u32[]{:S(2)}, u32[]{:S(2)}) collective-permute-start(bf16[48,4096]{1,0:T(8,128)(2,1)} %collective-permute-done.5.refs_0_), channel_id=1, source_target_pairs={{0,16},{4,12},{8,24},{12,4},{16,0},{20,28},{24,8},{28,20},{1,17},{... | collective-permute-start | bytes 1179656 | tf_op jit(solution)/shard_map/ppermute | solution.py:96
  64.1 15.5 %copy-start.13 = (bf16[48,4096]{1,0:T(8,128)(2,1)}, bf16[48,4096]{1,0:T(8,128)(2,1)S(1)}, u32[]{:S(2)}) copy-start(bf16[48,4096]{1,0:T(8,128)(2,1)S(1)} %collective-permute-done.16.refs_1_) | copy-start | bytes 1179652
  64.1 15.6 %collective-permute-start.18 = (bf16[48,4096]{1,0:T(8,128)(2,1)S(1)}, bf16[48,4096]{1,0:T(8,128)(2,1)S(1)}, u32[]{:S(2)}, u32[]{:S(2)}) collective-permute-start(bf16[48,4096]{1,0:T(8,128)(2,1)S(1)} %collective-permute-done.16.refs_1_), channel_id=1, source_target_pairs={{0,16},{4,12},{8,24},{12,4},{16,0},{20,28},{24,8},{28,20},{1,17},{... | collective-permute-start | bytes 1179656 | tf_op jit(solution)/shard_map/ppermute | solution.py:96
  67.2 1.1 copy-start
  72.1 20.6 %collective-permute-start.13 = (f32[192,256]{1,0:T(8,128)}, f32[192,256]{1,0:T(8,128)S(1)}, u32[]{:S(2)}, u32[]{:S(2)}) collective-permute-start(f32[192,256]{1,0:T(8,128)} %bitcast.89), channel_id=1, source_target_pairs={{0,3},{1,0},{2,1},{3,2},{4,7},{5,4},{6,5},{7,6},{8,11},{9,8},{10,9... | collective-permute-start | bytes 589832 | tf_op jit(solution)/shard_map/ppermute | solution.py:91
  79.6 5.9 %copy-start.24 = (f32[384]{0:T(512)S(1)}, f32[384]{0:T(512)}, u32[]{:S(2)}) copy-start(f32[384]{0:T(512)} %param.10) | copy-start | bytes 4612
  79.6 13.0 %collective-permute-start.15 = (f32[192,256]{1,0:T(8,128)}, f32[192,256]{1,0:T(8,128)S(1)}, u32[]{:S(2)}, u32[]{:S(2)}) collective-permute-start(f32[192,256]{1,0:T(8,128)} %bitcast.90), channel_id=1, source_target_pairs={{0,1},{1,2},{2,3},{3,0},{4,5},{5,6},{6,7},{7,4},{8,9},{9,10},{10,1... | collective-permute-start | bytes 589832 | tf_op jit(solution)/shard_map/ppermute | solution.py:91
  85.0 10.8 %collective-permute-start.19 = (f32[192,256]{1,0:T(8,128)}, f32[192,256]{1,0:T(8,128)S(1)}, u32[]{:S(2)}, u32[]{:S(2)}) collective-permute-start(f32[192,256]{1,0:T(8,128)} %bitcast.91), channel_id=1, source_target_pairs={{0,2},{1,3},{2,0},{3,1},{4,6},{5,7},{6,4},{7,5},{8,10},{9,11},{10,... | collective-permute-start | bytes 589832 | tf_op jit(solution)/shard_map/ppermute | solution.py:91
  92.7 4.2 %copy-start.22 = (f32[1,256]{1,0:T(1,128)S(1)}, f32[1,256]{1,0:T(1,128)}, u32[]{:S(2)}) copy-start(f32[1,256]{1,0:T(1,128)} %get-tuple-element.32) | copy-start | bytes 3076
  95.8 5.5 %copy-start.2 = (bf16[4,128,256]{2,1,0:T(8,128)(2,1)S(1)}, bf16[4,128,256]{2,1,0:T(8,128)(2,1)}, u32[]{:S(2)}) copy-start(bf16[4,128,256]{2,1,0:T(8,128)(2,1)} %window_slices.1) | copy-start | bytes 786436
  97.7 5.4 %collective-permute-start.20 = (bf16[198,256]{1,0:T(8,128)(2,1)S(1)}, bf16[198,256]{1,0:T(8,128)(2,1)S(1)}, u32[]{:S(2)}, u32[]{:S(2)}) collective-permute-start(bf16[198,256]{1,0:T(8,128)(2,1)S(1)} %get-tuple-element.75), channel_id=1, source_target_pairs={{0,8},{4,12},{8,0},{12,4},{16,24},{20,28},{24,16},{28,20},{1,9},{5... | collective-permute-start | bytes 304136 | tf_op jit(solution)/shard_map/ppermute | solution.py:96
  98.4 5.6 %collective-permute-start.21 = (bf16[198,256]{1,0:T(8,128)(2,1)S(1)}, bf16[198,256]{1,0:T(8,128)(2,1)S(1)}, u32[]{:S(2)}, u32[]{:S(2)}) collective-permute-start(bf16[198,256]{1,0:T(8,128)(2,1)S(1)} %get-tuple-element.75), channel_id=1, source_target_pairs={{0,16},{4,20},{8,24},{12,28},{16,0},{20,4},{24,8},{28,12},{1,17},{... | collective-permute-start | bytes 304136 | tf_op jit(solution)/shard_map/ppermute | solution.py:96
  99.5 5.6 %collective-permute-start.22 = (bf16[198,256]{1,0:T(8,128)(2,1)S(1)}, bf16[198,256]{1,0:T(8,128)(2,1)S(1)}, u32[]{:S(2)}, u32[]{:S(2)}) collective-permute-start(bf16[198,256]{1,0:T(8,128)(2,1)S(1)} %get-tuple-element.75), channel_id=1, source_target_pairs={{0,24},{4,28},{8,16},{12,20},{16,8},{20,12},{24,0},{28,4},{1,25},{... | collective-permute-start | bytes 304136 | tf_op jit(solution)/shard_map/ppermute | solution.py:96
  105.3 4.3 %collective-permute-start.23 = (f32[194,128]{1,0:T(8,128)S(1)}, f32[194,128]{1,0:T(8,128)S(1)}, u32[]{:S(2)}, u32[]{:S(2)}) collective-permute-start(f32[194,128]{1,0:T(8,128)S(1)} %pad_maximum_fusion.10), channel_id=1, source_target_pairs={{0,4},{4,0},{8,12},{12,8},{16,20},{20,16},{24,28},{28,24},{1,5},{5... | collective-permute-start | bytes 297992 | tf_op jit(solution)/shard_map/ppermute | solution.py:96
  105.8 9.1 %copy-start.18 = (bf16[4,48,128]{2,1,0:T(8,128)(2,1)}, bf16[4,48,128]{2,1,0:T(8,128)(2,1)S(1)}, u32[]{:S(2)}) copy-start(bf16[4,48,128]{2,1,0:T(8,128)(2,1)S(1)} %pad_maximum_fusion.11) | copy-start | bytes 147460
  105.8 6.4 %collective-permute-start.24 = (bf16[192,128]{1,0:T(8,128)(2,1)S(1)}, bf16[192,128]{1,0:T(8,128)(2,1)S(1)}, u32[]{:S(2)}, u32[]{:S(2)}) collective-permute-start(bf16[192,128]{1,0:T(8,128)(2,1)S(1)} %bitcast.75), channel_id=1, source_target_pairs={{0,1},{1,2},{2,3},{3,0},{4,5},{5,6},{6,7},{7,4},{8,9},{9,10},{10,1... | collective-permute-start | bytes 147464 | tf_op jit(solution)/shard_map/ppermute | solution.py:91
  106.6 5.6 %collective-permute-start.25 = (bf16[192,128]{1,0:T(8,128)(2,1)S(1)}, bf16[192,128]{1,0:T(8,128)(2,1)S(1)}, u32[]{:S(2)}, u32[]{:S(2)}) collective-permute-start(bf16[192,128]{1,0:T(8,128)(2,1)S(1)} %bitcast.76), channel_id=1, source_target_pairs={{0,3},{1,0},{2,1},{3,2},{4,7},{5,4},{6,5},{7,6},{8,11},{9,8},{10,9... | collective-permute-start | bytes 147464 | tf_op jit(solution)/shard_map/ppermute | solution.py:91
  109.7 5.2 %collective-permute-start.26 = (bf16[192,128]{1,0:T(8,128)(2,1)S(1)}, bf16[192,128]{1,0:T(8,128)(2,1)S(1)}, u32[]{:S(2)}, u32[]{:S(2)}) collective-permute-start(bf16[192,128]{1,0:T(8,128)(2,1)S(1)} %bitcast.77), channel_id=1, source_target_pairs={{0,2},{1,3},{2,0},{3,1},{4,6},{5,7},{6,4},{7,5},{8,10},{9,11},{10,... | collective-permute-start | bytes 147464 | tf_op jit(solution)/shard_map/ppermute | solution.py:91
  112.2 2.7 %copy-start.19 = (bf16[192,128]{1,0:T(8,128)(2,1)}, bf16[192,128]{1,0:T(8,128)(2,1)S(1)}, u32[]{:S(2)}) copy-start(bf16[192,128]{1,0:T(8,128)(2,1)S(1)} %collective-permute-done.24.refs_1_) | copy-start | bytes 147460
  112.2 2.7 %copy-start.20 = (bf16[192,128]{1,0:T(8,128)(2,1)}, bf16[192,128]{1,0:T(8,128)(2,1)S(1)}, u32[]{:S(2)}) copy-start(bf16[192,128]{1,0:T(8,128)(2,1)S(1)} %collective-permute-done.25.refs_2_) | copy-start | bytes 147460
  119.9 2.1 %collective-permute-start.27 = (bf16[64,4096]{1,0:T(8,128)(2,1)}, bf16[64,4096]{1,0:T(8,128)(2,1)S(1)}, u32[]{:S(2)}, u32[]{:S(2)}) collective-permute-start(bf16[64,4096]{1,0:T(8,128)(2,1)} %get-tuple-element.40), channel_id=1, source_target_pairs={{0,4},{4,0},{8,12},{12,8},{16,20},{20,16},{24,28},{28,24},{1,5},{5... | collective-permute-start | bytes 1572872 | tf_op jit(solution)/shard_map/ppermute | solution.py:96
  (7 other events, 5.2 us)

commit v4 on v3

--- a/solution.py
+++ b/solution.py
@@ -366,7 +366,8 @@
     mine = after(mine, fetched[-1], *sum(near, []))
     theirs = paired(mine, (1, 1))
 
-    own = [lax.dynamic_slice(images, (i * rows, batch * block), (rows, block)) for i in own_order]
+    later = after(images, mine)
+    own = [lax.dynamic_slice(later, (i * rows, batch * block), (rows, block)) for i in own_order]
     total, pixels = match(order, mine, theirs, [own])
     total = total[0]
     pixels = [pixels]
@@ -383,7 +384,8 @@
     def by_rows(blocks):
         return pick(blocks, chip_places(core))
 
-    noise = lax.dynamic_index_in_dim(noise_precision.reshape(chips, 2, rows), core, 1, False)
+    noise, prior = lax.optimization_barrier((noise_precision, prior, part))[:2]
+    noise = lax.dynamic_index_in_dim(noise.reshape(chips, 2, rows), core, 1, False)
     score = noise[:, :, None] * by_rows(total) + prior
     own_top = jnp.max(score, axis=2)
     shifted_exp = jnp.exp(score - own_top[:, :, None])
@@ -407,7 +409,7 @@
     chip_order = [i // 2 for i in own_order]
     places = list(zip(held_masks(slabs, 0), held_masks(slabs, 1)))
     places = [(even + core * (odd - even)) // 2 for even, odd in places]
-    both = pick(window_slices(order, tables, planes, classes, own_o), places)
+    both = pick(window_slices(order, after(tables, part), planes, classes, own_o), places)
     inserted = jnp.einsum("qzo,qno->nz", both, weights, preferred_element_type=f32).astype(bf16)
     inserted = pick(inserted.reshape(chips, rows, 2 * width), chip_order)
     inserted = inserted.reshape(count, 2 * width)

time: 126 us -> 124 us (0.984)
  waiting for transfers between devices: 39.6 us -> 37.5 us
    ppermute x9, waiting for transfers between devices: 19.3 us -> 16.5 us  [shifted(): lax.ppermute(value, axis, [(i, (i + step) % size) for i in range(size)])]
    dynamic_slice x3 -> x4, local copies, waits for them, and re-layouts: 4.27 us -> 6 us  [the longest x1 2.5 us: local(): lax.dynamic_slice(later, (i * rows, batch * block), (rows, block))]
    unnamed x55 -> x49, local copies, waits for them, and re-layouts: 6.32 us -> 4.79 us
  transfers between devices with their start and end apart: 28 -> 28, of which waited for: 13 -> 15; matrix products, arithmetic and copies ran while one was open for 3% -> 5% of each run, Pallas kernels for 17% -> 18%
where the time goes in v4:
time: 124 us; the launch traced here: 123 us
  starting transfers between devices  39.3 us (32%)
  waiting for transfers between devices  37.5 us (30%)
  Pallas kernels  28.7 us (23%)
  local copies, waits for them, and re-layouts  13.8 us (11%)
  other arithmetic  2.63 us (2%)
    ppermute x19, starting transfers between devices, paired(): lax.ppermute(value, 'slab', [(i, i ^ masks[i % 2]) for i in range(size)])  23.4 us
    ppermute x19, waiting for transfers between devices, paired(): lax.ppermute(value, 'slab', [(i, i ^ masks[i % 2]) for i in range(size)])  20.9 us
    ppermute x9, waiting for transfers between devices, shifted(): lax.ppermute(value, axis, [(i, (i + step) % size) for i in range(size)])  16.5 us
    ppermute x9, starting transfers between devices, shifted(): lax.ppermute(value, axis, [(i, (i + step) % size) for i in range(size)])  15.9 us
    pallas_call x4, Pallas kernels, match(): pl.pallas_call(match_kernel, in_specs=[pl.BlockSpec(memory_space=pltpu.SM...  15.1 us
    unnamed x49, local copies, waits for them, and re-layouts  4.79 us
    pallas_call x1, Pallas kernels, project(): pl.pallas_call(lambda *refs: project_kernel(planes, classes, own_o, depth...  4.7 us
    pallas_call x1, Pallas kernels, sum_images(): pl.pallas_call(sum_images_kernel, grid=(block // tile,), in_specs=[pl.Blo...  4.47 us
  transfers between devices with their start and end apart: 28, of which 15 were waited for; matrix products, arithmetic and copies ran while one was open for 5% of the time, Pallas kernels for 18%

profile of v4, /device:TPU:0, one launch (start us, length us, event | category | flops | bytes accessed | tf_op | source)
XLA Modules:
  0.0 123.4 jit_solution(13185916482078006612)
XLA Ops:
  0.7 2.3 %fusion.29 = (bf16[48,4096]{1,0:T(8,128)(2,1)}, bf16[48,4096]{1,0:T(8,128)(2,1)}, bf16[48,4096]{1,0:T(8,128)(2,1)S(1)}) fusion(bf16[384,16384]{1,0:T(8,128)(2,1)} %param.9, s32[]{:T(128)S(6)} %select_n.175, s32[]{:T(128)S(6)} %select_n.178, s32[]{:T(128)S(6)} %select_n.177, s32[]{:T(128)S(6)} %select_n.176), kind=kLoop, calls=%fused_computation.100 | loop fusion | bytes 2359312 | tf_op jit(solution)/shard_map/dynamic_slice | solution.py:330
  4.5 1.2 collective-permute-done
  5.8 2.9 %collective-permute-start.1 = (bf16[134,2048]{1,0:T(8,128)(2,1)S(1)}, bf16[134,2048]{1,0:T(8,128)(2,1)S(1)}, u32[]{:S(2)}, u32[]{:S(2)}) collective-permute-start(bf16[134,2048]{1,0:T(8,128)(2,1)S(1)} %pad_maximum_fusion.refs_1_), channel_id=1, source_target_pairs={{0,8},{4,20},{8,0},{12,28},{16,24},{20,4},{24,16},{28,12},{1,9},{5... | collective-permute-start | bytes 1646600 | tf_op jit(solution)/shard_map/ppermute | solution.py:96
  8.7 1.6 %collective-permute-start.2 = (bf16[48,4096]{1,0:T(8,128)(2,1)S(1)}, bf16[48,4096]{1,0:T(8,128)(2,1)S(1)}, u32[]{:S(2)}, u32[]{:S(2)}) collective-permute-start(bf16[48,4096]{1,0:T(8,128)(2,1)S(1)} %get-tuple-element.64), channel_id=1, source_target_pairs={{0,1},{1,2},{2,3},{3,0},{4,5},{5,6},{6,7},{7,4},{8,9},{9,10},{10,1... | collective-permute-start | bytes 1179656 | tf_op jit(solution)/shard_map/ppermute | solution.py:91
  10.3 1.5 %collective-permute-start.3 = (bf16[134,2048]{1,0:T(8,128)(2,1)S(1)}, bf16[134,2048]{1,0:T(8,128)(2,1)S(1)}, u32[]{:S(2)}, u32[]{:S(2)}) collective-permute-start(bf16[134,2048]{1,0:T(8,128)(2,1)S(1)} %pad_maximum_fusion.refs_1_), channel_id=1, source_target_pairs={{0,16},{4,12},{8,24},{12,4},{16,0},{20,28},{24,8},{28,20},{1,17},{... | collective-permute-start | bytes 1646600 | tf_op jit(solution)/shard_map/ppermute | solution.py:96
  11.8 9.7 %collective-permute-done.2.refs_0_ = bf16[48,4096]{1,0:T(8,128)(2,1)S(1)} collective-permute-done((bf16[48,4096]{1,0:T(8,128)(2,1)S(1)}, bf16[48,4096]{1,0:T(8,128)(2,1)S(1)}, u32[]{:S(2)}, u32[]{:S(2)}) %collective-permute-start.2) | collective-permute-done | bytes 393248 | tf_op jit(solution)/shard_map/ppermute | solution.py:91
  21.5 2.1 %collective-permute-start.4 = (bf16[134,2048]{1,0:T(8,128)(2,1)S(1)}, bf16[134,2048]{1,0:T(8,128)(2,1)S(1)}, u32[]{:S(2)}, u32[]{:S(2)}) collective-permute-start(bf16[134,2048]{1,0:T(8,128)(2,1)S(1)} %collective-permute-done.1.refs_2_), channel_id=1, source_target_pairs={{0,16},{4,12},{8,24},{12,4},{16,0},{20,28},{24,8},{28,20},{1,17},{... | collective-permute-start | bytes 1646600 | tf_op jit(solution)/shard_map/ppermute | solution.py:96
  23.6 3.6 %collective-permute-start.8 = (bf16[48,4096]{1,0:T(8,128)(2,1)}, bf16[48,4096]{1,0:T(8,128)(2,1)S(1)}, u32[]{:S(2)}, u32[]{:S(2)}) collective-permute-start(bf16[48,4096]{1,0:T(8,128)(2,1)} %get-tuple-element.63), channel_id=1, source_target_pairs={{0,3},{1,0},{2,1},{3,2},{4,7},{5,4},{6,5},{7,6},{8,11},{9,8},{10,9... | collective-permute-start | bytes 1179656 | tf_op jit(solution)/shard_map/ppermute | solution.py:91
  27.2 3.9 %collective-permute-done.4.refs_4_ = bf16[134,2048]{1,0:T(8,128)(2,1)S(1)} collective-permute-done((bf16[134,2048]{1,0:T(8,128)(2,1)S(1)}, bf16[134,2048]{1,0:T(8,128)(2,1)S(1)}, u32[]{:S(2)}, u32[]{:S(2)}) %collective-permute-start.4) | collective-permute-done | bytes 548896 | tf_op jit(solution)/shard_map/ppermute | solution.py:96
  31.1 1.5 %collective-permute-start.6 = (bf16[48,4096]{1,0:T(8,128)(2,1)S(1)}, bf16[48,4096]{1,0:T(8,128)(2,1)}, u32[]{:S(2)}, u32[]{:S(2)}) collective-permute-start(bf16[48,4096]{1,0:T(8,128)(2,1)S(1)} %collective-permute-done.2.refs_0_), channel_id=1, source_target_pairs={{0,8},{4,20},{8,0},{12,28},{16,24},{20,4},{24,16},{28,12},{1,9},{5... | collective-permute-start | bytes 1179656 | tf_op jit(solution)/shard_map/ppermute | solution.py:96
  32.6 2.2 %collective-permute-start.7 = (bf16[48,4096]{1,0:T(8,128)(2,1)S(1)}, bf16[48,4096]{1,0:T(8,128)(2,1)S(1)}, u32[]{:S(2)}, u32[]{:S(2)}) collective-permute-start(bf16[48,4096]{1,0:T(8,128)(2,1)S(1)} %collective-permute-done.2.refs_0_), channel_id=1, source_target_pairs={{0,16},{4,12},{8,24},{12,4},{16,0},{20,28},{24,8},{28,20},{1,17},{... | collective-permute-start | bytes 1179656 | tf_op jit(solution)/shard_map/ppermute | solution.py:96
  34.8 2.6 %collective-permute-start.5 = (bf16[48,4096]{1,0:T(8,128)(2,1)}, bf16[48,4096]{1,0:T(8,128)(2,1)S(1)}, u32[]{:S(2)}, u32[]{:S(2)}) collective-permute-start(bf16[48,4096]{1,0:T(8,128)(2,1)} %get-tuple-element.62), channel_id=1, source_target_pairs={{0,2},{1,3},{2,0},{3,1},{4,6},{5,7},{6,4},{7,5},{8,10},{9,11},{10,... | collective-permute-start | bytes 1179656 | tf_op jit(solution)/shard_map/ppermute | solution.py:91
  37.4 3.8 %collective-permute-done.6.refs_1_ = bf16[48,4096]{1,0:T(8,128)(2,1)} collective-permute-done((bf16[48,4096]{1,0:T(8,128)(2,1)S(1)}, bf16[48,4096]{1,0:T(8,128)(2,1)}, u32[]{:S(2)}, u32[]{:S(2)}) %collective-permute-start.6) | collective-permute-done | bytes 393248 | tf_op jit(solution)/shard_map/ppermute | solution.py:96
  41.2 0.8 copy-done.11
  41.9 1.5 %collective-permute-start.10 = (bf16[48,4096]{1,0:T(8,128)(2,1)S(1)}, bf16[48,4096]{1,0:T(8,128)(2,1)}, u32[]{:S(2)}, u32[]{:S(2)}) collective-permute-start(bf16[48,4096]{1,0:T(8,128)(2,1)S(1)} %collective-permute-done.8.refs_0_), channel_id=1, source_target_pairs={{0,16},{4,12},{8,24},{12,4},{16,0},{20,28},{24,8},{28,20},{1,17},{... | collective-permute-start | bytes 1179656 | tf_op jit(solution)/shard_map/ppermute | solution.py:96
  43.4 1.7 %collective-permute-start.9 = (bf16[48,4096]{1,0:T(8,128)(2,1)S(1)}, bf16[48,4096]{1,0:T(8,128)(2,1)}, u32[]{:S(2)}, u32[]{:S(2)}) collective-permute-start(bf16[48,4096]{1,0:T(8,128)(2,1)S(1)} %collective-permute-done.8.refs_0_), channel_id=1, source_target_pairs={{0,8},{4,20},{8,0},{12,28},{16,24},{20,4},{24,16},{28,12},{1,9},{5... | collective-permute-start | bytes 1179656 | tf_op jit(solution)/shard_map/ppermute | solution.py:96
  45.8 4.7 %project.1 = (bf16[2064,256]{1,0:T(8,128)(2,1)}, f32[1,256]{1,0:T(1,128)}, f32[8,37,128]{2,1,0:T(8,128)}) custom-call(s32[4]{0:T(128)} %pad_add_fusion.refs_0_.order_ref, bf16[134,2048]{1,0:T(8,128)(2,1)} %copy-done.1, bf16[134,2048]{1,0:T(8,128)(2,1)} %copy-done.3, bf16[134,2048]{1,0:T(8,128)(2,1)} %copy-done.4, bf16[134,2048]{1,0:T(8,128)(2,1)} %copy-done.5), custom_call_target="tpu_custom_call" | custom-call | flops 536870912 | bytes 2195456 | tf_op jit(solution)/shard_map/project/pallas_call | solution.py:253
  50.5 1.3 %collective-permute-done.5.refs_0_ = bf16[48,4096]{1,0:T(8,128)(2,1)S(1)} collective-permute-done((bf16[48,4096]{1,0:T(8,128)(2,1)}, bf16[48,4096]{1,0:T(8,128)(2,1)S(1)}, u32[]{:S(2)}, u32[]{:S(2)}) %collective-permute-start.5) | collective-permute-done | bytes 393248 | tf_op jit(solution)/shard_map/ppermute | solution.py:91
  52.3 0.8 collective-permute-start.12
  53.0 0.9 collective-permute-start.15
  54.0 1.1 collective-permute-start.17
  55.1 0.9 collective-permute-start.13
  56.0 7.5 %collective-permute-done.12.refs_1_ = bf16[48,4096]{1,0:T(8,128)(2,1)S(1)} collective-permute-done((bf16[48,4096]{1,0:T(8,128)(2,1)S(1)}, bf16[48,4096]{1,0:T(8,128)(2,1)S(1)}, u32[]{:S(2)}, u32[]{:S(2)}) %collective-permute-start.12) | collective-permute-done | bytes 393248 | tf_op jit(solution)/shard_map/ppermute | solution.py:96
  63.5 2.1 %collective-permute-start.14 = (bf16[48,4096]{1,0:T(8,128)(2,1)S(1)}, bf16[48,4096]{1,0:T(8,128)(2,1)S(1)}, u32[]{:S(2)}, u32[]{:S(2)}) collective-permute-start(bf16[48,4096]{1,0:T(8,128)(2,1)S(1)} %collective-permute-done.12.refs_1_), channel_id=1, source_target_pairs={{0,16},{4,12},{8,24},{12,4},{16,0},{20,28},{24,8},{28,20},{1,17},{... | collective-permute-start | bytes 1179656 | tf_op jit(solution)/shard_map/ppermute | solution.py:96
  65.6 1.0 copy-done
  66.7 3.8 %match.6 = (f32[1,192,256]{2,1,0:T(8,128)}, bf16[192,4096]{1,0:T(8,128)(2,1)}) custom-call(s32[4]{0:T(128)} %pad_add_fusion.refs_0_.order_ref, bf16[2064,256]{1,0:T(8,128)(2,1)} %get-tuple-element.32.mine_ref, bf16[2064,256]{1,0:T(8,128)(2,1)} %copy-done, bf16[48,4096]{1,0:T(8,128)(2,1)} %copy-done.8, bf16[48,4096]{1,0:T(8,128)(2,1)} %collective-permute-done.6.refs_1_, ...), custom_call_target="tpu_custom_call" | custom-call | flops 402653184 | bytes 3686400 | tf_op jit(solution)/shard_map/match/pallas_call | solution.py:290
  70.5 2.8 %collective-permute-start.16 = (f32[192,256]{1,0:T(8,128)}, f32[192,256]{1,0:T(8,128)S(1)}, u32[]{:S(2)}, u32[]{:S(2)}) collective-permute-start(f32[192,256]{1,0:T(8,128)} %bitcast.89), channel_id=1, source_target_pairs={{0,3},{1,0},{2,1},{3,2},{4,7},{5,4},{6,5},{7,6},{8,11},{9,8},{10,9... | collective-permute-start | bytes 589832 | tf_op jit(solution)/shard_map/ppermute | solution.py:91
  73.3 3.8 %match.7 = (f32[1,192,256]{2,1,0:T(8,128)}, bf16[192,4096]{1,0:T(8,128)(2,1)}) custom-call(s32[4]{0:T(128)} %pad_add_fusion.refs_0_.order_ref, bf16[2064,256]{1,0:T(8,128)(2,1)} %get-tuple-element.32.mine_ref, bf16[2064,256]{1,0:T(8,128)(2,1)} %copy-done, bf16[48,4096]{1,0:T(8,128)(2,1)} %copy-done.9, bf16[48,4096]{1,0:T(8,128)(2,1)} %collective-permute-done.9.refs_1_, ...), custom_call_target="tpu_custom_call" | custom-call | flops 402653184 | bytes 3686400 | tf_op jit(solution)/shard_map/match/pallas_call | solution.py:290
  77.9 0.8 copy-done.14
  78.6 3.7 %match.4 = (f32[1,192,256]{2,1,0:T(8,128)}, bf16[192,4096]{1,0:T(8,128)(2,1)}) custom-call(s32[4]{0:T(128)} %pad_add_fusion.refs_0_.order_ref, bf16[2064,256]{1,0:T(8,128)(2,1)} %get-tuple-element.32.mine_ref, bf16[2064,256]{1,0:T(8,128)(2,1)} %copy-done, bf16[48,4096]{1,0:T(8,128)(2,1)} %copy-done.10, bf16[48,4096]{1,0:T(8,128)(2,1)} %copy-done.12, ...), custom_call_target="tpu_custom_call" | custom-call | flops 402653184 | bytes 3686400 | tf_op jit(solution)/shard_map/match/pallas_call | solution.py:290
  82.4 1.2 collective-permute-start.19
  83.5 2.5 %fusion.28 = (bf16[48,4096]{1,0:T(8,128)(2,1)}, bf16[48,4096]{1,0:T(8,128)(2,1)}, bf16[48,4096]{1,0:T(8,128)(2,1)}, bf16[48,4096]{1,0:T(8,128)(2,1)}) fusion(bf16[384,16384]{1,0:T(8,128)(2,1)} %param.9, s32[]{:T(128)S(6)} %select_n.186, s32[]{:T(128)S(6)} %select_n.183, s32[]{:T(128)S(6)} %select_n.185, s32[]{:T(128)S(6)} %select_n.184, s32[]{:T(128)S(6)} %select_n.175), kind=kLoop, calls=%fused_computation.99 | loop fusion | bytes 3145748 | tf_op jit(solution)/shard_map/dynamic_slice | solution.py:370
  87.4 2.0 %window_slices.1 = bf16[4,128,256]{2,1,0:T(8,128)(2,1)} custom-call(s32[4]{0:T(128)} %pad_add_fusion.refs_0_.order_ref, f32[8,37,128]{2,1,0:T(8,128)} %get-tuple-element.41.refs_1_), custom_call_target="tpu_custom_call" | custom-call | bytes 151552 | tf_op jit(solution)/shard_map/window_slices/pallas_call | solution.py:78
  89.4 3.8 %match.5 = (f32[1,192,256]{2,1,0:T(8,128)}, bf16[192,4096]{1,0:T(8,128)(2,1)}) custom-call(s32[4]{0:T(128)} %pad_add_fusion.refs_0_.order_ref, bf16[2064,256]{1,0:T(8,128)(2,1)} %get-tuple-element.32.mine_ref, bf16[2064,256]{1,0:T(8,128)(2,1)} %copy-done, bf16[48,4096]{1,0:T(8,128)(2,1)} %get-tuple-element.61.refs_0_, ...), custom_call_target="tpu_custom_call" | custom-call | flops 402653184 | bytes 3686400 | tf_op jit(solution)/shard_map/match/pallas_call | solution.py:290
  93.5 1.0 fusion.13
  96.1 1.0 collective-permute-start.21
  97.1 1.8 %collective-permute-start.22 = (bf16[198,256]{1,0:T(8,128)(2,1)S(1)}, bf16[198,256]{1,0:T(8,128)(2,1)S(1)}, u32[]{:S(2)}, u32[]{:S(2)}) collective-permute-start(bf16[198,256]{1,0:T(8,128)(2,1)S(1)} %get-tuple-element.83), channel_id=1, source_target_pairs={{0,24},{4,28},{8,16},{12,20},{16,8},{20,12},{24,0},{28,4},{1,25},{... | collective-permute-start | bytes 304136 | tf_op jit(solution)/shard_map/ppermute | solution.py:96
  99.0 2.1 %collective-permute-done.20 = bf16[198,256]{1,0:T(8,128)(2,1)S(1)} collective-permute-done((bf16[198,256]{1,0:T(8,128)(2,1)S(1)}, bf16[198,256]{1,0:T(8,128)(2,1)S(1)}, u32[]{:S(2)}, u32[]{:S(2)}) %collective-permute-start.20) | collective-permute-done | bytes 101408 | tf_op jit(solution)/shard_map/ppermute | solution.py:96
  101.4 1.3 %collective-permute-done.22 = bf16[198,256]{1,0:T(8,128)(2,1)S(1)} collective-permute-done((bf16[198,256]{1,0:T(8,128)(2,1)S(1)}, bf16[198,256]{1,0:T(8,128)(2,1)S(1)}, u32[]{:S(2)}, u32[]{:S(2)}) %collective-permute-start.22) | collective-permute-done | bytes 101408 | tf_op jit(solution)/shard_map/ppermute | solution.py:96
  103.4 2.4 %collective-permute-start.24 = (bf16[192,128]{1,0:T(8,128)(2,1)S(1)}, bf16[192,128]{1,0:T(8,128)(2,1)S(1)}, u32[]{:S(2)}, u32[]{:S(2)}) collective-permute-start(bf16[192,128]{1,0:T(8,128)(2,1)S(1)} %bitcast.75), channel_id=1, source_target_pairs={{0,1},{1,2},{2,3},{3,0},{4,5},{5,6},{6,7},{7,4},{8,9},{9,10},{10,1... | collective-permute-start | bytes 147464 | tf_op jit(solution)/shard_map/ppermute | solution.py:91
  105.8 1.5 %collective-permute-start.25 = (bf16[192,128]{1,0:T(8,128)(2,1)S(1)}, bf16[192,128]{1,0:T(8,128)(2,1)S(1)}, u32[]{:S(2)}, u32[]{:S(2)}) collective-permute-start(bf16[192,128]{1,0:T(8,128)(2,1)S(1)} %bitcast.76), channel_id=1, source_target_pairs={{0,3},{1,0},{2,1},{3,2},{4,7},{5,4},{6,5},{7,6},{8,11},{9,8},{10,9... | collective-permute-start | bytes 147464 | tf_op jit(solution)/shard_map/ppermute | solution.py:91
  107.5 2.0 %collective-permute-done.24.refs_1_ = bf16[192,128]{1,0:T(8,128)(2,1)S(1)} collective-permute-done((bf16[192,128]{1,0:T(8,128)(2,1)S(1)}, bf16[192,128]{1,0:T(8,128)(2,1)S(1)}, u32[]{:S(2)}, u32[]{:S(2)}) %collective-permute-start.24) | collective-permute-done | bytes 49184 | tf_op jit(solution)/shard_map/ppermute | solution.py:91
  109.5 1.0 collective-permute-done.25.refs_2_
  110.5 2.3 %collective-permute-done.26.refs_3_ = bf16[192,128]{1,0:T(8,128)(2,1)S(1)} collective-permute-done((bf16[192,128]{1,0:T(8,128)(2,1)S(1)}, bf16[192,128]{1,0:T(8,128)(2,1)S(1)}, u32[]{:S(2)}, u32[]{:S(2)}) %collective-permute-start.26) | collective-permute-done | bytes 49184 | tf_op jit(solution)/shard_map/ppermute | solution.py:91
  113.5 4.5 %sum_images.1 = (f32[64,4096]{1,0:T(8,128)}, bf16[64,4096]{1,0:T(8,128)(2,1)}) custom-call(bf16[192,128]{1,0:T(8,128)(2,1)} %bitcast.78, bf16[192,128]{1,0:T(8,128)(2,1)} %copy-done.16, bf16[192,128]{1,0:T(8,128)(2,1)} %copy-done.17, bf16[192,128]{1,0:T(8,128)(2,1)} %copy-done.18, bf16[192,4096]{1,0:T(8,128)(2,1)} %get-tuple-element.43.refs_4_, ...), custom_call_target="tpu_custom_call" | custom-call | flops 805306368 | bytes 6488064 | tf_op jit(solution)/shard_map/sum_images/pallas_call | solution.py:170
  118.8 0.8 copy.27
  120.0 0.8 copy-done.6
  120.9 2.5 %add_parts.1 = f32[32,2,4096]{2,1,0:T(2,128)} custom-call(f32[64,4096]{1,0:T(8,128)} %get-tuple-element.47.one_ref, bf16[64,4096]{1,0:T(8,128)(2,1)} %copy-done.6), custom_call_target="tpu_custom_call" | custom-call | flops 524288 | bytes 2621440 | tf_op jit(solution)/shard_map/add_parts/pallas_call | solution.py:192
  (124 shorter events, 9.8 us)
Async XLA Ops:
  0.7 2.4 %copy-start.7 = (bf16[32,2,4096]{2,1,0:T(2,128)(2,1)S(1)}, bf16[32,2,4096]{2,1,0:T(2,128)(2,1)}, u32[]{:S(2)}) copy-start(bf16[32,2,4096]{2,1,0:T(2,128)(2,1)} %param.6) | copy-start | bytes 1572868
  0.7 2.6 %copy-start.22 = (f32[2,64]{1,0:T(2,128)S(1)}, f32[2,64]{1,0:T(2,128)}, u32[]{:S(2)}) copy-start(f32[2,64]{1,0:T(2,128)} %param.11) | copy-start | bytes 1540
  0.7 2.8 %copy-start.23 = (s32[2,64]{1,0:T(2,128)S(1)}, s32[2,64]{1,0:T(2,128)}, u32[]{:S(2)}) copy-start(s32[2,64]{1,0:T(2,128)} %param.8) | copy-start | bytes 1540
  0.7 3.0 %copy-start.20 = (bf16[2,64,32]{1,2,0:T(8,128)(2,1)S(1)}, bf16[2,64,32]{1,2,0:T(8,128)(2,1)}, u32[]{:S(2)}) copy-start(bf16[2,64,32]{1,2,0:T(8,128)(2,1)} %param.7) | copy-start | bytes 24580
  4.0 1.7 %collective-permute-start = (bf16[67,2048]{1,0:T(8,128)(2,1)S(1)}, bf16[67,2048]{1,0:T(8,128)(2,1)S(1)}, u32[]{:S(2)}, u32[]{:S(2)}) collective-permute-start(bf16[67,2048]{1,0:T(8,128)(2,1)S(1)} %pad_maximum_fusion.7), channel_id=1, source_target_pairs={{0,4},{4,0},{8,12},{12,8},{16,20},{20,16},{24,28},{28,24},{1,5},{5... | collective-permute-start | bytes 823304 | tf_op jit(solution)/shard_map/ppermute | solution.py:96
  5.8 40.0 %copy-start.1 = (bf16[134,2048]{1,0:T(8,128)(2,1)}, bf16[134,2048]{1,0:T(8,128)(2,1)S(1)}, u32[]{:S(2)}) copy-start(bf16[134,2048]{1,0:T(8,128)(2,1)S(1)} %pad_maximum_fusion.refs_1_) | copy-start | bytes 1646596
  5.8 15.7 %collective-permute-start.1 = (bf16[134,2048]{1,0:T(8,128)(2,1)S(1)}, bf16[134,2048]{1,0:T(8,128)(2,1)S(1)}, u32[]{:S(2)}, u32[]{:S(2)}) collective-permute-start(bf16[134,2048]{1,0:T(8,128)(2,1)S(1)} %pad_maximum_fusion.refs_1_), channel_id=1, source_target_pairs={{0,8},{4,20},{8,0},{12,28},{16,24},{20,4},{24,16},{28,12},{1,9},{5... | collective-permute-start | bytes 1646600 | tf_op jit(solution)/shard_map/ppermute | solution.py:96
  8.7 12.8 %collective-permute-start.2 = (bf16[48,4096]{1,0:T(8,128)(2,1)S(1)}, bf16[48,4096]{1,0:T(8,128)(2,1)S(1)}, u32[]{:S(2)}, u32[]{:S(2)}) collective-permute-start(bf16[48,4096]{1,0:T(8,128)(2,1)S(1)} %get-tuple-element.64), channel_id=1, source_target_pairs={{0,1},{1,2},{2,3},{3,0},{4,5},{5,6},{6,7},{7,4},{8,9},{9,10},{10,1... | collective-permute-start | bytes 1179656 | tf_op jit(solution)/shard_map/ppermute | solution.py:91
  10.3 17.0 %collective-permute-start.3 = (bf16[134,2048]{1,0:T(8,128)(2,1)S(1)}, bf16[134,2048]{1,0:T(8,128)(2,1)S(1)}, u32[]{:S(2)}, u32[]{:S(2)}) collective-permute-start(bf16[134,2048]{1,0:T(8,128)(2,1)S(1)} %pad_maximum_fusion.refs_1_), channel_id=1, source_target_pairs={{0,16},{4,12},{8,24},{12,4},{16,0},{20,28},{24,8},{28,20},{1,17},{... | collective-permute-start | bytes 1646600 | tf_op jit(solution)/shard_map/ppermute | solution.py:96
  21.5 44.1 %copy-start.8 = (bf16[48,4096]{1,0:T(8,128)(2,1)}, bf16[48,4096]{1,0:T(8,128)(2,1)S(1)}, u32[]{:S(2)}) copy-start(bf16[48,4096]{1,0:T(8,128)(2,1)S(1)} %collective-permute-done.2.refs_0_) | copy-start | bytes 1179652
  21.5 24.3 %copy-start.3 = (bf16[134,2048]{1,0:T(8,128)(2,1)}, bf16[134,2048]{1,0:T(8,128)(2,1)S(1)}, u32[]{:S(2)}) copy-start(bf16[134,2048]{1,0:T(8,128)(2,1)S(1)} %collective-permute-done.1.refs_2_) | copy-start | bytes 1646596
  21.5 9.6 %collective-permute-start.4 = (bf16[134,2048]{1,0:T(8,128)(2,1)S(1)}, bf16[134,2048]{1,0:T(8,128)(2,1)S(1)}, u32[]{:S(2)}, u32[]{:S(2)}) collective-permute-start(bf16[134,2048]{1,0:T(8,128)(2,1)S(1)} %collective-permute-done.1.refs_2_), channel_id=1, source_target_pairs={{0,16},{4,12},{8,24},{12,4},{16,0},{20,28},{24,8},{28,20},{1,17},{... | collective-permute-start | bytes 1646600 | tf_op jit(solution)/shard_map/ppermute | solution.py:96
  23.6 13.8 %collective-permute-start.8 = (bf16[48,4096]{1,0:T(8,128)(2,1)}, bf16[48,4096]{1,0:T(8,128)(2,1)S(1)}, u32[]{:S(2)}, u32[]{:S(2)}) collective-permute-start(bf16[48,4096]{1,0:T(8,128)(2,1)} %get-tuple-element.63), channel_id=1, source_target_pairs={{0,3},{1,0},{2,1},{3,2},{4,7},{5,4},{6,5},{7,6},{8,11},{9,8},{10,9... | collective-permute-start | bytes 1179656 | tf_op jit(solution)/shard_map/ppermute | solution.py:91
  27.2 18.6 %copy-start.4 = (bf16[134,2048]{1,0:T(8,128)(2,1)}, bf16[134,2048]{1,0:T(8,128)(2,1)S(1)}, u32[]{:S(2)}) copy-start(bf16[134,2048]{1,0:T(8,128)(2,1)S(1)} %collective-permute-done.3.refs_3_) | copy-start | bytes 1646596
  31.1 14.7 %copy-start.5 = (bf16[134,2048]{1,0:T(8,128)(2,1)}, bf16[134,2048]{1,0:T(8,128)(2,1)S(1)}, u32[]{:S(2)}) copy-start(bf16[134,2048]{1,0:T(8,128)(2,1)S(1)} %collective-permute-done.4.refs_4_) | copy-start | bytes 1646596
  31.1 10.1 %collective-permute-start.6 = (bf16[48,4096]{1,0:T(8,128)(2,1)S(1)}, bf16[48,4096]{1,0:T(8,128)(2,1)}, u32[]{:S(2)}, u32[]{:S(2)}) collective-permute-start(bf16[48,4096]{1,0:T(8,128)(2,1)S(1)} %collective-permute-done.2.refs_0_), channel_id=1, source_target_pairs={{0,8},{4,20},{8,0},{12,28},{16,24},{20,4},{24,16},{28,12},{1,9},{5... | collective-permute-start | bytes 1179656 | tf_op jit(solution)/shard_map/ppermute | solution.py:96
  32.6 8.6 %collective-permute-start.7 = (bf16[48,4096]{1,0:T(8,128)(2,1)S(1)}, bf16[48,4096]{1,0:T(8,128)(2,1)S(1)}, u32[]{:S(2)}, u32[]{:S(2)}) collective-permute-start(bf16[48,4096]{1,0:T(8,128)(2,1)S(1)} %collective-permute-done.2.refs_0_), channel_id=1, source_target_pairs={{0,16},{4,12},{8,24},{12,4},{16,0},{20,28},{24,8},{28,20},{1,17},{... | collective-permute-start | bytes 1179656 | tf_op jit(solution)/shard_map/ppermute | solution.py:96
  34.8 17.1 %collective-permute-start.5 = (bf16[48,4096]{1,0:T(8,128)(2,1)}, bf16[48,4096]{1,0:T(8,128)(2,1)S(1)}, u32[]{:S(2)}, u32[]{:S(2)}) collective-permute-start(bf16[48,4096]{1,0:T(8,128)(2,1)} %get-tuple-element.62), channel_id=1, source_target_pairs={{0,2},{1,3},{2,0},{3,1},{4,6},{5,7},{6,4},{7,5},{8,10},{9,11},{10,... | collective-permute-start | bytes 1179656 | tf_op jit(solution)/shard_map/ppermute | solution.py:91
  37.4 13.2 %copy-start.9 = (bf16[48,4096]{1,0:T(8,128)(2,1)}, bf16[48,4096]{1,0:T(8,128)(2,1)S(1)}, u32[]{:S(2)}) copy-start(bf16[48,4096]{1,0:T(8,128)(2,1)S(1)} %collective-permute-done.8.refs_0_) | copy-start | bytes 1179652
  41.9 10.3 %collective-permute-start.10 = (bf16[48,4096]{1,0:T(8,128)(2,1)S(1)}, bf16[48,4096]{1,0:T(8,128)(2,1)}, u32[]{:S(2)}, u32[]{:S(2)}) collective-permute-start(bf16[48,4096]{1,0:T(8,128)(2,1)S(1)} %collective-permute-done.8.refs_0_), channel_id=1, source_target_pairs={{0,16},{4,12},{8,24},{12,4},{16,0},{20,28},{24,8},{28,20},{1,17},{... | collective-permute-start | bytes 1179656 | tf_op jit(solution)/shard_map/ppermute | solution.py:96
  43.4 8.9 %collective-permute-start.9 = (bf16[48,4096]{1,0:T(8,128)(2,1)S(1)}, bf16[48,4096]{1,0:T(8,128)(2,1)}, u32[]{:S(2)}, u32[]{:S(2)}) collective-permute-start(bf16[48,4096]{1,0:T(8,128)(2,1)S(1)} %collective-permute-done.8.refs_0_), channel_id=1, source_target_pairs={{0,8},{4,20},{8,0},{12,28},{16,24},{20,4},{24,16},{28,12},{1,9},{5... | collective-permute-start | bytes 1179656 | tf_op jit(solution)/shard_map/ppermute | solution.py:96
  51.8 25.2 %copy-start.10 = (bf16[48,4096]{1,0:T(8,128)(2,1)}, bf16[48,4096]{1,0:T(8,128)(2,1)S(1)}, u32[]{:S(2)}) copy-start(bf16[48,4096]{1,0:T(8,128)(2,1)S(1)} %collective-permute-done.5.refs_0_) | copy-start | bytes 1179652
  52.3 13.3 %collective-permute-start.11 = (bf16[2064,256]{1,0:T(8,128)(2,1)}, bf16[2064,256]{1,0:T(8,128)(2,1)S(1)}, u32[]{:S(2)}, u32[]{:S(2)}) collective-permute-start(bf16[2064,256]{1,0:T(8,128)(2,1)} %get-tuple-element.32.mine_ref), channel_id=1, source_target_pairs={{0,4},{4,0},{8,12},{12,8},{16,20},{20,16},{24,28},{28,24},{1,5},{5... | collective-permute-start | bytes 3170312 | tf_op jit(solution)/shard_map/ppermute | solution.py:96
  52.3 11.2 %collective-permute-start.12 = (bf16[48,4096]{1,0:T(8,128)(2,1)S(1)}, bf16[48,4096]{1,0:T(8,128)(2,1)S(1)}, u32[]{:S(2)}, u32[]{:S(2)}) collective-permute-start(bf16[48,4096]{1,0:T(8,128)(2,1)S(1)} %collective-permute-done.5.refs_0_), channel_id=1, source_target_pairs={{0,8},{4,20},{8,0},{12,28},{16,24},{20,4},{24,16},{28,12},{1,9},{5... | collective-permute-start | bytes 1179656 | tf_op jit(solution)/shard_map/ppermute | solution.py:96
  53.0 12.6 %collective-permute-start.15 = (bf16[48,4096]{1,0:T(8,128)(2,1)}, bf16[48,4096]{1,0:T(8,128)(2,1)}, u32[]{:S(2)}, u32[]{:S(2)}) collective-permute-start(bf16[48,4096]{1,0:T(8,128)(2,1)} %collective-permute-done.6.refs_1_), channel_id=1, source_target_pairs={{0,16},{4,12},{8,24},{12,4},{16,0},{20,28},{24,8},{28,20},{1,17},{... | collective-permute-start | bytes 1179656 | tf_op jit(solution)/shard_map/ppermute | solution.py:96
  54.0 19.3 %collective-permute-start.17 = (bf16[48,4096]{1,0:T(8,128)(2,1)}, bf16[48,4096]{1,0:T(8,128)(2,1)}, u32[]{:S(2)}, u32[]{:S(2)}) collective-permute-start(bf16[48,4096]{1,0:T(8,128)(2,1)} %collective-permute-done.9.refs_1_), channel_id=1, source_target_pairs={{0,16},{4,12},{8,24},{12,4},{16,0},{20,28},{24,8},{28,20},{1,17},{... | collective-permute-start | bytes 1179656 | tf_op jit(solution)/shard_map/ppermute | solution.py:96
  55.1 22.0 %collective-permute-start.13 = (bf16[48,4096]{1,0:T(8,128)(2,1)S(1)}, bf16[48,4096]{1,0:T(8,128)(2,1)S(1)}, u32[]{:S(2)}, u32[]{:S(2)}) collective-permute-start(bf16[48,4096]{1,0:T(8,128)(2,1)S(1)} %collective-permute-done.5.refs_0_), channel_id=1, source_target_pairs={{0,16},{4,12},{8,24},{12,4},{16,0},{20,28},{24,8},{28,20},{1,17},{... | collective-permute-start | bytes 1179656 | tf_op jit(solution)/shard_map/ppermute | solution.py:96
  63.5 13.5 %copy-start.12 = (bf16[48,4096]{1,0:T(8,128)(2,1)}, bf16[48,4096]{1,0:T(8,128)(2,1)S(1)}, u32[]{:S(2)}) copy-start(bf16[48,4096]{1,0:T(8,128)(2,1)S(1)} %collective-permute-done.12.refs_1_) | copy-start | bytes 1179652
  63.5 13.6 %collective-permute-start.14 = (bf16[48,4096]{1,0:T(8,128)(2,1)S(1)}, bf16[48,4096]{1,0:T(8,128)(2,1)S(1)}, u32[]{:S(2)}, u32[]{:S(2)}) collective-permute-start(bf16[48,4096]{1,0:T(8,128)(2,1)S(1)} %collective-permute-done.12.refs_1_), channel_id=1, source_target_pairs={{0,16},{4,12},{8,24},{12,4},{16,0},{20,28},{24,8},{28,20},{1,17},{... | collective-permute-start | bytes 1179656 | tf_op jit(solution)/shard_map/ppermute | solution.py:96
  65.6 1.1 copy-start
  70.5 22.7 %collective-permute-start.16 = (f32[192,256]{1,0:T(8,128)}, f32[192,256]{1,0:T(8,128)S(1)}, u32[]{:S(2)}, u32[]{:S(2)}) collective-permute-start(f32[192,256]{1,0:T(8,128)} %bitcast.89), channel_id=1, source_target_pairs={{0,3},{1,0},{2,1},{3,2},{4,7},{5,4},{6,5},{7,6},{8,11},{9,8},{10,9... | collective-permute-start | bytes 589832 | tf_op jit(solution)/shard_map/ppermute | solution.py:91
  77.0 16.1 %collective-permute-start.18 = (f32[192,256]{1,0:T(8,128)}, f32[192,256]{1,0:T(8,128)S(1)}, u32[]{:S(2)}, u32[]{:S(2)}) collective-permute-start(f32[192,256]{1,0:T(8,128)} %bitcast.90), channel_id=1, source_target_pairs={{0,1},{1,2},{2,3},{3,0},{4,5},{5,6},{6,7},{7,4},{8,9},{9,10},{10,1... | collective-permute-start | bytes 589832 | tf_op jit(solution)/shard_map/ppermute | solution.py:91
  82.4 3.7 %copy-start.21 = (f32[384]{0:T(512)S(1)}, f32[384]{0:T(512)}, u32[]{:S(2)}) copy-start(f32[384]{0:T(512)} %param.10) | copy-start | bytes 4612
  82.4 11.1 %collective-permute-start.19 = (f32[192,256]{1,0:T(8,128)}, f32[192,256]{1,0:T(8,128)S(1)}, u32[]{:S(2)}, u32[]{:S(2)}) collective-permute-start(f32[192,256]{1,0:T(8,128)} %bitcast.91), channel_id=1, source_target_pairs={{0,2},{1,3},{2,0},{3,1},{4,6},{5,7},{6,4},{7,5},{8,10},{9,11},{10,... | collective-permute-start | bytes 589832 | tf_op jit(solution)/shard_map/ppermute | solution.py:91
  93.2 1.4 %copy-start.19 = (f32[1,256]{1,0:T(1,128)S(1)}, f32[1,256]{1,0:T(1,128)}, u32[]{:S(2)}) copy-start(f32[1,256]{1,0:T(1,128)} %get-tuple-element.39) | copy-start | bytes 3076
  93.5 5.5 %copy-start.2 = (bf16[4,128,256]{2,1,0:T(8,128)(2,1)S(1)}, bf16[4,128,256]{2,1,0:T(8,128)(2,1)}, u32[]{:S(2)}) copy-start(bf16[4,128,256]{2,1,0:T(8,128)(2,1)} %window_slices.1) | copy-start | bytes 786436
  95.4 5.6 %collective-permute-start.20 = (bf16[198,256]{1,0:T(8,128)(2,1)S(1)}, bf16[198,256]{1,0:T(8,128)(2,1)S(1)}, u32[]{:S(2)}, u32[]{:S(2)}) collective-permute-start(bf16[198,256]{1,0:T(8,128)(2,1)S(1)} %get-tuple-element.83), channel_id=1, source_target_pairs={{0,8},{4,12},{8,0},{12,4},{16,24},{20,28},{24,16},{28,20},{1,9},{5... | collective-permute-start | bytes 304136 | tf_op jit(solution)/shard_map/ppermute | solution.py:96
  96.1 5.3 %collective-permute-start.21 = (bf16[198,256]{1,0:T(8,128)(2,1)S(1)}, bf16[198,256]{1,0:T(8,128)(2,1)S(1)}, u32[]{:S(2)}, u32[]{:S(2)}) collective-permute-start(bf16[198,256]{1,0:T(8,128)(2,1)S(1)} %get-tuple-element.83), channel_id=1, source_target_pairs={{0,16},{4,20},{8,24},{12,28},{16,0},{20,4},{24,8},{28,12},{1,17},{... | collective-permute-start | bytes 304136 | tf_op jit(solution)/shard_map/ppermute | solution.py:96
  97.1 5.6 %collective-permute-start.22 = (bf16[198,256]{1,0:T(8,128)(2,1)S(1)}, bf16[198,256]{1,0:T(8,128)(2,1)S(1)}, u32[]{:S(2)}, u32[]{:S(2)}) collective-permute-start(bf16[198,256]{1,0:T(8,128)(2,1)S(1)} %get-tuple-element.83), channel_id=1, source_target_pairs={{0,24},{4,28},{8,16},{12,20},{16,8},{20,12},{24,0},{28,4},{1,25},{... | collective-permute-start | bytes 304136 | tf_op jit(solution)/shard_map/ppermute | solution.py:96
  103.0 4.5 %collective-permute-start.23 = (f32[194,128]{1,0:T(8,128)S(1)}, f32[194,128]{1,0:T(8,128)S(1)}, u32[]{:S(2)}, u32[]{:S(2)}) collective-permute-start(f32[194,128]{1,0:T(8,128)S(1)} %pad_maximum_fusion.10), channel_id=1, source_target_pairs={{0,4},{4,0},{8,12},{12,8},{16,20},{20,16},{24,28},{28,24},{1,5},{5... | collective-permute-start | bytes 297992 | tf_op jit(solution)/shard_map/ppermute | solution.py:96
  103.4 9.4 %copy-start.15 = (bf16[4,48,128]{2,1,0:T(8,128)(2,1)}, bf16[4,48,128]{2,1,0:T(8,128)(2,1)S(1)}, u32[]{:S(2)}) copy-start(bf16[4,48,128]{2,1,0:T(8,128)(2,1)S(1)} %pad_maximum_fusion.11) | copy-start | bytes 147460
  103.4 6.1 %collective-permute-start.24 = (bf16[192,128]{1,0:T(8,128)(2,1)S(1)}, bf16[192,128]{1,0:T(8,128)(2,1)S(1)}, u32[]{:S(2)}, u32[]{:S(2)}) collective-permute-start(bf16[192,128]{1,0:T(8,128)(2,1)S(1)} %bitcast.75), channel_id=1, source_target_pairs={{0,1},{1,2},{2,3},{3,0},{4,5},{5,6},{6,7},{7,4},{8,9},{9,10},{10,1... | collective-permute-start | bytes 147464 | tf_op jit(solution)/shard_map/ppermute | solution.py:91
  105.8 4.7 %collective-permute-start.25 = (bf16[192,128]{1,0:T(8,128)(2,1)S(1)}, bf16[192,128]{1,0:T(8,128)(2,1)S(1)}, u32[]{:S(2)}, u32[]{:S(2)}) collective-permute-start(bf16[192,128]{1,0:T(8,128)(2,1)S(1)} %bitcast.76), channel_id=1, source_target_pairs={{0,3},{1,0},{2,1},{3,2},{4,7},{5,4},{6,5},{7,6},{8,11},{9,8},{10,9... | collective-permute-start | bytes 147464 | tf_op jit(solution)/shard_map/ppermute | solution.py:91
  107.3 5.5 %collective-permute-start.26 = (bf16[192,128]{1,0:T(8,128)(2,1)S(1)}, bf16[192,128]{1,0:T(8,128)(2,1)S(1)}, u32[]{:S(2)}, u32[]{:S(2)}) collective-permute-start(bf16[192,128]{1,0:T(8,128)(2,1)S(1)} %bitcast.77), channel_id=1, source_target_pairs={{0,2},{1,3},{2,0},{3,1},{4,6},{5,7},{6,4},{7,5},{8,10},{9,11},{10,... | collective-permute-start | bytes 147464 | tf_op jit(solution)/shard_map/ppermute | solution.py:91
  109.5 3.3 %copy-start.16 = (bf16[192,128]{1,0:T(8,128)(2,1)}, bf16[192,128]{1,0:T(8,128)(2,1)S(1)}, u32[]{:S(2)}) copy-start(bf16[192,128]{1,0:T(8,128)(2,1)S(1)} %collective-permute-done.24.refs_1_) | copy-start | bytes 147460
  110.5 2.3 %copy-start.17 = (bf16[192,128]{1,0:T(8,128)(2,1)}, bf16[192,128]{1,0:T(8,128)(2,1)S(1)}, u32[]{:S(2)}) copy-start(bf16[192,128]{1,0:T(8,128)(2,1)S(1)} %collective-permute-done.25.refs_2_) | copy-start | bytes 147460
  117.9 2.1 %collective-permute-start.27 = (bf16[64,4096]{1,0:T(8,128)(2,1)}, bf16[64,4096]{1,0:T(8,128)(2,1)S(1)}, u32[]{:S(2)}, u32[]{:S(2)}) collective-permute-start(bf16[64,4096]{1,0:T(8,128)(2,1)} %get-tuple-element.48), channel_id=1, source_target_pairs={{0,4},{4,0},{8,12},{12,8},{16,20},{20,16},{24,28},{28,24},{1,5},{5... | collective-permute-start | bytes 1572872 | tf_op jit(solution)/shard_map/ppermute | solution.py:96
  120.0 0.8 copy-start.6
  (4 other events, 2.9 us)

commit v5 on v4

--- a/solution.py
+++ b/solution.py
@@ -6,7 +6,7 @@
 from jax.sharding import PartitionSpec as P
 
 f32, bf16 = jnp.float32, jnp.bfloat16
-params = pltpu.CompilerParams(vmem_limit_bytes=60 << 20)
+params = pltpu.CompilerParams(vmem_limit_bytes=66000000)
 
 
 def cost(flops, *arrays):
@@ -187,7 +187,7 @@
 
 def add_parts(one, two, classes):
     width, block = one.shape
-    tile = min(block, 4096)
+    tile = min(block, 2048)
     part = pl.BlockSpec((width, tile), lambda i: (0, i))
     return pl.pallas_call(
         add_parts_kernel,

time: 124 us -> 124 us (level)
  waiting for transfers between devices: 37.5 us -> 43.9 us
  starting transfers between devices: 39.3 us -> 35.8 us
  local copies, waits for them, and re-layouts: 13.8 us -> 11.1 us
    ppermute x19, waiting for transfers between devices: 20.9 us -> 25.4 us  [paired(): lax.ppermute(value, 'slab', [(i, i ^ masks[i % 2]) for i in range(size)])]
    ppermute x19, starting transfers between devices: 23.4 us -> 20.3 us  [paired(): lax.ppermute(value, 'slab', [(i, i ^ masks[i % 2]) for i in range(size)])]
    unnamed x49 -> x41, local copies, waits for them, and re-layouts: 4.79 us -> 2.24 us
    ppermute x9, waiting for transfers between devices: 16.5 us -> 18.5 us  [shifted(): lax.ppermute(value, axis, [(i, (i + step) % size) for i in range(size)])]
  transfers between devices with their start and end apart: 28 -> 28, of which waited for: 15 -> 14; matrix products, arithmetic and copies ran while one was open for 5% -> 5% of each run, Pallas kernels for 18% -> 18%
where the time goes in v5:
time: 124 us; the launch traced here: 123 us
  waiting for transfers between devices  43.9 us (35%)
  starting transfers between devices  35.8 us (29%)
  Pallas kernels  28.6 us (23%)
  local copies, waits for them, and re-layouts  11.1 us (9%)
  other arithmetic  2.59 us (2%)
    ppermute x19, waiting for transfers between devices, paired(): lax.ppermute(value, 'slab', [(i, i ^ masks[i % 2]) for i in range(size)])  25.4 us
    ppermute x19, starting transfers between devices, paired(): lax.ppermute(value, 'slab', [(i, i ^ masks[i % 2]) for i in range(size)])  20.3 us
    ppermute x9, waiting for transfers between devices, shifted(): lax.ppermute(value, axis, [(i, (i + step) % size) for i in range(size)])  18.5 us
    ppermute x9, starting transfers between devices, shifted(): lax.ppermute(value, axis, [(i, (i + step) % size) for i in range(size)])  15.5 us
    pallas_call x4, Pallas kernels, match(): pl.pallas_call(match_kernel, in_specs=[pl.BlockSpec(memory_space=pltpu.SM...  15.2 us
    pallas_call x1, Pallas kernels, project(): pl.pallas_call(lambda *refs: project_kernel(planes, classes, own_o, depth...  4.71 us
    pallas_call x1, Pallas kernels, sum_images(): pl.pallas_call(sum_images_kernel, grid=(block // tile,), in_specs=[pl.Blo...  4.45 us
    dynamic_slice x1, local copies, waits for them, and re-layouts, local(): lax.dynamic_slice(later, (i * rows, batch * block), (rows, block))  2.51 us
  transfers between devices with their start and end apart: 28, of which 14 were waited for; matrix products, arithmetic and copies ran while one was open for 5% of the time, Pallas kernels for 18%

profile of v5, /device:TPU:0, one launch (start us, length us, event | category | flops | bytes accessed | tf_op | source)
XLA Modules:
  0.0 123.3 jit_solution(9466599543291872593)
XLA Ops:
  0.7 2.1 %fusion.29 = (bf16[48,4096]{1,0:T(8,128)(2,1)}, bf16[48,4096]{1,0:T(8,128)(2,1)S(1)}, bf16[48,4096]{1,0:T(8,128)(2,1)S(1)}) fusion(bf16[384,16384]{1,0:T(8,128)(2,1)} %param.9, s32[]{:T(128)S(6)} %select_n.175, s32[]{:T(128)S(6)} %select_n.178, s32[]{:T(128)S(6)} %select_n.177, s32[]{:T(128)S(6)} %select_n.176), kind=kLoop, calls=%fused_computation.100 | loop fusion | bytes 2359312 | tf_op jit(solution)/shard_map/dynamic_slice | solution.py:330
  4.3 1.2 collective-permute-done
  5.6 2.9 %collective-permute-start.1 = (bf16[134,2048]{1,0:T(8,128)(2,1)S(1)}, bf16[134,2048]{1,0:T(8,128)(2,1)S(1)}, u32[]{:S(2)}, u32[]{:S(2)}) collective-permute-start(bf16[134,2048]{1,0:T(8,128)(2,1)S(1)} %pad_maximum_fusion.refs_1_), channel_id=1, source_target_pairs={{0,8},{4,20},{8,0},{12,28},{16,24},{20,4},{24,16},{28,12},{1,9},{5... | collective-permute-start | bytes 1646600 | tf_op jit(solution)/shard_map/ppermute | solution.py:96
  8.5 1.6 %collective-permute-start.2 = (bf16[48,4096]{1,0:T(8,128)(2,1)S(1)}, bf16[48,4096]{1,0:T(8,128)(2,1)S(1)}, u32[]{:S(2)}, u32[]{:S(2)}) collective-permute-start(bf16[48,4096]{1,0:T(8,128)(2,1)S(1)} %get-tuple-element.64), channel_id=1, source_target_pairs={{0,1},{1,2},{2,3},{3,0},{4,5},{5,6},{6,7},{7,4},{8,9},{9,10},{10,1... | collective-permute-start | bytes 1179656 | tf_op jit(solution)/shard_map/ppermute | solution.py:91
  10.1 1.5 %collective-permute-start.3 = (bf16[134,2048]{1,0:T(8,128)(2,1)S(1)}, bf16[134,2048]{1,0:T(8,128)(2,1)S(1)}, u32[]{:S(2)}, u32[]{:S(2)}) collective-permute-start(bf16[134,2048]{1,0:T(8,128)(2,1)S(1)} %pad_maximum_fusion.refs_1_), channel_id=1, source_target_pairs={{0,16},{4,12},{8,24},{12,4},{16,0},{20,28},{24,8},{28,20},{1,17},{... | collective-permute-start | bytes 1646600 | tf_op jit(solution)/shard_map/ppermute | solution.py:96
  11.6 9.7 %collective-permute-done.2.refs_0_ = bf16[48,4096]{1,0:T(8,128)(2,1)S(1)} collective-permute-done((bf16[48,4096]{1,0:T(8,128)(2,1)S(1)}, bf16[48,4096]{1,0:T(8,128)(2,1)S(1)}, u32[]{:S(2)}, u32[]{:S(2)}) %collective-permute-start.2) | collective-permute-done | bytes 393248 | tf_op jit(solution)/shard_map/ppermute | solution.py:91
  21.3 2.1 %collective-permute-start.4 = (bf16[134,2048]{1,0:T(8,128)(2,1)S(1)}, bf16[134,2048]{1,0:T(8,128)(2,1)S(1)}, u32[]{:S(2)}, u32[]{:S(2)}) collective-permute-start(bf16[134,2048]{1,0:T(8,128)(2,1)S(1)} %collective-permute-done.1.refs_2_), channel_id=1, source_target_pairs={{0,16},{4,12},{8,24},{12,4},{16,0},{20,28},{24,8},{28,20},{1,17},{... | collective-permute-start | bytes 1646600 | tf_op jit(solution)/shard_map/ppermute | solution.py:96
  23.4 3.6 %collective-permute-start.8 = (bf16[48,4096]{1,0:T(8,128)(2,1)S(1)}, bf16[48,4096]{1,0:T(8,128)(2,1)}, u32[]{:S(2)}, u32[]{:S(2)}) collective-permute-start(bf16[48,4096]{1,0:T(8,128)(2,1)S(1)} %get-tuple-element.63), channel_id=1, source_target_pairs={{0,3},{1,0},{2,1},{3,2},{4,7},{5,4},{6,5},{7,6},{8,11},{9,8},{10,9... | collective-permute-start | bytes 1179656 | tf_op jit(solution)/shard_map/ppermute | solution.py:91
  27.1 3.9 %collective-permute-done.4.refs_4_ = bf16[134,2048]{1,0:T(8,128)(2,1)S(1)} collective-permute-done((bf16[134,2048]{1,0:T(8,128)(2,1)S(1)}, bf16[134,2048]{1,0:T(8,128)(2,1)S(1)}, u32[]{:S(2)}, u32[]{:S(2)}) %collective-permute-start.4) | collective-permute-done | bytes 548896 | tf_op jit(solution)/shard_map/ppermute | solution.py:96
  30.9 1.5 %collective-permute-start.6 = (bf16[48,4096]{1,0:T(8,128)(2,1)S(1)}, bf16[48,4096]{1,0:T(8,128)(2,1)S(1)}, u32[]{:S(2)}, u32[]{:S(2)}) collective-permute-start(bf16[48,4096]{1,0:T(8,128)(2,1)S(1)} %collective-permute-done.2.refs_0_), channel_id=1, source_target_pairs={{0,8},{4,20},{8,0},{12,28},{16,24},{20,4},{24,16},{28,12},{1,9},{5... | collective-permute-start | bytes 1179656 | tf_op jit(solution)/shard_map/ppermute | solution.py:96
  32.4 2.1 %collective-permute-start.7 = (bf16[48,4096]{1,0:T(8,128)(2,1)S(1)}, bf16[48,4096]{1,0:T(8,128)(2,1)S(1)}, u32[]{:S(2)}, u32[]{:S(2)}) collective-permute-start(bf16[48,4096]{1,0:T(8,128)(2,1)S(1)} %collective-permute-done.2.refs_0_), channel_id=1, source_target_pairs={{0,16},{4,12},{8,24},{12,4},{16,0},{20,28},{24,8},{28,20},{1,17},{... | collective-permute-start | bytes 1179656 | tf_op jit(solution)/shard_map/ppermute | solution.py:96
  34.5 2.6 %collective-permute-start.5 = (bf16[48,4096]{1,0:T(8,128)(2,1)}, bf16[48,4096]{1,0:T(8,128)(2,1)}, u32[]{:S(2)}, u32[]{:S(2)}) collective-permute-start(bf16[48,4096]{1,0:T(8,128)(2,1)} %get-tuple-element.62), channel_id=1, source_target_pairs={{0,2},{1,3},{2,0},{3,1},{4,6},{5,7},{6,4},{7,5},{8,10},{9,11},{10,... | collective-permute-start | bytes 1179656 | tf_op jit(solution)/shard_map/ppermute | solution.py:91
  37.1 4.5 %collective-permute-done.6.refs_1_ = bf16[48,4096]{1,0:T(8,128)(2,1)S(1)} collective-permute-done((bf16[48,4096]{1,0:T(8,128)(2,1)S(1)}, bf16[48,4096]{1,0:T(8,128)(2,1)S(1)}, u32[]{:S(2)}, u32[]{:S(2)}) %collective-permute-start.6) | collective-permute-done | bytes 393248 | tf_op jit(solution)/shard_map/ppermute | solution.py:96
  41.5 0.8 copy-done.8
  42.3 0.9 collective-permute-start.10
  43.2 1.7 %collective-permute-start.9 = (bf16[48,4096]{1,0:T(8,128)(2,1)}, bf16[48,4096]{1,0:T(8,128)(2,1)}, u32[]{:S(2)}, u32[]{:S(2)}) collective-permute-start(bf16[48,4096]{1,0:T(8,128)(2,1)} %collective-permute-done.8.refs_0_), channel_id=1, source_target_pairs={{0,8},{4,20},{8,0},{12,28},{16,24},{20,4},{24,16},{28,12},{1,9},{5... | collective-permute-start | bytes 1179656 | tf_op jit(solution)/shard_map/ppermute | solution.py:96
  45.0 0.6 pad_add_fusion.refs_0_.order_ref
  45.6 4.7 %project.1 = (bf16[2064,256]{1,0:T(8,128)(2,1)}, f32[1,256]{1,0:T(1,128)}, f32[8,37,128]{2,1,0:T(8,128)}) custom-call(s32[4]{0:T(128)} %pad_add_fusion.refs_0_.order_ref, bf16[134,2048]{1,0:T(8,128)(2,1)} %copy-done, bf16[134,2048]{1,0:T(8,128)(2,1)} %copy-done.2, bf16[134,2048]{1,0:T(8,128)(2,1)} %copy-done.3, bf16[134,2048]{1,0:T(8,128)(2,1)} %copy-done.4), custom_call_target="tpu_custom_call" | custom-call | flops 536870912 | bytes 2195456 | tf_op jit(solution)/shard_map/project/pallas_call | solution.py:253
  50.3 2.3 %collective-permute-done.5.refs_0_ = bf16[48,4096]{1,0:T(8,128)(2,1)} collective-permute-done((bf16[48,4096]{1,0:T(8,128)(2,1)}, bf16[48,4096]{1,0:T(8,128)(2,1)}, u32[]{:S(2)}, u32[]{:S(2)}) %collective-permute-start.5) | collective-permute-done | bytes 393248 | tf_op jit(solution)/shard_map/ppermute | solution.py:91
  52.6 0.8 collective-permute-done.10.refs_2_
  53.4 1.1 collective-permute-start.12
  54.7 1.7 %collective-permute-start.17 = (bf16[48,4096]{1,0:T(8,128)(2,1)}, bf16[48,4096]{1,0:T(8,128)(2,1)}, u32[]{:S(2)}, u32[]{:S(2)}) collective-permute-start(bf16[48,4096]{1,0:T(8,128)(2,1)} %collective-permute-done.9.refs_1_), channel_id=1, source_target_pairs={{0,16},{4,12},{8,24},{12,4},{16,0},{20,28},{24,8},{28,20},{1,17},{... | collective-permute-start | bytes 1179656 | tf_op jit(solution)/shard_map/ppermute | solution.py:96
  56.8 8.8 %collective-permute-done.12.refs_1_ = bf16[48,4096]{1,0:T(8,128)(2,1)S(1)} collective-permute-done((bf16[48,4096]{1,0:T(8,128)(2,1)}, bf16[48,4096]{1,0:T(8,128)(2,1)S(1)}, u32[]{:S(2)}, u32[]{:S(2)}) %collective-permute-start.12) | collective-permute-done | bytes 393248 | tf_op jit(solution)/shard_map/ppermute | solution.py:96
  65.6 3.9 %match.6 = (f32[1,192,256]{2,1,0:T(8,128)}, bf16[192,4096]{1,0:T(8,128)(2,1)}) custom-call(s32[4]{0:T(128)} %pad_add_fusion.refs_0_.order_ref, bf16[2064,256]{1,0:T(8,128)(2,1)} %get-tuple-element.32.mine_ref, bf16[2064,256]{1,0:T(8,128)(2,1)} %collective-permute-done.11.theirs_ref, bf16[48,4096]{1,0:T(8,128)(2,1)} %copy-done.7, bf16[48,4096]{1,0:T(8,128)(2,1)} %copy-done.8, ...), custom_call_target="tpu_custom_call" | custom-call | flops 402653184 | bytes 3686400 | tf_op jit(solution)/shard_map/match/pallas_call | solution.py:290
  69.5 2.9 %collective-permute-start.16 = (f32[192,256]{1,0:T(8,128)}, f32[192,256]{1,0:T(8,128)S(1)}, u32[]{:S(2)}, u32[]{:S(2)}) collective-permute-start(f32[192,256]{1,0:T(8,128)} %bitcast.89), channel_id=1, source_target_pairs={{0,3},{1,0},{2,1},{3,2},{4,7},{5,4},{6,5},{7,6},{8,11},{9,8},{10,9... | collective-permute-start | bytes 589832 | tf_op jit(solution)/shard_map/ppermute | solution.py:91
  72.4 3.8 %match.7 = (f32[1,192,256]{2,1,0:T(8,128)}, bf16[192,4096]{1,0:T(8,128)(2,1)}) custom-call(s32[4]{0:T(128)} %pad_add_fusion.refs_0_.order_ref, bf16[2064,256]{1,0:T(8,128)(2,1)} %get-tuple-element.32.mine_ref, bf16[2064,256]{1,0:T(8,128)(2,1)} %collective-permute-done.11.theirs_ref, bf16[48,4096]{1,0:T(8,128)(2,1)} %collective-permute-done.8.refs_0_, ...), custom_call_target="tpu_custom_call" | custom-call | flops 402653184 | bytes 3686400 | tf_op jit(solution)/shard_map/match/pallas_call | solution.py:290
  76.1 1.8 %collective-permute-done.14.refs_3_ = bf16[48,4096]{1,0:T(8,128)(2,1)} collective-permute-done((bf16[48,4096]{1,0:T(8,128)(2,1)S(1)}, bf16[48,4096]{1,0:T(8,128)(2,1)}, u32[]{:S(2)}, u32[]{:S(2)}) %collective-permute-start.14) | collective-permute-done | bytes 393248 | tf_op jit(solution)/shard_map/ppermute | solution.py:96
  77.9 3.7 %match.4 = (f32[1,192,256]{2,1,0:T(8,128)}, bf16[192,4096]{1,0:T(8,128)(2,1)}) custom-call(s32[4]{0:T(128)} %pad_add_fusion.refs_0_.order_ref, bf16[2064,256]{1,0:T(8,128)(2,1)} %get-tuple-element.32.mine_ref, bf16[2064,256]{1,0:T(8,128)(2,1)} %collective-permute-done.11.theirs_ref, bf16[48,4096]{1,0:T(8,128)(2,1)} %collective-permute-done.5.refs_0_, ...), custom_call_target="tpu_custom_call" | custom-call | flops 402653184 | bytes 3686400 | tf_op jit(solution)/shard_map/match/pallas_call | solution.py:290
  81.6 1.0 collective-permute-start.19
  82.6 2.5 %fusion.28 = (bf16[48,4096]{1,0:T(8,128)(2,1)}, bf16[48,4096]{1,0:T(8,128)(2,1)}, bf16[48,4096]{1,0:T(8,128)(2,1)}, bf16[48,4096]{1,0:T(8,128)(2,1)}) fusion(bf16[384,16384]{1,0:T(8,128)(2,1)} %param.9, s32[]{:T(128)S(6)} %select_n.186, s32[]{:T(128)S(6)} %select_n.183, s32[]{:T(128)S(6)} %select_n.185, s32[]{:T(128)S(6)} %select_n.184, s32[]{:T(128)S(6)} %select_n.175), kind=kLoop, calls=%fused_computation.99 | loop fusion | bytes 3145748 | tf_op jit(solution)/shard_map/dynamic_slice | solution.py:370
  85.7 0.6 fusion.27
  86.5 2.0 %window_slices.1 = bf16[4,128,256]{2,1,0:T(8,128)(2,1)} custom-call(s32[4]{0:T(128)} %pad_add_fusion.refs_0_.order_ref, f32[8,37,128]{2,1,0:T(8,128)} %get-tuple-element.41.refs_1_), custom_call_target="tpu_custom_call" | custom-call | bytes 151552 | tf_op jit(solution)/shard_map/window_slices/pallas_call | solution.py:78
  88.5 3.8 %match.5 = (f32[1,192,256]{2,1,0:T(8,128)}, bf16[192,4096]{1,0:T(8,128)(2,1)}) custom-call(s32[4]{0:T(128)} %pad_add_fusion.refs_0_.order_ref, bf16[2064,256]{1,0:T(8,128)(2,1)} %get-tuple-element.32.mine_ref, bf16[2064,256]{1,0:T(8,128)(2,1)} %collective-permute-done.11.theirs_ref, bf16[48,4096]{1,0:T(8,128)(2,1)} %get-tuple-element.61.refs_0_, ...), custom_call_target="tpu_custom_call" | custom-call | flops 402653184 | bytes 3686400 | tf_op jit(solution)/shard_map/match/pallas_call | solution.py:290
  92.3 1.3 %collective-permute-done.19 = f32[192,256]{1,0:T(8,128)S(1)} collective-permute-done((f32[192,256]{1,0:T(8,128)}, f32[192,256]{1,0:T(8,128)S(1)}, u32[]{:S(2)}, u32[]{:S(2)}) %collective-permute-start.19) | collective-permute-done | bytes 196640 | tf_op jit(solution)/shard_map/ppermute | solution.py:91
  93.6 1.0 fusion.13
  95.5 0.9 collective-permute-start.20
  96.4 0.9 collective-permute-start.21
  97.3 1.7 %collective-permute-start.22 = (bf16[198,256]{1,0:T(8,128)(2,1)S(1)}, bf16[198,256]{1,0:T(8,128)(2,1)S(1)}, u32[]{:S(2)}, u32[]{:S(2)}) collective-permute-start(bf16[198,256]{1,0:T(8,128)(2,1)S(1)} %get-tuple-element.83), channel_id=1, source_target_pairs={{0,24},{4,28},{8,16},{12,20},{16,8},{20,12},{24,0},{28,4},{1,25},{... | collective-permute-start | bytes 304136 | tf_op jit(solution)/shard_map/ppermute | solution.py:96
  99.1 1.8 %collective-permute-done.20 = bf16[198,256]{1,0:T(8,128)(2,1)S(1)} collective-permute-done((bf16[198,256]{1,0:T(8,128)(2,1)S(1)}, bf16[198,256]{1,0:T(8,128)(2,1)S(1)}, u32[]{:S(2)}, u32[]{:S(2)}) %collective-permute-start.20) | collective-permute-done | bytes 101408 | tf_op jit(solution)/shard_map/ppermute | solution.py:96
  100.9 2.4 %collective-permute-done.21 = bf16[198,256]{1,0:T(8,128)(2,1)S(1)} collective-permute-done((bf16[198,256]{1,0:T(8,128)(2,1)S(1)}, bf16[198,256]{1,0:T(8,128)(2,1)S(1)}, u32[]{:S(2)}, u32[]{:S(2)}) %collective-permute-start.21) | collective-permute-done | bytes 101408 | tf_op jit(solution)/shard_map/ppermute | solution.py:96
  104.4 3.4 %collective-permute-start.25 = (bf16[192,128]{1,0:T(8,128)(2,1)S(1)}, bf16[192,128]{1,0:T(8,128)(2,1)S(1)}, u32[]{:S(2)}, u32[]{:S(2)}) collective-permute-start(bf16[192,128]{1,0:T(8,128)(2,1)S(1)} %bitcast.76), channel_id=1, source_target_pairs={{0,3},{1,0},{2,1},{3,2},{4,7},{5,4},{6,5},{7,6},{8,11},{9,8},{10,9... | collective-permute-start | bytes 147464 | tf_op jit(solution)/shard_map/ppermute | solution.py:91
  107.9 2.5 %collective-permute-done.24.refs_1_ = bf16[192,128]{1,0:T(8,128)(2,1)S(1)} collective-permute-done((bf16[192,128]{1,0:T(8,128)(2,1)S(1)}, bf16[192,128]{1,0:T(8,128)(2,1)S(1)}, u32[]{:S(2)}, u32[]{:S(2)}) %collective-permute-start.24) | collective-permute-done | bytes 49184 | tf_op jit(solution)/shard_map/ppermute | solution.py:91
  110.4 2.7 %collective-permute-done.26.refs_3_ = bf16[192,128]{1,0:T(8,128)(2,1)S(1)} collective-permute-done((bf16[192,128]{1,0:T(8,128)(2,1)S(1)}, bf16[192,128]{1,0:T(8,128)(2,1)S(1)}, u32[]{:S(2)}, u32[]{:S(2)}) %collective-permute-start.26) | collective-permute-done | bytes 49184 | tf_op jit(solution)/shard_map/ppermute | solution.py:91
  113.7 4.5 %sum_images.1 = (f32[64,4096]{1,0:T(8,128)}, bf16[64,4096]{1,0:T(8,128)(2,1)}) custom-call(bf16[192,128]{1,0:T(8,128)(2,1)} %bitcast.78, bf16[192,128]{1,0:T(8,128)(2,1)} %copy-done.12, bf16[192,128]{1,0:T(8,128)(2,1)} %copy-done.13, bf16[192,128]{1,0:T(8,128)(2,1)} %copy-done.14, bf16[192,4096]{1,0:T(8,128)(2,1)} %get-tuple-element.43.refs_4_, ...), custom_call_target="tpu_custom_call" | custom-call | flops 805306368 | bytes 6488064 | tf_op jit(solution)/shard_map/sum_images/pallas_call | solution.py:170
  118.4 0.7 reshape.324
  119.1 0.8 copy.27
  120.3 0.8 copy-done.5
  121.1 2.2 %add_parts.1 = f32[32,2,4096]{2,1,0:T(2,128)} custom-call(f32[64,4096]{1,0:T(8,128)} %get-tuple-element.47.one_ref, bf16[64,4096]{1,0:T(8,128)(2,1)} %copy-done.5), custom_call_target="tpu_custom_call" | custom-call | flops 524288 | bytes 2621440 | tf_op jit(solution)/shard_map/add_parts/pallas_call | solution.py:192
  (116 shorter events, 6.1 us)
Async XLA Ops:
  0.7 2.2 %copy-start.6 = (bf16[32,2,4096]{2,1,0:T(2,128)(2,1)S(1)}, bf16[32,2,4096]{2,1,0:T(2,128)(2,1)}, u32[]{:S(2)}) copy-start(bf16[32,2,4096]{2,1,0:T(2,128)(2,1)} %param.6) | copy-start | bytes 1572868
  0.7 2.4 %copy-start.18 = (f32[2,64]{1,0:T(2,128)S(1)}, f32[2,64]{1,0:T(2,128)}, u32[]{:S(2)}) copy-start(f32[2,64]{1,0:T(2,128)} %param.11) | copy-start | bytes 1540
  0.7 2.6 %copy-start.19 = (s32[2,64]{1,0:T(2,128)S(1)}, s32[2,64]{1,0:T(2,128)}, u32[]{:S(2)}) copy-start(s32[2,64]{1,0:T(2,128)} %param.8) | copy-start | bytes 1540
  0.7 2.8 %copy-start.16 = (bf16[2,64,32]{1,2,0:T(8,128)(2,1)S(1)}, bf16[2,64,32]{1,2,0:T(8,128)(2,1)}, u32[]{:S(2)}) copy-start(bf16[2,64,32]{1,2,0:T(8,128)(2,1)} %param.7) | copy-start | bytes 24580
  3.8 1.7 %collective-permute-start = (bf16[67,2048]{1,0:T(8,128)(2,1)S(1)}, bf16[67,2048]{1,0:T(8,128)(2,1)S(1)}, u32[]{:S(2)}, u32[]{:S(2)}) collective-permute-start(bf16[67,2048]{1,0:T(8,128)(2,1)S(1)} %pad_maximum_fusion.7), channel_id=1, source_target_pairs={{0,4},{4,0},{8,12},{12,8},{16,20},{20,16},{24,28},{28,24},{1,5},{5... | collective-permute-start | bytes 823304 | tf_op jit(solution)/shard_map/ppermute | solution.py:96
  5.6 40.0 %copy-start = (bf16[134,2048]{1,0:T(8,128)(2,1)}, bf16[134,2048]{1,0:T(8,128)(2,1)S(1)}, u32[]{:S(2)}) copy-start(bf16[134,2048]{1,0:T(8,128)(2,1)S(1)} %pad_maximum_fusion.refs_1_) | copy-start | bytes 1646596
  5.6 15.7 %collective-permute-start.1 = (bf16[134,2048]{1,0:T(8,128)(2,1)S(1)}, bf16[134,2048]{1,0:T(8,128)(2,1)S(1)}, u32[]{:S(2)}, u32[]{:S(2)}) collective-permute-start(bf16[134,2048]{1,0:T(8,128)(2,1)S(1)} %pad_maximum_fusion.refs_1_), channel_id=1, source_target_pairs={{0,8},{4,20},{8,0},{12,28},{16,24},{20,4},{24,16},{28,12},{1,9},{5... | collective-permute-start | bytes 1646600 | tf_op jit(solution)/shard_map/ppermute | solution.py:96
  8.5 12.8 %collective-permute-start.2 = (bf16[48,4096]{1,0:T(8,128)(2,1)S(1)}, bf16[48,4096]{1,0:T(8,128)(2,1)S(1)}, u32[]{:S(2)}, u32[]{:S(2)}) collective-permute-start(bf16[48,4096]{1,0:T(8,128)(2,1)S(1)} %get-tuple-element.64), channel_id=1, source_target_pairs={{0,1},{1,2},{2,3},{3,0},{4,5},{5,6},{6,7},{7,4},{8,9},{9,10},{10,1... | collective-permute-start | bytes 1179656 | tf_op jit(solution)/shard_map/ppermute | solution.py:91
  10.1 17.0 %collective-permute-start.3 = (bf16[134,2048]{1,0:T(8,128)(2,1)S(1)}, bf16[134,2048]{1,0:T(8,128)(2,1)S(1)}, u32[]{:S(2)}, u32[]{:S(2)}) collective-permute-start(bf16[134,2048]{1,0:T(8,128)(2,1)S(1)} %pad_maximum_fusion.refs_1_), channel_id=1, source_target_pairs={{0,16},{4,12},{8,24},{12,4},{16,0},{20,28},{24,8},{28,20},{1,17},{... | collective-permute-start | bytes 1646600 | tf_op jit(solution)/shard_map/ppermute | solution.py:96
  21.3 44.3 %copy-start.7 = (bf16[48,4096]{1,0:T(8,128)(2,1)}, bf16[48,4096]{1,0:T(8,128)(2,1)S(1)}, u32[]{:S(2)}) copy-start(bf16[48,4096]{1,0:T(8,128)(2,1)S(1)} %collective-permute-done.2.refs_0_) | copy-start | bytes 1179652
  21.3 5.8 %copy-start.2 = (bf16[134,2048]{1,0:T(8,128)(2,1)}, bf16[134,2048]{1,0:T(8,128)(2,1)S(1)}, u32[]{:S(2)}) copy-start(bf16[134,2048]{1,0:T(8,128)(2,1)S(1)} %collective-permute-done.1.refs_2_) | copy-start | bytes 1646596
  21.3 9.6 %collective-permute-start.4 = (bf16[134,2048]{1,0:T(8,128)(2,1)S(1)}, bf16[134,2048]{1,0:T(8,128)(2,1)S(1)}, u32[]{:S(2)}, u32[]{:S(2)}) collective-permute-start(bf16[134,2048]{1,0:T(8,128)(2,1)S(1)} %collective-permute-done.1.refs_2_), channel_id=1, source_target_pairs={{0,16},{4,12},{8,24},{12,4},{16,0},{20,28},{24,8},{28,20},{1,17},{... | collective-permute-start | bytes 1646600 | tf_op jit(solution)/shard_map/ppermute | solution.py:96
  23.4 13.7 %collective-permute-start.8 = (bf16[48,4096]{1,0:T(8,128)(2,1)S(1)}, bf16[48,4096]{1,0:T(8,128)(2,1)}, u32[]{:S(2)}, u32[]{:S(2)}) collective-permute-start(bf16[48,4096]{1,0:T(8,128)(2,1)S(1)} %get-tuple-element.63), channel_id=1, source_target_pairs={{0,3},{1,0},{2,1},{3,2},{4,7},{5,4},{6,5},{7,6},{8,11},{9,8},{10,9... | collective-permute-start | bytes 1179656 | tf_op jit(solution)/shard_map/ppermute | solution.py:91
  27.1 3.9 %copy-start.3 = (bf16[134,2048]{1,0:T(8,128)(2,1)}, bf16[134,2048]{1,0:T(8,128)(2,1)S(1)}, u32[]{:S(2)}) copy-start(bf16[134,2048]{1,0:T(8,128)(2,1)S(1)} %collective-permute-done.3.refs_3_) | copy-start | bytes 1646596
  30.9 1.5 %copy-start.4 = (bf16[134,2048]{1,0:T(8,128)(2,1)}, bf16[134,2048]{1,0:T(8,128)(2,1)S(1)}, u32[]{:S(2)}) copy-start(bf16[134,2048]{1,0:T(8,128)(2,1)S(1)} %collective-permute-done.4.refs_4_) | copy-start | bytes 1646596
  30.9 10.6 %collective-permute-start.6 = (bf16[48,4096]{1,0:T(8,128)(2,1)S(1)}, bf16[48,4096]{1,0:T(8,128)(2,1)S(1)}, u32[]{:S(2)}, u32[]{:S(2)}) collective-permute-start(bf16[48,4096]{1,0:T(8,128)(2,1)S(1)} %collective-permute-done.2.refs_0_), channel_id=1, source_target_pairs={{0,8},{4,20},{8,0},{12,28},{16,24},{20,4},{24,16},{28,12},{1,9},{5... | collective-permute-start | bytes 1179656 | tf_op jit(solution)/shard_map/ppermute | solution.py:96
  32.4 9.1 %collective-permute-start.7 = (bf16[48,4096]{1,0:T(8,128)(2,1)S(1)}, bf16[48,4096]{1,0:T(8,128)(2,1)S(1)}, u32[]{:S(2)}, u32[]{:S(2)}) collective-permute-start(bf16[48,4096]{1,0:T(8,128)(2,1)S(1)} %collective-permute-done.2.refs_0_), channel_id=1, source_target_pairs={{0,16},{4,12},{8,24},{12,4},{16,0},{20,28},{24,8},{28,20},{1,17},{... | collective-permute-start | bytes 1179656 | tf_op jit(solution)/shard_map/ppermute | solution.py:96
  34.5 18.2 %collective-permute-start.5 = (bf16[48,4096]{1,0:T(8,128)(2,1)}, bf16[48,4096]{1,0:T(8,128)(2,1)}, u32[]{:S(2)}, u32[]{:S(2)}) collective-permute-start(bf16[48,4096]{1,0:T(8,128)(2,1)} %get-tuple-element.62), channel_id=1, source_target_pairs={{0,2},{1,3},{2,0},{3,1},{4,6},{5,7},{6,4},{7,5},{8,10},{9,11},{10,... | collective-permute-start | bytes 1179656 | tf_op jit(solution)/shard_map/ppermute | solution.py:91
  41.5 0.8 copy-start.8
  42.3 0.9 copy-start.9
  42.3 11.1 %collective-permute-start.10 = (bf16[48,4096]{1,0:T(8,128)(2,1)}, bf16[48,4096]{1,0:T(8,128)(2,1)}, u32[]{:S(2)}, u32[]{:S(2)}) collective-permute-start(bf16[48,4096]{1,0:T(8,128)(2,1)} %collective-permute-done.8.refs_0_), channel_id=1, source_target_pairs={{0,16},{4,12},{8,24},{12,4},{16,0},{20,28},{24,8},{28,20},{1,17},{... | collective-permute-start | bytes 1179656 | tf_op jit(solution)/shard_map/ppermute | solution.py:96
  43.2 10.2 %collective-permute-start.9 = (bf16[48,4096]{1,0:T(8,128)(2,1)}, bf16[48,4096]{1,0:T(8,128)(2,1)}, u32[]{:S(2)}, u32[]{:S(2)}) collective-permute-start(bf16[48,4096]{1,0:T(8,128)(2,1)} %collective-permute-done.8.refs_0_), channel_id=1, source_target_pairs={{0,8},{4,20},{8,0},{12,28},{16,24},{20,4},{24,16},{28,12},{1,9},{5... | collective-permute-start | bytes 1179656 | tf_op jit(solution)/shard_map/ppermute | solution.py:96
  53.4 12.1 %collective-permute-start.11 = (bf16[2064,256]{1,0:T(8,128)(2,1)}, bf16[2064,256]{1,0:T(8,128)(2,1)}, u32[]{:S(2)}, u32[]{:S(2)}) collective-permute-start(bf16[2064,256]{1,0:T(8,128)(2,1)} %get-tuple-element.32.mine_ref), channel_id=1, source_target_pairs={{0,4},{4,0},{8,12},{12,8},{16,20},{20,16},{24,28},{28,24},{1,5},{5... | collective-permute-start | bytes 3170312 | tf_op jit(solution)/shard_map/ppermute | solution.py:96
  53.4 12.1 %collective-permute-start.12 = (bf16[48,4096]{1,0:T(8,128)(2,1)}, bf16[48,4096]{1,0:T(8,128)(2,1)S(1)}, u32[]{:S(2)}, u32[]{:S(2)}) collective-permute-start(bf16[48,4096]{1,0:T(8,128)(2,1)} %collective-permute-done.5.refs_0_), channel_id=1, source_target_pairs={{0,8},{4,20},{8,0},{12,28},{16,24},{20,4},{24,16},{28,12},{1,9},{5... | collective-permute-start | bytes 1179656 | tf_op jit(solution)/shard_map/ppermute | solution.py:96
  54.5 11.1 %collective-permute-start.15 = (bf16[48,4096]{1,0:T(8,128)(2,1)}, bf16[48,4096]{1,0:T(8,128)(2,1)}, u32[]{:S(2)}, u32[]{:S(2)}) collective-permute-start(bf16[48,4096]{1,0:T(8,128)(2,1)} %copy-done.8), channel_id=1, source_target_pairs={{0,16},{4,12},{8,24},{12,4},{16,0},{20,28},{24,8},{28,20},{1,17},{... | collective-permute-start | bytes 1179656 | tf_op jit(solution)/shard_map/ppermute | solution.py:96
  54.7 17.6 %collective-permute-start.17 = (bf16[48,4096]{1,0:T(8,128)(2,1)}, bf16[48,4096]{1,0:T(8,128)(2,1)}, u32[]{:S(2)}, u32[]{:S(2)}) collective-permute-start(bf16[48,4096]{1,0:T(8,128)(2,1)} %collective-permute-done.9.refs_1_), channel_id=1, source_target_pairs={{0,16},{4,12},{8,24},{12,4},{16,0},{20,28},{24,8},{28,20},{1,17},{... | collective-permute-start | bytes 1179656 | tf_op jit(solution)/shard_map/ppermute | solution.py:96
  56.5 19.6 %collective-permute-start.13 = (bf16[48,4096]{1,0:T(8,128)(2,1)}, bf16[48,4096]{1,0:T(8,128)(2,1)}, u32[]{:S(2)}, u32[]{:S(2)}) collective-permute-start(bf16[48,4096]{1,0:T(8,128)(2,1)} %collective-permute-done.5.refs_0_), channel_id=1, source_target_pairs={{0,16},{4,12},{8,24},{12,4},{16,0},{20,28},{24,8},{28,20},{1,17},{... | collective-permute-start | bytes 1179656 | tf_op jit(solution)/shard_map/ppermute | solution.py:96
  65.5 3.9 %copy-start.10 = (bf16[48,4096]{1,0:T(8,128)(2,1)}, bf16[48,4096]{1,0:T(8,128)(2,1)S(1)}, u32[]{:S(2)}) copy-start(bf16[48,4096]{1,0:T(8,128)(2,1)S(1)} %collective-permute-done.12.refs_1_) | copy-start | bytes 1179652
  65.5 12.4 %collective-permute-start.14 = (bf16[48,4096]{1,0:T(8,128)(2,1)S(1)}, bf16[48,4096]{1,0:T(8,128)(2,1)}, u32[]{:S(2)}, u32[]{:S(2)}) collective-permute-start(bf16[48,4096]{1,0:T(8,128)(2,1)S(1)} %collective-permute-done.12.refs_1_), channel_id=1, source_target_pairs={{0,16},{4,12},{8,24},{12,4},{16,0},{20,28},{24,8},{28,20},{1,17},{... | collective-permute-start | bytes 1179656 | tf_op jit(solution)/shard_map/ppermute | solution.py:96
  69.5 22.8 %collective-permute-start.16 = (f32[192,256]{1,0:T(8,128)}, f32[192,256]{1,0:T(8,128)S(1)}, u32[]{:S(2)}, u32[]{:S(2)}) collective-permute-start(f32[192,256]{1,0:T(8,128)} %bitcast.89), channel_id=1, source_target_pairs={{0,3},{1,0},{2,1},{3,2},{4,7},{5,4},{6,5},{7,6},{8,11},{9,8},{10,9... | collective-permute-start | bytes 589832 | tf_op jit(solution)/shard_map/ppermute | solution.py:91
  76.1 16.2 %collective-permute-start.18 = (f32[192,256]{1,0:T(8,128)}, f32[192,256]{1,0:T(8,128)S(1)}, u32[]{:S(2)}, u32[]{:S(2)}) collective-permute-start(f32[192,256]{1,0:T(8,128)} %bitcast.90), channel_id=1, source_target_pairs={{0,1},{1,2},{2,3},{3,0},{4,5},{5,6},{6,7},{7,4},{8,9},{9,10},{10,1... | collective-permute-start | bytes 589832 | tf_op jit(solution)/shard_map/ppermute | solution.py:91
  81.6 3.5 %copy-start.17 = (f32[384]{0:T(512)S(1)}, f32[384]{0:T(512)}, u32[]{:S(2)}) copy-start(f32[384]{0:T(512)} %param.10) | copy-start | bytes 4612
  81.6 12.0 %collective-permute-start.19 = (f32[192,256]{1,0:T(8,128)}, f32[192,256]{1,0:T(8,128)S(1)}, u32[]{:S(2)}, u32[]{:S(2)}) collective-permute-start(f32[192,256]{1,0:T(8,128)} %bitcast.91), channel_id=1, source_target_pairs={{0,2},{1,3},{2,0},{3,1},{4,6},{5,7},{6,4},{7,5},{8,10},{9,11},{10,... | collective-permute-start | bytes 589832 | tf_op jit(solution)/shard_map/ppermute | solution.py:91
  92.3 2.4 %copy-start.15 = (f32[1,256]{1,0:T(1,128)S(1)}, f32[1,256]{1,0:T(1,128)}, u32[]{:S(2)}) copy-start(f32[1,256]{1,0:T(1,128)} %get-tuple-element.39) | copy-start | bytes 3076
  93.6 5.5 %copy-start.1 = (bf16[4,128,256]{2,1,0:T(8,128)(2,1)S(1)}, bf16[4,128,256]{2,1,0:T(8,128)(2,1)}, u32[]{:S(2)}) copy-start(bf16[4,128,256]{2,1,0:T(8,128)(2,1)} %window_slices.1) | copy-start | bytes 786436
  95.5 5.4 %collective-permute-start.20 = (bf16[198,256]{1,0:T(8,128)(2,1)S(1)}, bf16[198,256]{1,0:T(8,128)(2,1)S(1)}, u32[]{:S(2)}, u32[]{:S(2)}) collective-permute-start(bf16[198,256]{1,0:T(8,128)(2,1)S(1)} %get-tuple-element.83), channel_id=1, source_target_pairs={{0,8},{4,12},{8,0},{12,4},{16,24},{20,28},{24,16},{28,20},{1,9},{5... | collective-permute-start | bytes 304136 | tf_op jit(solution)/shard_map/ppermute | solution.py:96
  96.4 6.9 %collective-permute-start.21 = (bf16[198,256]{1,0:T(8,128)(2,1)S(1)}, bf16[198,256]{1,0:T(8,128)(2,1)S(1)}, u32[]{:S(2)}, u32[]{:S(2)}) collective-permute-start(bf16[198,256]{1,0:T(8,128)(2,1)S(1)} %get-tuple-element.83), channel_id=1, source_target_pairs={{0,16},{4,20},{8,24},{12,28},{16,0},{20,4},{24,8},{28,12},{1,17},{... | collective-permute-start | bytes 304136 | tf_op jit(solution)/shard_map/ppermute | solution.py:96
  97.3 5.9 %collective-permute-start.22 = (bf16[198,256]{1,0:T(8,128)(2,1)S(1)}, bf16[198,256]{1,0:T(8,128)(2,1)S(1)}, u32[]{:S(2)}, u32[]{:S(2)}) collective-permute-start(bf16[198,256]{1,0:T(8,128)(2,1)S(1)} %get-tuple-element.83), channel_id=1, source_target_pairs={{0,24},{4,28},{8,16},{12,20},{16,8},{20,12},{24,0},{28,4},{1,25},{... | collective-permute-start | bytes 304136 | tf_op jit(solution)/shard_map/ppermute | solution.py:96
  103.6 4.3 %collective-permute-start.23 = (f32[194,128]{1,0:T(8,128)S(1)}, f32[194,128]{1,0:T(8,128)S(1)}, u32[]{:S(2)}, u32[]{:S(2)}) collective-permute-start(f32[194,128]{1,0:T(8,128)S(1)} %pad_maximum_fusion.10), channel_id=1, source_target_pairs={{0,4},{4,0},{8,12},{12,8},{16,20},{20,16},{24,28},{28,24},{1,5},{5... | collective-permute-start | bytes 297992 | tf_op jit(solution)/shard_map/ppermute | solution.py:96
  104.0 9.1 %copy-start.11 = (bf16[4,48,128]{2,1,0:T(8,128)(2,1)}, bf16[4,48,128]{2,1,0:T(8,128)(2,1)S(1)}, u32[]{:S(2)}) copy-start(bf16[4,48,128]{2,1,0:T(8,128)(2,1)S(1)} %pad_maximum_fusion.11) | copy-start | bytes 147460
  104.0 6.4 %collective-permute-start.24 = (bf16[192,128]{1,0:T(8,128)(2,1)S(1)}, bf16[192,128]{1,0:T(8,128)(2,1)S(1)}, u32[]{:S(2)}, u32[]{:S(2)}) collective-permute-start(bf16[192,128]{1,0:T(8,128)(2,1)S(1)} %bitcast.75), channel_id=1, source_target_pairs={{0,1},{1,2},{2,3},{3,0},{4,5},{5,6},{6,7},{7,4},{8,9},{9,10},{10,1... | collective-permute-start | bytes 147464 | tf_op jit(solution)/shard_map/ppermute | solution.py:91
  104.4 6.0 %collective-permute-start.25 = (bf16[192,128]{1,0:T(8,128)(2,1)S(1)}, bf16[192,128]{1,0:T(8,128)(2,1)S(1)}, u32[]{:S(2)}, u32[]{:S(2)}) collective-permute-start(bf16[192,128]{1,0:T(8,128)(2,1)S(1)} %bitcast.76), channel_id=1, source_target_pairs={{0,3},{1,0},{2,1},{3,2},{4,7},{5,4},{6,5},{7,6},{8,11},{9,8},{10,9... | collective-permute-start | bytes 147464 | tf_op jit(solution)/shard_map/ppermute | solution.py:91
  107.9 5.2 %collective-permute-start.26 = (bf16[192,128]{1,0:T(8,128)(2,1)S(1)}, bf16[192,128]{1,0:T(8,128)(2,1)S(1)}, u32[]{:S(2)}, u32[]{:S(2)}) collective-permute-start(bf16[192,128]{1,0:T(8,128)(2,1)S(1)} %bitcast.77), channel_id=1, source_target_pairs={{0,2},{1,3},{2,0},{3,1},{4,6},{5,7},{6,4},{7,5},{8,10},{9,11},{10,... | collective-permute-start | bytes 147464 | tf_op jit(solution)/shard_map/ppermute | solution.py:91
  110.4 2.7 %copy-start.12 = (bf16[192,128]{1,0:T(8,128)(2,1)}, bf16[192,128]{1,0:T(8,128)(2,1)S(1)}, u32[]{:S(2)}) copy-start(bf16[192,128]{1,0:T(8,128)(2,1)S(1)} %collective-permute-done.24.refs_1_) | copy-start | bytes 147460
  110.4 2.7 %copy-start.13 = (bf16[192,128]{1,0:T(8,128)(2,1)}, bf16[192,128]{1,0:T(8,128)(2,1)S(1)}, u32[]{:S(2)}) copy-start(bf16[192,128]{1,0:T(8,128)(2,1)S(1)} %collective-permute-done.25.refs_2_) | copy-start | bytes 147460
  113.1 0.6 copy-start.14
  118.2 2.1 %collective-permute-start.27 = (bf16[64,4096]{1,0:T(8,128)(2,1)}, bf16[64,4096]{1,0:T(8,128)(2,1)S(1)}, u32[]{:S(2)}, u32[]{:S(2)}) collective-permute-start(bf16[64,4096]{1,0:T(8,128)(2,1)} %get-tuple-element.48), channel_id=1, source_target_pairs={{0,4},{4,0},{8,12},{12,8},{16,20},{20,16},{24,28},{28,24},{1,5},{5... | collective-permute-start | bytes 1572872 | tf_op jit(solution)/shard_map/ppermute | solution.py:96
  120.3 0.8 copy-start.5

commit v6 on v5

--- a/solution.py
+++ b/solution.py
@@ -413,7 +413,8 @@
     inserted = jnp.einsum("qzo,qno->nz", both, weights, preferred_element_type=f32).astype(bf16)
     inserted = pick(inserted.reshape(chips, rows, 2 * width), chip_order)
     inserted = inserted.reshape(count, 2 * width)
-    there = [inserted] + [shifted(inserted, "batch", step) for step in steps]
+    far = shifted(inserted, "batch", steps[-1])
+    there = [inserted] + [shifted(inserted, "batch", step) for step in steps[:-1]] + [far]
 
     responsibilities = jnp.exp(score.reshape(count, 2 * group) - log_evidence[:, None])
     lines = -(-count // group)

time: 124 us -> 124 us (level)
  no operation moved by 1% of the time
where the time goes in v6:
time: 124 us; the launch traced here: 123 us
  waiting for transfers between devices  43.9 us (35%)
  starting transfers between devices  35.8 us (29%)
  Pallas kernels  28.6 us (23%)
  local copies, waits for them, and re-layouts  11.1 us (9%)
  other arithmetic  2.59 us (2%)
    ppermute x19, waiting for transfers between devices, paired(): lax.ppermute(value, 'slab', [(i, i ^ masks[i % 2]) for i in range(size)])  25.4 us
    ppermute x19, starting transfers between devices, paired(): lax.ppermute(value, 'slab', [(i, i ^ masks[i % 2]) for i in range(size)])  20.3 us
    ppermute x9, waiting for transfers between devices, shifted(): lax.ppermute(value, axis, [(i, (i + step) % size) for i in range(size)])  18.5 us
    ppermute x9, starting transfers between devices, shifted(): lax.ppermute(value, axis, [(i, (i + step) % size) for i in range(size)])  15.5 us
    pallas_call x4, Pallas kernels, match(): pl.pallas_call(match_kernel, in_specs=[pl.BlockSpec(memory_space=pltpu.SM...  15.2 us
    pallas_call x1, Pallas kernels, project(): pl.pallas_call(lambda *refs: project_kernel(planes, classes, own_o, depth...  4.71 us
    pallas_call x1, Pallas kernels, sum_images(): pl.pallas_call(sum_images_kernel, grid=(block // tile,), in_specs=[pl.Blo...  4.45 us
    dynamic_slice x1, local copies, waits for them, and re-layouts, local(): lax.dynamic_slice(later, (i * rows, batch * block), (rows, block))  2.51 us
  transfers between devices with their start and end apart: 28, of which 14 were waited for; matrix products, arithmetic and copies ran while one was open for 5% of the time, Pallas kernels for 18%

profile of v6, /device:TPU:0, one launch (start us, length us, event | category | flops | bytes accessed | tf_op | source)
XLA Modules:
  0.0 123.3 jit_solution(9466599543291872593)
XLA Ops:
  0.7 2.1 %fusion.29 = (bf16[48,4096]{1,0:T(8,128)(2,1)}, bf16[48,4096]{1,0:T(8,128)(2,1)S(1)}, bf16[48,4096]{1,0:T(8,128)(2,1)S(1)}) fusion(bf16[384,16384]{1,0:T(8,128)(2,1)} %param.9, s32[]{:T(128)S(6)} %select_n.175, s32[]{:T(128)S(6)} %select_n.178, s32[]{:T(128)S(6)} %select_n.177, s32[]{:T(128)S(6)} %select_n.176), kind=kLoop, calls=%fused_computation.100 | loop fusion | bytes 2359312 | tf_op jit(solution)/shard_map/dynamic_slice | solution.py:330
  4.3 1.2 collective-permute-done
  5.6 2.9 %collective-permute-start.1 = (bf16[134,2048]{1,0:T(8,128)(2,1)S(1)}, bf16[134,2048]{1,0:T(8,128)(2,1)S(1)}, u32[]{:S(2)}, u32[]{:S(2)}) collective-permute-start(bf16[134,2048]{1,0:T(8,128)(2,1)S(1)} %pad_maximum_fusion.refs_1_), channel_id=1, source_target_pairs={{0,8},{4,20},{8,0},{12,28},{16,24},{20,4},{24,16},{28,12},{1,9},{5... | collective-permute-start | bytes 1646600 | tf_op jit(solution)/shard_map/ppermute | solution.py:96
  8.5 1.6 %collective-permute-start.2 = (bf16[48,4096]{1,0:T(8,128)(2,1)S(1)}, bf16[48,4096]{1,0:T(8,128)(2,1)S(1)}, u32[]{:S(2)}, u32[]{:S(2)}) collective-permute-start(bf16[48,4096]{1,0:T(8,128)(2,1)S(1)} %get-tuple-element.64), channel_id=1, source_target_pairs={{0,1},{1,2},{2,3},{3,0},{4,5},{5,6},{6,7},{7,4},{8,9},{9,10},{10,1... | collective-permute-start | bytes 1179656 | tf_op jit(solution)/shard_map/ppermute | solution.py:91
  10.1 1.5 %collective-permute-start.3 = (bf16[134,2048]{1,0:T(8,128)(2,1)S(1)}, bf16[134,2048]{1,0:T(8,128)(2,1)S(1)}, u32[]{:S(2)}, u32[]{:S(2)}) collective-permute-start(bf16[134,2048]{1,0:T(8,128)(2,1)S(1)} %pad_maximum_fusion.refs_1_), channel_id=1, source_target_pairs={{0,16},{4,12},{8,24},{12,4},{16,0},{20,28},{24,8},{28,20},{1,17},{... | collective-permute-start | bytes 1646600 | tf_op jit(solution)/shard_map/ppermute | solution.py:96
  11.6 9.7 %collective-permute-done.2.refs_0_ = bf16[48,4096]{1,0:T(8,128)(2,1)S(1)} collective-permute-done((bf16[48,4096]{1,0:T(8,128)(2,1)S(1)}, bf16[48,4096]{1,0:T(8,128)(2,1)S(1)}, u32[]{:S(2)}, u32[]{:S(2)}) %collective-permute-start.2) | collective-permute-done | bytes 393248 | tf_op jit(solution)/shard_map/ppermute | solution.py:91
  21.3 2.1 %collective-permute-start.4 = (bf16[134,2048]{1,0:T(8,128)(2,1)S(1)}, bf16[134,2048]{1,0:T(8,128)(2,1)S(1)}, u32[]{:S(2)}, u32[]{:S(2)}) collective-permute-start(bf16[134,2048]{1,0:T(8,128)(2,1)S(1)} %collective-permute-done.1.refs_2_), channel_id=1, source_target_pairs={{0,16},{4,12},{8,24},{12,4},{16,0},{20,28},{24,8},{28,20},{1,17},{... | collective-permute-start | bytes 1646600 | tf_op jit(solution)/shard_map/ppermute | solution.py:96
  23.4 3.6 %collective-permute-start.8 = (bf16[48,4096]{1,0:T(8,128)(2,1)S(1)}, bf16[48,4096]{1,0:T(8,128)(2,1)}, u32[]{:S(2)}, u32[]{:S(2)}) collective-permute-start(bf16[48,4096]{1,0:T(8,128)(2,1)S(1)} %get-tuple-element.63), channel_id=1, source_target_pairs={{0,3},{1,0},{2,1},{3,2},{4,7},{5,4},{6,5},{7,6},{8,11},{9,8},{10,9... | collective-permute-start | bytes 1179656 | tf_op jit(solution)/shard_map/ppermute | solution.py:91
  27.1 3.9 %collective-permute-done.4.refs_4_ = bf16[134,2048]{1,0:T(8,128)(2,1)S(1)} collective-permute-done((bf16[134,2048]{1,0:T(8,128)(2,1)S(1)}, bf16[134,2048]{1,0:T(8,128)(2,1)S(1)}, u32[]{:S(2)}, u32[]{:S(2)}) %collective-permute-start.4) | collective-permute-done | bytes 548896 | tf_op jit(solution)/shard_map/ppermute | solution.py:96
  30.9 1.5 %collective-permute-start.6 = (bf16[48,4096]{1,0:T(8,128)(2,1)S(1)}, bf16[48,4096]{1,0:T(8,128)(2,1)S(1)}, u32[]{:S(2)}, u32[]{:S(2)}) collective-permute-start(bf16[48,4096]{1,0:T(8,128)(2,1)S(1)} %collective-permute-done.2.refs_0_), channel_id=1, source_target_pairs={{0,8},{4,20},{8,0},{12,28},{16,24},{20,4},{24,16},{28,12},{1,9},{5... | collective-permute-start | bytes 1179656 | tf_op jit(solution)/shard_map/ppermute | solution.py:96
  32.4 2.1 %collective-permute-start.7 = (bf16[48,4096]{1,0:T(8,128)(2,1)S(1)}, bf16[48,4096]{1,0:T(8,128)(2,1)S(1)}, u32[]{:S(2)}, u32[]{:S(2)}) collective-permute-start(bf16[48,4096]{1,0:T(8,128)(2,1)S(1)} %collective-permute-done.2.refs_0_), channel_id=1, source_target_pairs={{0,16},{4,12},{8,24},{12,4},{16,0},{20,28},{24,8},{28,20},{1,17},{... | collective-permute-start | bytes 1179656 | tf_op jit(solution)/shard_map/ppermute | solution.py:96
  34.5 2.6 %collective-permute-start.5 = (bf16[48,4096]{1,0:T(8,128)(2,1)}, bf16[48,4096]{1,0:T(8,128)(2,1)}, u32[]{:S(2)}, u32[]{:S(2)}) collective-permute-start(bf16[48,4096]{1,0:T(8,128)(2,1)} %get-tuple-element.62), channel_id=1, source_target_pairs={{0,2},{1,3},{2,0},{3,1},{4,6},{5,7},{6,4},{7,5},{8,10},{9,11},{10,... | collective-permute-start | bytes 1179656 | tf_op jit(solution)/shard_map/ppermute | solution.py:91
  37.1 4.5 %collective-permute-done.6.refs_1_ = bf16[48,4096]{1,0:T(8,128)(2,1)S(1)} collective-permute-done((bf16[48,4096]{1,0:T(8,128)(2,1)S(1)}, bf16[48,4096]{1,0:T(8,128)(2,1)S(1)}, u32[]{:S(2)}, u32[]{:S(2)}) %collective-permute-start.6) | collective-permute-done | bytes 393248 | tf_op jit(solution)/shard_map/ppermute | solution.py:96
  41.5 0.8 copy-done.8
  42.3 0.9 collective-permute-start.10
  43.2 1.7 %collective-permute-start.9 = (bf16[48,4096]{1,0:T(8,128)(2,1)}, bf16[48,4096]{1,0:T(8,128)(2,1)}, u32[]{:S(2)}, u32[]{:S(2)}) collective-permute-start(bf16[48,4096]{1,0:T(8,128)(2,1)} %collective-permute-done.8.refs_0_), channel_id=1, source_target_pairs={{0,8},{4,20},{8,0},{12,28},{16,24},{20,4},{24,16},{28,12},{1,9},{5... | collective-permute-start | bytes 1179656 | tf_op jit(solution)/shard_map/ppermute | solution.py:96
  45.0 0.6 pad_add_fusion.refs_0_.order_ref
  45.6 4.7 %project.1 = (bf16[2064,256]{1,0:T(8,128)(2,1)}, f32[1,256]{1,0:T(1,128)}, f32[8,37,128]{2,1,0:T(8,128)}) custom-call(s32[4]{0:T(128)} %pad_add_fusion.refs_0_.order_ref, bf16[134,2048]{1,0:T(8,128)(2,1)} %copy-done, bf16[134,2048]{1,0:T(8,128)(2,1)} %copy-done.2, bf16[134,2048]{1,0:T(8,128)(2,1)} %copy-done.3, bf16[134,2048]{1,0:T(8,128)(2,1)} %copy-done.4), custom_call_target="tpu_custom_call" | custom-call | flops 536870912 | bytes 2195456 | tf_op jit(solution)/shard_map/project/pallas_call | solution.py:253
  50.3 2.3 %collective-permute-done.5.refs_0_ = bf16[48,4096]{1,0:T(8,128)(2,1)} collective-permute-done((bf16[48,4096]{1,0:T(8,128)(2,1)}, bf16[48,4096]{1,0:T(8,128)(2,1)}, u32[]{:S(2)}, u32[]{:S(2)}) %collective-permute-start.5) | collective-permute-done | bytes 393248 | tf_op jit(solution)/shard_map/ppermute | solution.py:91
  52.6 0.8 collective-permute-done.10.refs_2_
  53.4 1.1 collective-permute-start.12
  54.7 1.7 %collective-permute-start.17 = (bf16[48,4096]{1,0:T(8,128)(2,1)}, bf16[48,4096]{1,0:T(8,128)(2,1)}, u32[]{:S(2)}, u32[]{:S(2)}) collective-permute-start(bf16[48,4096]{1,0:T(8,128)(2,1)} %collective-permute-done.9.refs_1_), channel_id=1, source_target_pairs={{0,16},{4,12},{8,24},{12,4},{16,0},{20,28},{24,8},{28,20},{1,17},{... | collective-permute-start | bytes 1179656 | tf_op jit(solution)/shard_map/ppermute | solution.py:96
  56.8 8.8 %collective-permute-done.12.refs_1_ = bf16[48,4096]{1,0:T(8,128)(2,1)S(1)} collective-permute-done((bf16[48,4096]{1,0:T(8,128)(2,1)}, bf16[48,4096]{1,0:T(8,128)(2,1)S(1)}, u32[]{:S(2)}, u32[]{:S(2)}) %collective-permute-start.12) | collective-permute-done | bytes 393248 | tf_op jit(solution)/shard_map/ppermute | solution.py:96
  65.6 3.9 %match.6 = (f32[1,192,256]{2,1,0:T(8,128)}, bf16[192,4096]{1,0:T(8,128)(2,1)}) custom-call(s32[4]{0:T(128)} %pad_add_fusion.refs_0_.order_ref, bf16[2064,256]{1,0:T(8,128)(2,1)} %get-tuple-element.32.mine_ref, bf16[2064,256]{1,0:T(8,128)(2,1)} %collective-permute-done.11.theirs_ref, bf16[48,4096]{1,0:T(8,128)(2,1)} %copy-done.7, bf16[48,4096]{1,0:T(8,128)(2,1)} %copy-done.8, ...), custom_call_target="tpu_custom_call" | custom-call | flops 402653184 | bytes 3686400 | tf_op jit(solution)/shard_map/match/pallas_call | solution.py:290
  69.5 2.9 %collective-permute-start.16 = (f32[192,256]{1,0:T(8,128)}, f32[192,256]{1,0:T(8,128)S(1)}, u32[]{:S(2)}, u32[]{:S(2)}) collective-permute-start(f32[192,256]{1,0:T(8,128)} %bitcast.89), channel_id=1, source_target_pairs={{0,3},{1,0},{2,1},{3,2},{4,7},{5,4},{6,5},{7,6},{8,11},{9,8},{10,9... | collective-permute-start | bytes 589832 | tf_op jit(solution)/shard_map/ppermute | solution.py:91
  72.4 3.8 %match.7 = (f32[1,192,256]{2,1,0:T(8,128)}, bf16[192,4096]{1,0:T(8,128)(2,1)}) custom-call(s32[4]{0:T(128)} %pad_add_fusion.refs_0_.order_ref, bf16[2064,256]{1,0:T(8,128)(2,1)} %get-tuple-element.32.mine_ref, bf16[2064,256]{1,0:T(8,128)(2,1)} %collective-permute-done.11.theirs_ref, bf16[48,4096]{1,0:T(8,128)(2,1)} %collective-permute-done.8.refs_0_, ...), custom_call_target="tpu_custom_call" | custom-call | flops 402653184 | bytes 3686400 | tf_op jit(solution)/shard_map/match/pallas_call | solution.py:290
  76.1 1.8 %collective-permute-done.14.refs_3_ = bf16[48,4096]{1,0:T(8,128)(2,1)} collective-permute-done((bf16[48,4096]{1,0:T(8,128)(2,1)S(1)}, bf16[48,4096]{1,0:T(8,128)(2,1)}, u32[]{:S(2)}, u32[]{:S(2)}) %collective-permute-start.14) | collective-permute-done | bytes 393248 | tf_op jit(solution)/shard_map/ppermute | solution.py:96
  77.9 3.7 %match.4 = (f32[1,192,256]{2,1,0:T(8,128)}, bf16[192,4096]{1,0:T(8,128)(2,1)}) custom-call(s32[4]{0:T(128)} %pad_add_fusion.refs_0_.order_ref, bf16[2064,256]{1,0:T(8,128)(2,1)} %get-tuple-element.32.mine_ref, bf16[2064,256]{1,0:T(8,128)(2,1)} %collective-permute-done.11.theirs_ref, bf16[48,4096]{1,0:T(8,128)(2,1)} %collective-permute-done.5.refs_0_, ...), custom_call_target="tpu_custom_call" | custom-call | flops 402653184 | bytes 3686400 | tf_op jit(solution)/shard_map/match/pallas_call | solution.py:290
  81.6 1.0 collective-permute-start.19
  82.6 2.5 %fusion.28 = (bf16[48,4096]{1,0:T(8,128)(2,1)}, bf16[48,4096]{1,0:T(8,128)(2,1)}, bf16[48,4096]{1,0:T(8,128)(2,1)}, bf16[48,4096]{1,0:T(8,128)(2,1)}) fusion(bf16[384,16384]{1,0:T(8,128)(2,1)} %param.9, s32[]{:T(128)S(6)} %select_n.186, s32[]{:T(128)S(6)} %select_n.183, s32[]{:T(128)S(6)} %select_n.185, s32[]{:T(128)S(6)} %select_n.184, s32[]{:T(128)S(6)} %select_n.175), kind=kLoop, calls=%fused_computation.99 | loop fusion | bytes 3145748 | tf_op jit(solution)/shard_map/dynamic_slice | solution.py:370
  85.7 0.6 fusion.27
  86.5 2.0 %window_slices.1 = bf16[4,128,256]{2,1,0:T(8,128)(2,1)} custom-call(s32[4]{0:T(128)} %pad_add_fusion.refs_0_.order_ref, f32[8,37,128]{2,1,0:T(8,128)} %get-tuple-element.41.refs_1_), custom_call_target="tpu_custom_call" | custom-call | bytes 151552 | tf_op jit(solution)/shard_map/window_slices/pallas_call | solution.py:78
  88.5 3.8 %match.5 = (f32[1,192,256]{2,1,0:T(8,128)}, bf16[192,4096]{1,0:T(8,128)(2,1)}) custom-call(s32[4]{0:T(128)} %pad_add_fusion.refs_0_.order_ref, bf16[2064,256]{1,0:T(8,128)(2,1)} %get-tuple-element.32.mine_ref, bf16[2064,256]{1,0:T(8,128)(2,1)} %collective-permute-done.11.theirs_ref, bf16[48,4096]{1,0:T(8,128)(2,1)} %get-tuple-element.61.refs_0_, ...), custom_call_target="tpu_custom_call" | custom-call | flops 402653184 | bytes 3686400 | tf_op jit(solution)/shard_map/match/pallas_call | solution.py:290
  92.3 1.3 %collective-permute-done.19 = f32[192,256]{1,0:T(8,128)S(1)} collective-permute-done((f32[192,256]{1,0:T(8,128)}, f32[192,256]{1,0:T(8,128)S(1)}, u32[]{:S(2)}, u32[]{:S(2)}) %collective-permute-start.19) | collective-permute-done | bytes 196640 | tf_op jit(solution)/shard_map/ppermute | solution.py:91
  93.6 1.0 fusion.13
  95.5 0.9 collective-permute-start.20
  96.4 0.9 collective-permute-start.21
  97.3 1.7 %collective-permute-start.22 = (bf16[198,256]{1,0:T(8,128)(2,1)S(1)}, bf16[198,256]{1,0:T(8,128)(2,1)S(1)}, u32[]{:S(2)}, u32[]{:S(2)}) collective-permute-start(bf16[198,256]{1,0:T(8,128)(2,1)S(1)} %get-tuple-element.83), channel_id=1, source_target_pairs={{0,24},{4,28},{8,16},{12,20},{16,8},{20,12},{24,0},{28,4},{1,25},{... | collective-permute-start | bytes 304136 | tf_op jit(solution)/shard_map/ppermute | solution.py:96
  99.1 1.8 %collective-permute-done.20 = bf16[198,256]{1,0:T(8,128)(2,1)S(1)} collective-permute-done((bf16[198,256]{1,0:T(8,128)(2,1)S(1)}, bf16[198,256]{1,0:T(8,128)(2,1)S(1)}, u32[]{:S(2)}, u32[]{:S(2)}) %collective-permute-start.20) | collective-permute-done | bytes 101408 | tf_op jit(solution)/shard_map/ppermute | solution.py:96
  100.9 2.4 %collective-permute-done.21 = bf16[198,256]{1,0:T(8,128)(2,1)S(1)} collective-permute-done((bf16[198,256]{1,0:T(8,128)(2,1)S(1)}, bf16[198,256]{1,0:T(8,128)(2,1)S(1)}, u32[]{:S(2)}, u32[]{:S(2)}) %collective-permute-start.21) | collective-permute-done | bytes 101408 | tf_op jit(solution)/shard_map/ppermute | solution.py:96
  104.4 3.4 %collective-permute-start.25 = (bf16[192,128]{1,0:T(8,128)(2,1)S(1)}, bf16[192,128]{1,0:T(8,128)(2,1)S(1)}, u32[]{:S(2)}, u32[]{:S(2)}) collective-permute-start(bf16[192,128]{1,0:T(8,128)(2,1)S(1)} %bitcast.76), channel_id=1, source_target_pairs={{0,3},{1,0},{2,1},{3,2},{4,7},{5,4},{6,5},{7,6},{8,11},{9,8},{10,9... | collective-permute-start | bytes 147464 | tf_op jit(solution)/shard_map/ppermute | solution.py:91
  107.9 2.5 %collective-permute-done.24.refs_1_ = bf16[192,128]{1,0:T(8,128)(2,1)S(1)} collective-permute-done((bf16[192,128]{1,0:T(8,128)(2,1)S(1)}, bf16[192,128]{1,0:T(8,128)(2,1)S(1)}, u32[]{:S(2)}, u32[]{:S(2)}) %collective-permute-start.24) | collective-permute-done | bytes 49184 | tf_op jit(solution)/shard_map/ppermute | solution.py:91
  110.4 2.7 %collective-permute-done.26.refs_3_ = bf16[192,128]{1,0:T(8,128)(2,1)S(1)} collective-permute-done((bf16[192,128]{1,0:T(8,128)(2,1)S(1)}, bf16[192,128]{1,0:T(8,128)(2,1)S(1)}, u32[]{:S(2)}, u32[]{:S(2)}) %collective-permute-start.26) | collective-permute-done | bytes 49184 | tf_op jit(solution)/shard_map/ppermute | solution.py:91
  113.7 4.5 %sum_images.1 = (f32[64,4096]{1,0:T(8,128)}, bf16[64,4096]{1,0:T(8,128)(2,1)}) custom-call(bf16[192,128]{1,0:T(8,128)(2,1)} %bitcast.78, bf16[192,128]{1,0:T(8,128)(2,1)} %copy-done.12, bf16[192,128]{1,0:T(8,128)(2,1)} %copy-done.13, bf16[192,128]{1,0:T(8,128)(2,1)} %copy-done.14, bf16[192,4096]{1,0:T(8,128)(2,1)} %get-tuple-element.43.refs_4_, ...), custom_call_target="tpu_custom_call" | custom-call | flops 805306368 | bytes 6488064 | tf_op jit(solution)/shard_map/sum_images/pallas_call | solution.py:170
  118.4 0.7 reshape.324
  119.1 0.8 copy.27
  120.3 0.8 copy-done.5
  121.1 2.2 %add_parts.1 = f32[32,2,4096]{2,1,0:T(2,128)} custom-call(f32[64,4096]{1,0:T(8,128)} %get-tuple-element.47.one_ref, bf16[64,4096]{1,0:T(8,128)(2,1)} %copy-done.5), custom_call_target="tpu_custom_call" | custom-call | flops 524288 | bytes 2621440 | tf_op jit(solution)/shard_map/add_parts/pallas_call | solution.py:192
  (116 shorter events, 6.1 us)
Async XLA Ops:
  0.7 2.2 %copy-start.6 = (bf16[32,2,4096]{2,1,0:T(2,128)(2,1)S(1)}, bf16[32,2,4096]{2,1,0:T(2,128)(2,1)}, u32[]{:S(2)}) copy-start(bf16[32,2,4096]{2,1,0:T(2,128)(2,1)} %param.6) | copy-start | bytes 1572868
  0.7 2.4 %copy-start.18 = (f32[2,64]{1,0:T(2,128)S(1)}, f32[2,64]{1,0:T(2,128)}, u32[]{:S(2)}) copy-start(f32[2,64]{1,0:T(2,128)} %param.11) | copy-start | bytes 1540
  0.7 2.6 %copy-start.19 = (s32[2,64]{1,0:T(2,128)S(1)}, s32[2,64]{1,0:T(2,128)}, u32[]{:S(2)}) copy-start(s32[2,64]{1,0:T(2,128)} %param.8) | copy-start | bytes 1540
  0.7 2.8 %copy-start.16 = (bf16[2,64,32]{1,2,0:T(8,128)(2,1)S(1)}, bf16[2,64,32]{1,2,0:T(8,128)(2,1)}, u32[]{:S(2)}) copy-start(bf16[2,64,32]{1,2,0:T(8,128)(2,1)} %param.7) | copy-start | bytes 24580
  3.8 1.7 %collective-permute-start = (bf16[67,2048]{1,0:T(8,128)(2,1)S(1)}, bf16[67,2048]{1,0:T(8,128)(2,1)S(1)}, u32[]{:S(2)}, u32[]{:S(2)}) collective-permute-start(bf16[67,2048]{1,0:T(8,128)(2,1)S(1)} %pad_maximum_fusion.7), channel_id=1, source_target_pairs={{0,4},{4,0},{8,12},{12,8},{16,20},{20,16},{24,28},{28,24},{1,5},{5... | collective-permute-start | bytes 823304 | tf_op jit(solution)/shard_map/ppermute | solution.py:96
  5.6 40.0 %copy-start = (bf16[134,2048]{1,0:T(8,128)(2,1)}, bf16[134,2048]{1,0:T(8,128)(2,1)S(1)}, u32[]{:S(2)}) copy-start(bf16[134,2048]{1,0:T(8,128)(2,1)S(1)} %pad_maximum_fusion.refs_1_) | copy-start | bytes 1646596
  5.6 15.7 %collective-permute-start.1 = (bf16[134,2048]{1,0:T(8,128)(2,1)S(1)}, bf16[134,2048]{1,0:T(8,128)(2,1)S(1)}, u32[]{:S(2)}, u32[]{:S(2)}) collective-permute-start(bf16[134,2048]{1,0:T(8,128)(2,1)S(1)} %pad_maximum_fusion.refs_1_), channel_id=1, source_target_pairs={{0,8},{4,20},{8,0},{12,28},{16,24},{20,4},{24,16},{28,12},{1,9},{5... | collective-permute-start | bytes 1646600 | tf_op jit(solution)/shard_map/ppermute | solution.py:96
  8.5 12.8 %collective-permute-start.2 = (bf16[48,4096]{1,0:T(8,128)(2,1)S(1)}, bf16[48,4096]{1,0:T(8,128)(2,1)S(1)}, u32[]{:S(2)}, u32[]{:S(2)}) collective-permute-start(bf16[48,4096]{1,0:T(8,128)(2,1)S(1)} %get-tuple-element.64), channel_id=1, source_target_pairs={{0,1},{1,2},{2,3},{3,0},{4,5},{5,6},{6,7},{7,4},{8,9},{9,10},{10,1... | collective-permute-start | bytes 1179656 | tf_op jit(solution)/shard_map/ppermute | solution.py:91
  10.1 17.0 %collective-permute-start.3 = (bf16[134,2048]{1,0:T(8,128)(2,1)S(1)}, bf16[134,2048]{1,0:T(8,128)(2,1)S(1)}, u32[]{:S(2)}, u32[]{:S(2)}) collective-permute-start(bf16[134,2048]{1,0:T(8,128)(2,1)S(1)} %pad_maximum_fusion.refs_1_), channel_id=1, source_target_pairs={{0,16},{4,12},{8,24},{12,4},{16,0},{20,28},{24,8},{28,20},{1,17},{... | collective-permute-start | bytes 1646600 | tf_op jit(solution)/shard_map/ppermute | solution.py:96
  21.3 44.3 %copy-start.7 = (bf16[48,4096]{1,0:T(8,128)(2,1)}, bf16[48,4096]{1,0:T(8,128)(2,1)S(1)}, u32[]{:S(2)}) copy-start(bf16[48,4096]{1,0:T(8,128)(2,1)S(1)} %collective-permute-done.2.refs_0_) | copy-start | bytes 1179652
  21.3 5.8 %copy-start.2 = (bf16[134,2048]{1,0:T(8,128)(2,1)}, bf16[134,2048]{1,0:T(8,128)(2,1)S(1)}, u32[]{:S(2)}) copy-start(bf16[134,2048]{1,0:T(8,128)(2,1)S(1)} %collective-permute-done.1.refs_2_) | copy-start | bytes 1646596
  21.3 9.6 %collective-permute-start.4 = (bf16[134,2048]{1,0:T(8,128)(2,1)S(1)}, bf16[134,2048]{1,0:T(8,128)(2,1)S(1)}, u32[]{:S(2)}, u32[]{:S(2)}) collective-permute-start(bf16[134,2048]{1,0:T(8,128)(2,1)S(1)} %collective-permute-done.1.refs_2_), channel_id=1, source_target_pairs={{0,16},{4,12},{8,24},{12,4},{16,0},{20,28},{24,8},{28,20},{1,17},{... | collective-permute-start | bytes 1646600 | tf_op jit(solution)/shard_map/ppermute | solution.py:96
  23.4 13.7 %collective-permute-start.8 = (bf16[48,4096]{1,0:T(8,128)(2,1)S(1)}, bf16[48,4096]{1,0:T(8,128)(2,1)}, u32[]{:S(2)}, u32[]{:S(2)}) collective-permute-start(bf16[48,4096]{1,0:T(8,128)(2,1)S(1)} %get-tuple-element.63), channel_id=1, source_target_pairs={{0,3},{1,0},{2,1},{3,2},{4,7},{5,4},{6,5},{7,6},{8,11},{9,8},{10,9... | collective-permute-start | bytes 1179656 | tf_op jit(solution)/shard_map/ppermute | solution.py:91
  27.1 3.9 %copy-start.3 = (bf16[134,2048]{1,0:T(8,128)(2,1)}, bf16[134,2048]{1,0:T(8,128)(2,1)S(1)}, u32[]{:S(2)}) copy-start(bf16[134,2048]{1,0:T(8,128)(2,1)S(1)} %collective-permute-done.3.refs_3_) | copy-start | bytes 1646596
  30.9 1.5 %copy-start.4 = (bf16[134,2048]{1,0:T(8,128)(2,1)}, bf16[134,2048]{1,0:T(8,128)(2,1)S(1)}, u32[]{:S(2)}) copy-start(bf16[134,2048]{1,0:T(8,128)(2,1)S(1)} %collective-permute-done.4.refs_4_) | copy-start | bytes 1646596
  30.9 10.6 %collective-permute-start.6 = (bf16[48,4096]{1,0:T(8,128)(2,1)S(1)}, bf16[48,4096]{1,0:T(8,128)(2,1)S(1)}, u32[]{:S(2)}, u32[]{:S(2)}) collective-permute-start(bf16[48,4096]{1,0:T(8,128)(2,1)S(1)} %collective-permute-done.2.refs_0_), channel_id=1, source_target_pairs={{0,8},{4,20},{8,0},{12,28},{16,24},{20,4},{24,16},{28,12},{1,9},{5... | collective-permute-start | bytes 1179656 | tf_op jit(solution)/shard_map/ppermute | solution.py:96
  32.4 9.1 %collective-permute-start.7 = (bf16[48,4096]{1,0:T(8,128)(2,1)S(1)}, bf16[48,4096]{1,0:T(8,128)(2,1)S(1)}, u32[]{:S(2)}, u32[]{:S(2)}) collective-permute-start(bf16[48,4096]{1,0:T(8,128)(2,1)S(1)} %collective-permute-done.2.refs_0_), channel_id=1, source_target_pairs={{0,16},{4,12},{8,24},{12,4},{16,0},{20,28},{24,8},{28,20},{1,17},{... | collective-permute-start | bytes 1179656 | tf_op jit(solution)/shard_map/ppermute | solution.py:96
  34.5 18.2 %collective-permute-start.5 = (bf16[48,4096]{1,0:T(8,128)(2,1)}, bf16[48,4096]{1,0:T(8,128)(2,1)}, u32[]{:S(2)}, u32[]{:S(2)}) collective-permute-start(bf16[48,4096]{1,0:T(8,128)(2,1)} %get-tuple-element.62), channel_id=1, source_target_pairs={{0,2},{1,3},{2,0},{3,1},{4,6},{5,7},{6,4},{7,5},{8,10},{9,11},{10,... | collective-permute-start | bytes 1179656 | tf_op jit(solution)/shard_map/ppermute | solution.py:91
  41.5 0.8 copy-start.8
  42.3 0.9 copy-start.9
  42.3 11.1 %collective-permute-start.10 = (bf16[48,4096]{1,0:T(8,128)(2,1)}, bf16[48,4096]{1,0:T(8,128)(2,1)}, u32[]{:S(2)}, u32[]{:S(2)}) collective-permute-start(bf16[48,4096]{1,0:T(8,128)(2,1)} %collective-permute-done.8.refs_0_), channel_id=1, source_target_pairs={{0,16},{4,12},{8,24},{12,4},{16,0},{20,28},{24,8},{28,20},{1,17},{... | collective-permute-start | bytes 1179656 | tf_op jit(solution)/shard_map/ppermute | solution.py:96
  43.2 10.2 %collective-permute-start.9 = (bf16[48,4096]{1,0:T(8,128)(2,1)}, bf16[48,4096]{1,0:T(8,128)(2,1)}, u32[]{:S(2)}, u32[]{:S(2)}) collective-permute-start(bf16[48,4096]{1,0:T(8,128)(2,1)} %collective-permute-done.8.refs_0_), channel_id=1, source_target_pairs={{0,8},{4,20},{8,0},{12,28},{16,24},{20,4},{24,16},{28,12},{1,9},{5... | collective-permute-start | bytes 1179656 | tf_op jit(solution)/shard_map/ppermute | solution.py:96
  53.4 12.1 %collective-permute-start.11 = (bf16[2064,256]{1,0:T(8,128)(2,1)}, bf16[2064,256]{1,0:T(8,128)(2,1)}, u32[]{:S(2)}, u32[]{:S(2)}) collective-permute-start(bf16[2064,256]{1,0:T(8,128)(2,1)} %get-tuple-element.32.mine_ref), channel_id=1, source_target_pairs={{0,4},{4,0},{8,12},{12,8},{16,20},{20,16},{24,28},{28,24},{1,5},{5... | collective-permute-start | bytes 3170312 | tf_op jit(solution)/shard_map/ppermute | solution.py:96
  53.4 12.1 %collective-permute-start.12 = (bf16[48,4096]{1,0:T(8,128)(2,1)}, bf16[48,4096]{1,0:T(8,128)(2,1)S(1)}, u32[]{:S(2)}, u32[]{:S(2)}) collective-permute-start(bf16[48,4096]{1,0:T(8,128)(2,1)} %collective-permute-done.5.refs_0_), channel_id=1, source_target_pairs={{0,8},{4,20},{8,0},{12,28},{16,24},{20,4},{24,16},{28,12},{1,9},{5... | collective-permute-start | bytes 1179656 | tf_op jit(solution)/shard_map/ppermute | solution.py:96
  54.5 11.1 %collective-permute-start.15 = (bf16[48,4096]{1,0:T(8,128)(2,1)}, bf16[48,4096]{1,0:T(8,128)(2,1)}, u32[]{:S(2)}, u32[]{:S(2)}) collective-permute-start(bf16[48,4096]{1,0:T(8,128)(2,1)} %copy-done.8), channel_id=1, source_target_pairs={{0,16},{4,12},{8,24},{12,4},{16,0},{20,28},{24,8},{28,20},{1,17},{... | collective-permute-start | bytes 1179656 | tf_op jit(solution)/shard_map/ppermute | solution.py:96
  54.7 17.6 %collective-permute-start.17 = (bf16[48,4096]{1,0:T(8,128)(2,1)}, bf16[48,4096]{1,0:T(8,128)(2,1)}, u32[]{:S(2)}, u32[]{:S(2)}) collective-permute-start(bf16[48,4096]{1,0:T(8,128)(2,1)} %collective-permute-done.9.refs_1_), channel_id=1, source_target_pairs={{0,16},{4,12},{8,24},{12,4},{16,0},{20,28},{24,8},{28,20},{1,17},{... | collective-permute-start | bytes 1179656 | tf_op jit(solution)/shard_map/ppermute | solution.py:96
  56.5 19.6 %collective-permute-start.13 = (bf16[48,4096]{1,0:T(8,128)(2,1)}, bf16[48,4096]{1,0:T(8,128)(2,1)}, u32[]{:S(2)}, u32[]{:S(2)}) collective-permute-start(bf16[48,4096]{1,0:T(8,128)(2,1)} %collective-permute-done.5.refs_0_), channel_id=1, source_target_pairs={{0,16},{4,12},{8,24},{12,4},{16,0},{20,28},{24,8},{28,20},{1,17},{... | collective-permute-start | bytes 1179656 | tf_op jit(solution)/shard_map/ppermute | solution.py:96
  65.5 3.9 %copy-start.10 = (bf16[48,4096]{1,0:T(8,128)(2,1)}, bf16[48,4096]{1,0:T(8,128)(2,1)S(1)}, u32[]{:S(2)}) copy-start(bf16[48,4096]{1,0:T(8,128)(2,1)S(1)} %collective-permute-done.12.refs_1_) | copy-start | bytes 1179652
  65.5 12.4 %collective-permute-start.14 = (bf16[48,4096]{1,0:T(8,128)(2,1)S(1)}, bf16[48,4096]{1,0:T(8,128)(2,1)}, u32[]{:S(2)}, u32[]{:S(2)}) collective-permute-start(bf16[48,4096]{1,0:T(8,128)(2,1)S(1)} %collective-permute-done.12.refs_1_), channel_id=1, source_target_pairs={{0,16},{4,12},{8,24},{12,4},{16,0},{20,28},{24,8},{28,20},{1,17},{... | collective-permute-start | bytes 1179656 | tf_op jit(solution)/shard_map/ppermute | solution.py:96
  69.5 22.8 %collective-permute-start.16 = (f32[192,256]{1,0:T(8,128)}, f32[192,256]{1,0:T(8,128)S(1)}, u32[]{:S(2)}, u32[]{:S(2)}) collective-permute-start(f32[192,256]{1,0:T(8,128)} %bitcast.89), channel_id=1, source_target_pairs={{0,3},{1,0},{2,1},{3,2},{4,7},{5,4},{6,5},{7,6},{8,11},{9,8},{10,9... | collective-permute-start | bytes 589832 | tf_op jit(solution)/shard_map/ppermute | solution.py:91
  76.1 16.2 %collective-permute-start.18 = (f32[192,256]{1,0:T(8,128)}, f32[192,256]{1,0:T(8,128)S(1)}, u32[]{:S(2)}, u32[]{:S(2)}) collective-permute-start(f32[192,256]{1,0:T(8,128)} %bitcast.90), channel_id=1, source_target_pairs={{0,1},{1,2},{2,3},{3,0},{4,5},{5,6},{6,7},{7,4},{8,9},{9,10},{10,1... | collective-permute-start | bytes 589832 | tf_op jit(solution)/shard_map/ppermute | solution.py:91
  81.6 3.5 %copy-start.17 = (f32[384]{0:T(512)S(1)}, f32[384]{0:T(512)}, u32[]{:S(2)}) copy-start(f32[384]{0:T(512)} %param.10) | copy-start | bytes 4612
  81.6 12.0 %collective-permute-start.19 = (f32[192,256]{1,0:T(8,128)}, f32[192,256]{1,0:T(8,128)S(1)}, u32[]{:S(2)}, u32[]{:S(2)}) collective-permute-start(f32[192,256]{1,0:T(8,128)} %bitcast.91), channel_id=1, source_target_pairs={{0,2},{1,3},{2,0},{3,1},{4,6},{5,7},{6,4},{7,5},{8,10},{9,11},{10,... | collective-permute-start | bytes 589832 | tf_op jit(solution)/shard_map/ppermute | solution.py:91
  92.3 2.4 %copy-start.15 = (f32[1,256]{1,0:T(1,128)S(1)}, f32[1,256]{1,0:T(1,128)}, u32[]{:S(2)}) copy-start(f32[1,256]{1,0:T(1,128)} %get-tuple-element.39) | copy-start | bytes 3076
  93.6 5.5 %copy-start.1 = (bf16[4,128,256]{2,1,0:T(8,128)(2,1)S(1)}, bf16[4,128,256]{2,1,0:T(8,128)(2,1)}, u32[]{:S(2)}) copy-start(bf16[4,128,256]{2,1,0:T(8,128)(2,1)} %window_slices.1) | copy-start | bytes 786436
  95.5 5.4 %collective-permute-start.20 = (bf16[198,256]{1,0:T(8,128)(2,1)S(1)}, bf16[198,256]{1,0:T(8,128)(2,1)S(1)}, u32[]{:S(2)}, u32[]{:S(2)}) collective-permute-start(bf16[198,256]{1,0:T(8,128)(2,1)S(1)} %get-tuple-element.83), channel_id=1, source_target_pairs={{0,8},{4,12},{8,0},{12,4},{16,24},{20,28},{24,16},{28,20},{1,9},{5... | collective-permute-start | bytes 304136 | tf_op jit(solution)/shard_map/ppermute | solution.py:96
  96.4 6.9 %collective-permute-start.21 = (bf16[198,256]{1,0:T(8,128)(2,1)S(1)}, bf16[198,256]{1,0:T(8,128)(2,1)S(1)}, u32[]{:S(2)}, u32[]{:S(2)}) collective-permute-start(bf16[198,256]{1,0:T(8,128)(2,1)S(1)} %get-tuple-element.83), channel_id=1, source_target_pairs={{0,16},{4,20},{8,24},{12,28},{16,0},{20,4},{24,8},{28,12},{1,17},{... | collective-permute-start | bytes 304136 | tf_op jit(solution)/shard_map/ppermute | solution.py:96
  97.3 5.9 %collective-permute-start.22 = (bf16[198,256]{1,0:T(8,128)(2,1)S(1)}, bf16[198,256]{1,0:T(8,128)(2,1)S(1)}, u32[]{:S(2)}, u32[]{:S(2)}) collective-permute-start(bf16[198,256]{1,0:T(8,128)(2,1)S(1)} %get-tuple-element.83), channel_id=1, source_target_pairs={{0,24},{4,28},{8,16},{12,20},{16,8},{20,12},{24,0},{28,4},{1,25},{... | collective-permute-start | bytes 304136 | tf_op jit(solution)/shard_map/ppermute | solution.py:96
  103.6 4.3 %collective-permute-start.23 = (f32[194,128]{1,0:T(8,128)S(1)}, f32[194,128]{1,0:T(8,128)S(1)}, u32[]{:S(2)}, u32[]{:S(2)}) collective-permute-start(f32[194,128]{1,0:T(8,128)S(1)} %pad_maximum_fusion.10), channel_id=1, source_target_pairs={{0,4},{4,0},{8,12},{12,8},{16,20},{20,16},{24,28},{28,24},{1,5},{5... | collective-permute-start | bytes 297992 | tf_op jit(solution)/shard_map/ppermute | solution.py:96
  104.0 9.1 %copy-start.11 = (bf16[4,48,128]{2,1,0:T(8,128)(2,1)}, bf16[4,48,128]{2,1,0:T(8,128)(2,1)S(1)}, u32[]{:S(2)}) copy-start(bf16[4,48,128]{2,1,0:T(8,128)(2,1)S(1)} %pad_maximum_fusion.11) | copy-start | bytes 147460
  104.0 6.4 %collective-permute-start.24 = (bf16[192,128]{1,0:T(8,128)(2,1)S(1)}, bf16[192,128]{1,0:T(8,128)(2,1)S(1)}, u32[]{:S(2)}, u32[]{:S(2)}) collective-permute-start(bf16[192,128]{1,0:T(8,128)(2,1)S(1)} %bitcast.75), channel_id=1, source_target_pairs={{0,1},{1,2},{2,3},{3,0},{4,5},{5,6},{6,7},{7,4},{8,9},{9,10},{10,1... | collective-permute-start | bytes 147464 | tf_op jit(solution)/shard_map/ppermute | solution.py:91
  104.4 6.0 %collective-permute-start.25 = (bf16[192,128]{1,0:T(8,128)(2,1)S(1)}, bf16[192,128]{1,0:T(8,128)(2,1)S(1)}, u32[]{:S(2)}, u32[]{:S(2)}) collective-permute-start(bf16[192,128]{1,0:T(8,128)(2,1)S(1)} %bitcast.76), channel_id=1, source_target_pairs={{0,3},{1,0},{2,1},{3,2},{4,7},{5,4},{6,5},{7,6},{8,11},{9,8},{10,9... | collective-permute-start | bytes 147464 | tf_op jit(solution)/shard_map/ppermute | solution.py:91
  107.9 5.2 %collective-permute-start.26 = (bf16[192,128]{1,0:T(8,128)(2,1)S(1)}, bf16[192,128]{1,0:T(8,128)(2,1)S(1)}, u32[]{:S(2)}, u32[]{:S(2)}) collective-permute-start(bf16[192,128]{1,0:T(8,128)(2,1)S(1)} %bitcast.77), channel_id=1, source_target_pairs={{0,2},{1,3},{2,0},{3,1},{4,6},{5,7},{6,4},{7,5},{8,10},{9,11},{10,... | collective-permute-start | bytes 147464 | tf_op jit(solution)/shard_map/ppermute | solution.py:91
  110.4 2.7 %copy-start.12 = (bf16[192,128]{1,0:T(8,128)(2,1)}, bf16[192,128]{1,0:T(8,128)(2,1)S(1)}, u32[]{:S(2)}) copy-start(bf16[192,128]{1,0:T(8,128)(2,1)S(1)} %collective-permute-done.24.refs_1_) | copy-start | bytes 147460
  110.4 2.7 %copy-start.13 = (bf16[192,128]{1,0:T(8,128)(2,1)}, bf16[192,128]{1,0:T(8,128)(2,1)S(1)}, u32[]{:S(2)}) copy-start(bf16[192,128]{1,0:T(8,128)(2,1)S(1)} %collective-permute-done.25.refs_2_) | copy-start | bytes 147460
  113.1 0.6 copy-start.14
  118.2 2.1 %collective-permute-start.27 = (bf16[64,4096]{1,0:T(8,128)(2,1)}, bf16[64,4096]{1,0:T(8,128)(2,1)S(1)}, u32[]{:S(2)}, u32[]{:S(2)}) collective-permute-start(bf16[64,4096]{1,0:T(8,128)(2,1)} %get-tuple-element.48), channel_id=1, source_target_pairs={{0,4},{4,0},{8,12},{12,8},{16,20},{20,16},{24,28},{28,24},{1,5},{5... | collective-permute-start | bytes 1572872 | tf_op jit(solution)/shard_map/ppermute | solution.py:96
  120.3 0.8 copy-start.5
